TPU v7x, 128 devices: a whole 4x4x4 slice. The times are simulated.
128 devices in a mesh: wide: 32 (over z, x, core), narrow: 4 (over y).
Axes of the slice: x: 4, y: 4, z: 4, core: 2. Of those that a mesh axis runs over, the one named last changes fastest.
Arguments:
- tokens: bfloat16 [131072, 512], P(('wide', 'narrow')), may hold values from -6 to 6
- rotation: int32 [131072], P(('wide', 'narrow')), may hold values from 0 to 131071, as said below
- qkv_weight: bfloat16 [512, 1536], replicated, may hold values from -0.25 to 0.25
- proj_weight: bfloat16 [512, 512], replicated, may hold values from -0.25 to 0.25
- up_weight: bfloat16 [512, 2048], P(None, 'narrow'), may hold values from -0.25 to 0.25
- down_weight: bfloat16 [2048, 512], P('narrow'), may hold values from -0.125 to 0.125
- cotangent: bfloat16 [131072, 512], P(('wide', 'narrow')), may hold values from -6 to 6
Outputs:
- output: bfloat16 [131072, 512], P(('wide', 'narrow'))
- grad_tokens: bfloat16 [131072, 512], P(('wide', 'narrow'))
- grad_qkv: float32 [512, 1536], replicated
- grad_proj: float32 [512, 512], replicated
- grad_up: float32 [512, 2048], P(None, 'narrow')
- grad_down: float32 [2048, 512], P('narrow')
Inputs may be any that keep to these rules, and one draw needn't show every extreme that they name: rotation is a permutation. A particle held by a device goes to a device with the same narrow index, and at most 48 particles go from one device to one device; that many do in every draw.
All inputs are finite; a program needn't handle non-finite values.
Results may differ from a plain program's by a relative error of at most 0.024.
Values may be sent and summed in bfloat16 or wider, within the bound.
No kernel may reach another device: no remote copies, remote signals or barrier semaphores. Data moves between devices by JAX's collectives and lax.ppermute only.
A program may use at most 192 MiB of HBM per device.

v0:
```python
import jax
import jax.numpy as jnp
from jax import lax
from jax.sharding import PartitionSpec as P

HEADS = 8
BALL = 256


epsilon = 1e-06


def row_scale(values):
    return lax.rsqrt(jnp.mean(values * values, axis=-1, keepdims=True) + epsilon)


def norm_back(values, scaling, gradient):
    unit = values * scaling
    return scaling * (gradient - unit * jnp.mean(gradient * unit, axis=-1, keepdims=True))


def gelu_tanh(values):
    return jax.nn.gelu(values, approximate=True)


def split_heads(block, head_size):
    row_count, columns = block.shape
    return block.reshape(row_count // BALL, BALL, columns // head_size, head_size)


def attend(packed, head_size):
    columns = packed.shape[1] // 3
    queries = split_heads(packed[:, :columns], head_size)
    key_rows = split_heads(packed[:, columns : 2 * columns], head_size)
    values = split_heads(packed[:, 2 * columns :], head_size)
    scaling = head_size ** (-0.5)
    scores = (
        jnp.einsum("bqhd,bkhd->bhqk", queries, key_rows, preferred_element_type=jnp.float32)
        * scaling
    )
    weights = jax.nn.softmax(scores, axis=-1).astype(jnp.bfloat16)
    result = jnp.einsum("bhqk,bkhd->bqhd", weights, values, preferred_element_type=jnp.float32)
    return result.reshape(packed.shape[0], columns).astype(jnp.bfloat16)


def attend_back(packed, grad_out, head_size):
    columns = packed.shape[1] // 3
    queries = split_heads(packed[:, :columns], head_size)
    key_rows = split_heads(packed[:, columns : 2 * columns], head_size)
    values = split_heads(packed[:, 2 * columns :], head_size)
    scaling = head_size ** (-0.5)
    scores = (
        jnp.einsum("bqhd,bkhd->bhqk", queries, key_rows, preferred_element_type=jnp.float32)
        * scaling
    )
    weights = jax.nn.softmax(scores, axis=-1)
    rounded = weights.astype(jnp.bfloat16)
    upstream = split_heads(grad_out, head_size)
    grad_values = jnp.einsum(
        "bhqk,bqhd->bkhd", rounded, upstream, preferred_element_type=jnp.float32
    )
    dprob = jnp.einsum("bqhd,bkhd->bhqk", upstream, values, preferred_element_type=jnp.float32)
    dscore = weights * (dprob - jnp.sum(dprob * weights, axis=-1, keepdims=True)) * scaling
    dscore = dscore.astype(jnp.bfloat16)
    grad_queries = jnp.einsum(
        "bhqk,bkhd->bqhd", dscore, key_rows, preferred_element_type=jnp.float32
    )
    grad_keys = jnp.einsum("bhqk,bqhd->bkhd", dscore, queries, preferred_element_type=jnp.float32)
    row_count = packed.shape[0]
    joined = [
        grad_queries.reshape(row_count, columns),
        grad_keys.reshape(row_count, columns),
        grad_values.reshape(row_count, columns),
    ]
    return jnp.concatenate(joined, axis=1).astype(jnp.bfloat16)


def body(tokens, rotation, qkv_weight, proj_weight, up_weight, down_weight, cotangent):
    row_count, columns = tokens.shape
    half_width = columns // 2
    head_size = columns // HEADS
    peers = lax.axis_size("wide")
    group_size = lax.axis_size("narrow")
    capacity = row_count // peers + row_count // peers // 2
    residual = tokens.astype(jnp.float32)
    first_scale = row_scale(residual)
    normed = (residual * first_scale).astype(jnp.bfloat16)
    packed = jnp.dot(normed, qkv_weight, preferred_element_type=jnp.float32).astype(jnp.bfloat16)
    local_part = packed[:, : 3 * half_width]
    target = rotation // row_count // group_size
    position = rotation % row_count
    onehot = (target[:, None] == jnp.arange(peers, dtype=jnp.int32)[None, :]).astype(jnp.int32)
    slot_index = jnp.sum((jnp.cumsum(onehot, axis=0) - onehot) * onehot, axis=1)
    send_rows = (
        jnp.zeros((peers, capacity, 3 * half_width), jnp.bfloat16)
        .at[target, slot_index]
        .set(packed[:, 3 * half_width :])
    )
    send_pos = (
        jnp.full((peers, capacity), row_count, jnp.int32).at[target, slot_index].set(position)
    )
    got_rows, got_pos = (
        lax.all_to_all(send_rows, "wide", split_axis=0, concat_axis=0, tiled=True),
        lax.all_to_all(send_pos, "wide", split_axis=0, concat_axis=0, tiled=True),
    )
    arrived = got_pos.reshape(-1)
    moved_part = (
        jnp.zeros((row_count, 3 * half_width), jnp.bfloat16)
        .at[arrived]
        .set(got_rows.reshape(-1, 3 * half_width), mode="drop")
    )
    local_heads = attend(local_part, head_size)
    moved_out = attend(moved_part, head_size)
    outgoing = jnp.take(moved_out, arrived, axis=0, mode="fill", fill_value=0).reshape(
        peers, capacity, half_width
    )
    returned = lax.all_to_all(outgoing, "wide", split_axis=0, concat_axis=0, tiled=True)
    moved_heads = returned[target, slot_index]
    mixed_heads = jnp.concatenate([local_heads, moved_heads], axis=1)
    middle = (
        residual + jnp.dot(mixed_heads, proj_weight, preferred_element_type=jnp.float32)
    ).astype(jnp.bfloat16)
    middle_f = middle.astype(jnp.float32)
    second_scale = row_scale(middle_f)
    second_normed = (middle_f * second_scale).astype(jnp.bfloat16)
    all_normed = lax.all_gather(second_normed, "narrow", axis=0, tiled=True)
    pre_act = jnp.dot(all_normed, up_weight, preferred_element_type=jnp.float32)
    activated = gelu_tanh(pre_act).astype(jnp.bfloat16)
    partial_mix = jnp.dot(activated, down_weight, preferred_element_type=jnp.float32)
    mixed = lax.psum_scatter(
        partial_mix.astype(jnp.bfloat16), "narrow", scatter_dimension=0, tiled=True
    ).astype(jnp.float32)
    output = (middle_f + mixed).astype(jnp.bfloat16)
    all_cotangent = lax.all_gather(cotangent, "narrow", axis=0, tiled=True)
    grad_act = lax.dot_general(
        all_cotangent, down_weight, (((1,), (1,)), ((), ())), preferred_element_type=jnp.float32
    ).astype(jnp.bfloat16)
    pullback = jax.vjp(gelu_tanh, pre_act)[1]
    grad_pre = pullback(grad_act.astype(jnp.float32))[0].astype(jnp.bfloat16)
    down_share = lax.dot_general(
        activated, all_cotangent, (((0,), (0,)), ((), ())), preferred_element_type=jnp.float32
    )
    up_share = lax.dot_general(
        all_normed, grad_pre, (((0,), (0,)), ((), ())), preferred_element_type=jnp.float32
    )
    partial_back = lax.dot_general(
        grad_pre, up_weight, (((1,), (1,)), ((), ())), preferred_element_type=jnp.float32
    )
    grad_second = lax.psum_scatter(
        partial_back.astype(jnp.bfloat16), "narrow", scatter_dimension=0, tiled=True
    ).astype(jnp.float32)
    grad_up, grad_down = (
        lax.psum(up_share.astype(jnp.bfloat16), "wide").astype(jnp.float32),
        lax.psum(down_share.astype(jnp.bfloat16), "wide").astype(jnp.float32),
    )
    grad_middle = (
        cotangent.astype(jnp.float32) + norm_back(middle_f, second_scale, grad_second)
    ).astype(jnp.bfloat16)
    grad_heads = lax.dot_general(
        grad_middle, proj_weight, (((1,), (1,)), ((), ())), preferred_element_type=jnp.float32
    ).astype(jnp.bfloat16)
    proj_local = lax.dot_general(
        mixed_heads, grad_middle, (((0,), (0,)), ((), ())), preferred_element_type=jnp.float32
    )
    send_grad = (
        jnp.zeros((peers, capacity, half_width), jnp.bfloat16)
        .at[target, slot_index]
        .set(grad_heads[:, half_width:])
    )
    got_grad = lax.all_to_all(send_grad, "wide", split_axis=0, concat_axis=0, tiled=True)
    moved_grad = (
        jnp.zeros((row_count, half_width), jnp.bfloat16)
        .at[arrived]
        .set(got_grad.reshape(-1, half_width), mode="drop")
    )
    grad_local = attend_back(local_part, grad_heads[:, :half_width], head_size)
    grad_placed = attend_back(moved_part, moved_grad, head_size)
    grad_outgoing = jnp.take(grad_placed, arrived, axis=0, mode="fill", fill_value=0).reshape(
        peers, capacity, 3 * half_width
    )
    grad_returned = lax.all_to_all(grad_outgoing, "wide", split_axis=0, concat_axis=0, tiled=True)
    grad_moved = grad_returned[target, slot_index]
    grad_packed = jnp.concatenate([grad_local, grad_moved], axis=1)
    qkv_local = lax.dot_general(
        normed, grad_packed, (((0,), (0,)), ((), ())), preferred_element_type=jnp.float32
    )
    grad_first = lax.dot_general(
        grad_packed, qkv_weight, (((1,), (1,)), ((), ())), preferred_element_type=jnp.float32
    )
    grad_tokens = (
        grad_middle.astype(jnp.float32) + norm_back(residual, first_scale, grad_first)
    ).astype(jnp.bfloat16)
    grad_qkv, grad_proj = lax.psum((qkv_local, proj_local), ("wide", "narrow"))
    return (output, grad_tokens, grad_qkv, grad_proj, grad_up, grad_down)


def solution(mesh):
    return jax.shard_map(
        body,
        mesh=mesh,
        in_specs=(
            P(("wide", "narrow"), None),
            P(("wide", "narrow")),
            P(),
            P(),
            P(None, "narrow"),
            P("narrow", None),
            P(("wide", "narrow"), None),
        ),
        out_specs=(
            P(("wide", "narrow"), None),
            P(("wide", "narrow"), None),
            P(),
            P(),
            P(None, "narrow"),
            P("narrow", None),
        ),
        check_vma=False,
    )
```

profile of v0, /device:TPU:1, one launch (start us, length us, event | category | flops | bytes accessed | tf_op | source)
XLA Modules:
  0.0 767.5 jit_solution(8731971695286520005)
XLA Ops:
  8.0 9.0 %reduce-window.6 = s32[32,8,128]{2,1,0:T(8,128)S(1)} reduce-window(s32[32,8,128]{2,1,0:T(8,128)S(1)} %fusion.115, s32[]{:T(128)} %constant.93.clone.1), window={size=1x1x128 pad=0_0x0_0x127_0}, to_apply=%region_3.4 | reduce-window | flops 4161536 | bytes 262148 | tf_op jit(solution)/shard_map/reduce-window
  19.1 4.3 scatter_custom_fusion.2
  24.1 9.4 %all-to-all-start = ((s32[32,1,48]{2,1,0:T(1,128)}), s32[32,1,48]{2,1,0:T(1,128)S(1)}, u32[]{:S(2)}, u32[]{:S(2)}) async-start(s32[32,1,48]{2,1,0:T(1,128)} %all_to_all.18), calls=%async_computation | async-start | bytes 32768 | tf_op jit(solution)/shard_map/all_to_all | solution.py:104
  35.3 3.5 convolution_convert_fusion.3
  38.8 7.4 scatter_custom_fusion.3
  46.3 7.8 %all-to-all-start.1 = ((bf16[32,48,768]{2,1,0:T(8,128)(2,1)}), bf16[32,48,768]{2,1,0:T(8,128)(2,1)}, u32[]{:S(2)}, u32[]{:S(2)}) async-start(bf16[32,48,768]{2,1,0:T(8,128)(2,1)} %bitcast.88), calls=%async_computation.1 | async-start | bytes 4718592 | tf_op jit(solution)/shard_map/all_to_all | solution.py:103
  66.5 18.3 %all-to-all-done.1 = bf16[32,48,768]{2,1,0:T(8,128)(2,1)} async-done(((bf16[32,48,768]{2,1,0:T(8,128)(2,1)}), bf16[32,48,768]{2,1,0:T(8,128)(2,1)}, u32[]{:S(2)}, u32[]{:S(2)}) %all-to-all-start.1) | async-done | bytes 2359328 | tf_op jit(solution)/shard_map/all_to_all | solution.py:103
  84.8 9.4 %scatter_custom_fusion = bf16[1024,768]{1,0:T(8,128)(2,1)} fusion(s32[1536]{0:T(1024)S(1)} %fusion.116, bf16[1536,768]{1,0:T(8,128)(2,1)} %bitcast.8, bf16[]{:T(256)} %constant.101.clone.1), kind=kCustom, calls=%fused_computation.111 | custom fusion | bytes 1573376 | tf_op jit(solution)/shard_map/scatter | solution.py:110
  109.4 4.9 fusion.136
  114.3 3.5 fusion.78
  122.1 5.4 gather_fusion
  129.8 6.1 all-to-all-start.2
  136.2 4.7 fusion.135
  145.9 3.6 fusion.77
  156.4 10.7 %gather_fusion.1 = bf16[1024,256]{1,0:T(8,128)(2,1)} fusion(bf16[32,48,256]{2,1,0:T(8,128)(2,1)S(1)} %all-to-all-done.2, s32[1024]{0:T(1024)S(1)} %bitcast.85), kind=kCustom, calls=%fused_computation.1 | custom fusion | bytes 1056768 | tf_op jit(solution)/shard_map/gather | solution.py:118
  174.8 48.3 %all-gather.3.cloned.1.call-done = bf16[4096,512]{0,1:T(8,128)(2,1)} async-done(((bf16[1024,512]{0,1:T(8,128)(2,1)}), bf16[4096,512]{0,1:T(8,128)(2,1)}) %all-gather.3.cloned.1.call-update) | async-done | bytes 4194320 | tf_op jit(solution)/shard_map/all_gather | solution.py:126
  223.1 7.8 %fusion.137 = f32[4096,512]{1,0:T(8,128)} fusion(bf16[4096,512]{0,1:T(8,128)(2,1)} %all-gather.3.cloned.1.call-done, bf16[512,512]{1,0:T(8,128)(2,1)S(1)} %copy-done.14), kind=kOutput, calls=%fused_computation.182 | convolution fusion | flops 2147483648 | bytes 13107200 | tf_op jit(solution)/shard_map/dot_general | solution.py:127
  230.9 42.5 %all-gather.5.cloned.1.call-done = bf16[4096,512]{1,0:T(8,128)(2,1)} async-done(((bf16[1024,512]{1,0:T(8,128)(2,1)}), bf16[4096,512]{1,0:T(8,128)(2,1)}) %all-gather.5.cloned.1.call-update) | async-done | bytes 4194320 | tf_op jit(solution)/shard_map/all_gather | solution.py:134
  273.4 9.7 %fusion.6 = bf16[4096,512]{1,0:T(8,128)(2,1)S(1)} fusion(f32[4096,512]{1,0:T(8,128)} %fusion.137, bf16[4096,512]{1,0:T(8,128)(2,1)} %all-gather.5.cloned.1.call-done, bf16[512,512]{1,0:T(8,128)(2,1)S(1)} %copy-done.21), kind=kOutput, calls=%fused_computation.19 | convolution fusion | flops 2193620992 | bytes 17301504 | tf_op jit(solution)/shard_map/dot_general | solution.py:135
  285.1 4.3 convolution_convert_fusion
  289.7 7.4 convolution_convert_fusion.2
  299.5 37.3 %reduce-scatter.5.cloned.1.call-done = bf16[1024,512]{0,1:T(8,128)(2,1)} async-done(((bf16[4096,512]{0,1:T(8,128)(2,1)}), bf16[1024,512]{0,1:T(8,128)(2,1)}) %reduce-scatter.5.cloned.1.call-update) | async-done | bytes 1048592 | tf_op jit(solution)/shard_map/reduce_scatter | solution.py:149
  338.5 47.2 %reduce-scatter.3.cloned.1.call-done = bf16[1024,512]{0,1:T(8,128)(2,1)} async-done(((bf16[4096,512]{0,1:T(8,128)(2,1)}), bf16[1024,512]{0,1:T(8,128)(2,1)}) %reduce-scatter.3.cloned.1.call-update) | async-done | bytes 1048592 | tf_op jit(solution)/shard_map/reduce_scatter | solution.py:130
  385.7 3.8 fusion.46
  391.4 5.9 scatter_custom_fusion.4
  397.3 7.7 all-to-all-start.3
  404.9 8.6 %convolution_convert_fusion.5 = bf16[512,512]{1,0:T(8,128)(2,1)} fusion(bf16[4096,512]{1,0:T(8,128)(2,1)} %all-gather.5.cloned.1.call-done, f32[4096,512]{1,0:T(8,128)} %fusion.137), kind=kOutput, calls=%fused_computation.91 | convolution fusion | flops 2166620160 | bytes 13107200 | tf_op jit(solution)/shard_map/dot_general | solution.py:140
  413.5 5.7 all-to-all-done.3
  419.2 8.4 %scatter_custom_fusion.1 = bf16[1024,256]{1,0:T(8,128)(2,1)} fusion(s32[1536]{0:T(1024)S(1)} %fusion.116, bf16[1536,256]{1,0:T(8,128)(2,1)} %bitcast.16, bf16[]{:T(256)} %constant.101.clone.1), kind=kCustom, calls=%fused_computation.119 | custom fusion | bytes 524800 | tf_op jit(solution)/shard_map/scatter | solution.py:174
  430.9 3.8 fusion.139
  434.7 8.0 %fusion.90 = bf16[4,256,4,64]{1,3,2,0:T(8,128)(2,1)} fusion(bf16[4,256,4,64]{1,3,2,0:T(8,128)(2,1)S(1)} %copy-done.18, f32[4,4,256,256]{2,3,1,0:T(8,128)} %fusion.139, f32[4,4,256,256]{2,3,1,0:T(8,128)} %get-tuple-element.50, f32[4,4,256]{2,1,0:T(4,128)S(1)} %get-tuple-element.49), kind=kOutput, calls=%fused_computation.104 | convolution fusion | flops 141824256 | bytes 9453568 | tf_op jit(solution)/shard_map/bhqk,bkhd->bqhd/dot_general | solution.py:65
  442.8 8.1 %fusion.87 = bf16[4,256,4,64]{1,3,2,0:T(8,128)(2,1)} fusion(bf16[4,256,4,64]{1,3,2,0:T(8,128)(2,1)S(1)} %copy-done.17, f32[4,4,256,256]{2,3,1,0:T(8,128)} %fusion.139, f32[4,4,256,256]{2,3,1,0:T(8,128)} %get-tuple-element.50, f32[4,4,256]{2,1,0:T(4,128)S(1)} %get-tuple-element.49), kind=kOutput, calls=%fused_computation.103 | convolution fusion | flops 141824256 | bytes 9453568 | tf_op jit(solution)/shard_map/bhqk,bqhd->bkhd/dot_general | solution.py:68
  450.8 3.0 fusion.80
  463.4 5.6 gather_fusion.2
  469.0 3.4 broadcast_select_fusion
  472.4 5.0 all-to-all-start.4
  477.4 6.6 convolution_convert_fusion.6
  486.0 4.0 fusion.79
  493.0 3.8 fusion.138
  496.8 8.0 %fusion.81 = bf16[4,256,4,64]{1,3,2,0:T(8,128)(2,1)} fusion(bf16[4,256,4,64]{1,3,2,0:T(8,128)(2,1)S(1)} %copy-done.16, f32[4,4,256,256]{2,3,1,0:T(8,128)} %fusion.138, f32[4,4,256,256]{2,3,1,0:T(8,128)} %get-tuple-element.48, f32[4,4,256]{2,1,0:T(4,128)S(1)} %get-tuple-element.47), kind=kOutput, calls=%fused_computation.101 | convolution fusion | flops 141824256 | bytes 9453568 | tf_op jit(solution)/shard_map/bhqk,bqhd->bkhd/dot_general | solution.py:68
  507.9 8.0 %fusion.84 = bf16[4,256,4,64]{1,3,2,0:T(8,128)(2,1)} fusion(bf16[4,256,4,64]{1,3,2,0:T(8,128)(2,1)S(1)} %copy-done.15, f32[4,4,256,256]{2,3,1,0:T(8,128)} %fusion.138, f32[4,4,256,256]{2,3,1,0:T(8,128)} %get-tuple-element.48, f32[4,4,256]{2,1,0:T(4,128)S(1)} %get-tuple-element.47), kind=kOutput, calls=%fused_computation.102 | convolution fusion | flops 141824256 | bytes 9453568 | tf_op jit(solution)/shard_map/bhqk,bkhd->bqhd/dot_general | solution.py:65
  523.6 3.3 fusion.140
  526.9 19.6 %gather_fusion.3 = bf16[1024,768]{1,0:T(8,128)(2,1)} fusion(bf16[32,48,768]{2,1,0:T(8,128)(2,1)} %all-to-all-done.4, s32[1024]{0:T(1024)S(1)} %bitcast.86), kind=kCustom, calls=%fused_computation.3 | custom fusion | bytes 3153920 | tf_op jit(solution)/shard_map/gather | solution.py:182
  549.1 5.4 fusion.98
  554.6 41.3 %all-reduce.7.cloned.1.call-done = (bf16[512,512]{1,0:T(8,128)(2,1)}, bf16[512,512]{1,0:T(8,128)(2,1)}) async-done(((bf16[512,512]{1,0:T(8,128)(2,1)}, bf16[512,512]{1,0:T(8,128)(2,1)}), (bf16[512,512]{1,0:T(8,128)(2,1)}, bf16[512,512]{1,0:T(8,128)(2,1)})) %all-reduce.7.cloned.1.call-update) | async-done | bytes 1048592 | tf_op jit(solution)/shard_map/psum | solution.py:153
  602.4 3.8 fusion.48
  610.1 145.3 %all-reduce.5.cloned.1.call-done = (f32[512,1536]{1,0:T(8,128)}, f32[512,512]{1,0:T(8,128)}) async-done(((f32[512,1536]{1,0:T(8,128)}, f32[512,512]{1,0:T(8,128)}), (f32[512,1536]{1,0:T(8,128)}, f32[512,512]{1,0:T(8,128)})) %all-reduce.5.cloned.1.call-update) | async-done | bytes 4194320 | tf_op jit(solution)/shard_map/psum | solution.py:193
  755.4 3.8 copy.251
  (144 shorter events, 109.8 us)
Async XLA Ops:
  7.2 28.1 %copy-start = (bf16[512,1536]{1,0:T(8,128)(2,1)S(1)}, bf16[512,1536]{1,0:T(8,128)(2,1)}, u32[]{:S(2)}) copy-start(bf16[512,1536]{1,0:T(8,128)(2,1)} %param.9) | copy-start | bytes 4718596
  24.1 22.2 %all-to-all-start = ((s32[32,1,48]{2,1,0:T(1,128)}), s32[32,1,48]{2,1,0:T(1,128)S(1)}, u32[]{:S(2)}, u32[]{:S(2)}) async-start(s32[32,1,48]{2,1,0:T(1,128)} %all_to_all.18), calls=%async_computation | async-start | bytes 32768 | tf_op jit(solution)/shard_map/all_to_all | solution.py:104
  35.0 133.9 %copy-start.1 = (bf16[1024,512]{0,1:T(8,128)(2,1)}, bf16[1024,512]{0,1:T(8,128)(2,1)S(1)}, u32[]{:S(2)}) copy-start(bf16[1024,512]{0,1:T(8,128)(2,1)S(1)} %copy.143) | copy-start | bytes 3145732
  35.3 3.5 copy-start.19
  46.3 38.5 %all-to-all-start.1 = ((bf16[32,48,768]{2,1,0:T(8,128)(2,1)}), bf16[32,48,768]{2,1,0:T(8,128)(2,1)}, u32[]{:S(2)}, u32[]{:S(2)}) async-start(bf16[32,48,768]{2,1,0:T(8,128)(2,1)} %bitcast.88), calls=%async_computation.1 | async-start | bytes 4718592 | tf_op jit(solution)/shard_map/all_to_all | solution.py:103
  109.4 8.4 %copy-start.8 = (bf16[4,256,4,64]{1,3,2,0:T(8,128)(2,1)}, bf16[4,256,4,64]{1,3,2,0:T(8,128)(2,1)S(1)}, u32[]{:S(2)}) copy-start(bf16[4,256,4,64]{1,3,2,0:T(8,128)(2,1)S(1)} %copy.159) | copy-start | bytes 1572868
  129.8 26.6 %all-to-all-start.2 = ((bf16[32,48,256]{2,1,0:T(8,128)(2,1)}), bf16[32,48,256]{2,1,0:T(8,128)(2,1)S(1)}, u32[]{:S(2)}, u32[]{:S(2)}) async-start(bf16[32,48,256]{2,1,0:T(8,128)(2,1)} %broadcast_select_fusion.1), calls=%async_computation.2 | async-start | bytes 1572864 | tf_op jit(solution)/shard_map/all_to_all | solution.py:117
  135.9 87.2 %all-gather.3.cloned.1.call-start = ((), (), s32[]{:S(2)}) async-start(), calls=%async_computation.7 | async-start | bytes 5242880 | tf_op jit(solution)/shard_map/all_gather | solution.py:126
  169.0 54.1 %copy-start.14 = (bf16[512,512]{1,0:T(8,128)(2,1)S(1)}, bf16[512,512]{1,0:T(8,128)(2,1)}, u32[]{:S(2)}) copy-start(bf16[512,512]{1,0:T(8,128)(2,1)} %param.11) | copy-start | bytes 1572868
  171.2 1.0 copy-start.3
  173.4 100.0 %all-gather.5.cloned.1.call-start = ((), (), s32[]{:S(2)}) async-start(), calls=%async_computation.9 | async-start | bytes 5242880 | tf_op jit(solution)/shard_map/all_gather | solution.py:134
  174.2 99.3 %copy-start.21 = (bf16[512,512]{1,0:T(8,128)(2,1)S(1)}, bf16[512,512]{1,0:T(8,128)(2,1)}, u32[]{:S(2)}) copy-start(bf16[512,512]{1,0:T(8,128)(2,1)} %param.12) | copy-start | bytes 1572868
  174.2 162.6 %reduce-scatter.5.cloned.1.call-start = ((), (), s32[]{:S(2)}) async-start(), calls=%async_computation.10 | async-start | bytes 5242880 | tf_op jit(solution)/shard_map/reduce_scatter | solution.py:149
  283.2 1.9 copy-start.23
  289.4 96.3 %reduce-scatter.3.cloned.1.call-start = ((), (), s32[]{:S(2)}) async-start(), calls=%async_computation.8 | async-start | bytes 5242880 | tf_op jit(solution)/shard_map/reduce_scatter | solution.py:130
  297.1 39.7 %copy-start.4 = (bf16[1024,512]{0,1:T(8,128)(2,1)S(1)}, bf16[1024,512]{0,1:T(8,128)(2,1)}, u32[]{:S(2)}) copy-start(bf16[1024,512]{0,1:T(8,128)(2,1)} %copy-done.3) | copy-start | bytes 3145732
  299.4 91.2 %copy-start.22 = (bf16[512,512]{1,0:T(8,128)(2,1)S(1)}, bf16[512,512]{1,0:T(8,128)(2,1)}, u32[]{:S(2)}) copy-start(bf16[512,512]{1,0:T(8,128)(2,1)} %param.10) | copy-start | bytes 1572868
  389.6 1.0 copy-start.5
  391.4 22.1 %copy-start.12 = (bf16[1024,512]{1,0:T(8,128)(2,1)}, bf16[1024,512]{1,0:T(8,128)(2,1)S(1)}, u32[]{:S(2)}) copy-start(bf16[1024,512]{1,0:T(8,128)(2,1)S(1)} %convolution_convert_fusion.4) | copy-start | bytes 3145732
  397.3 21.9 %all-to-all-start.3 = ((bf16[32,48,256]{2,1,0:T(8,128)(2,1)}), bf16[32,48,256]{2,1,0:T(8,128)(2,1)}, u32[]{:S(2)}, u32[]{:S(2)}) async-start(bf16[32,48,256]{2,1,0:T(8,128)(2,1)} %bitcast.15), calls=%async_computation.5 | async-start | bytes 1572864 | tf_op jit(solution)/shard_map/all_to_all | solution.py:170
  404.9 26.0 %copy-start.9 = (bf16[4,256,4,64]{1,3,2,0:T(8,128)(2,1)S(1)}, bf16[4,256,4,64]{1,3,2,0:T(8,128)(2,1)}, u32[]{:S(2)}) copy-start(bf16[4,256,4,64]{1,3,2,0:T(8,128)(2,1)} %copy-done.8) | copy-start | bytes 1572868
  430.9 3.8 copy-start.18
  434.7 8.0 %copy-start.17 = (bf16[4,256,4,64]{1,3,2,0:T(8,128)(2,1)S(1)}, bf16[4,256,4,64]{1,3,2,0:T(8,128)(2,1)}, u32[]{:S(2)}) copy-start(bf16[4,256,4,64]{1,3,2,0:T(8,128)(2,1)} %copy.157) | copy-start | bytes 1572868
  442.8 8.1 %copy-start.10 = (bf16[4,256,4,64]{1,3,2,0:T(8,128)(2,1)S(1)}, bf16[4,256,4,64]{1,3,2,0:T(8,128)(2,1)}, u32[]{:S(2)}) copy-start(bf16[4,256,4,64]{1,3,2,0:T(8,128)(2,1)} %copy.180) | copy-start | bytes 1572868
  472.4 54.5 %all-to-all-start.4 = ((bf16[32,48,768]{2,1,0:T(8,128)(2,1)}), bf16[32,48,768]{2,1,0:T(8,128)(2,1)}, u32[]{:S(2)}, u32[]{:S(2)}) async-start(bf16[32,48,768]{2,1,0:T(8,128)(2,1)} %broadcast_select_fusion), calls=%async_computation.6 | async-start | bytes 4718592 | tf_op jit(solution)/shard_map/all_to_all | solution.py:181
  477.3 6.7 slice-start
  477.4 118.5 %all-reduce.7.cloned.1.call-start = ((), (), s32[]{:S(2)}) async-start(), calls=%async_computation.12 | async-start | bytes 2097152 | tf_op jit(solution)/shard_map/psum | solution.py:153
  484.0 271.4 %all-reduce.5.cloned.1.call-start = ((), (), s32[]{:S(2)}) async-start(), calls=%async_computation.11 | async-start | bytes 8388608 | tf_op jit(solution)/shard_map/psum | solution.py:193
  486.0 7.0 copy-start.7
  493.0 3.8 copy-start.16
  496.8 11.1 %copy-start.15 = (bf16[4,256,4,64]{1,3,2,0:T(8,128)(2,1)S(1)}, bf16[4,256,4,64]{1,3,2,0:T(8,128)(2,1)}, u32[]{:S(2)}) copy-start(bf16[4,256,4,64]{1,3,2,0:T(8,128)(2,1)} %copy.148) | copy-start | bytes 1572868
  515.9 6.8 copy-start.11
  526.9 22.2 %copy-start.2 = (bf16[1024,512]{0,1:T(8,128)(2,1)S(1)}, bf16[1024,512]{0,1:T(8,128)(2,1)}, u32[]{:S(2)}) copy-start(bf16[1024,512]{0,1:T(8,128)(2,1)} %copy-done.1) | copy-start | bytes 3145732
  526.9 22.2 %copy-start.20 = (f32[1024]{0:T(1024)S(1)}, f32[1024]{0:T(1024)}, u32[]{:S(2)}) copy-start(f32[1024]{0:T(1024)} %copy-done.19) | copy-start | bytes 12292
  602.4 3.8 copy-start.6
  755.4 3.8 copy-start.13
Sparse Core Ops, SparseCore 0:
  173.5 49.5 all-gather.2
  224.8 48.6 all-gather.4
  289.6 47.1 reduce-scatter.4
  339.2 46.5 reduce-scatter.2
  484.2 111.5 all-reduce.6
  601.6 153.7 all-reduce.4
where the time goes:
time: 776 us; the launch traced here: 768 us
  waiting for transfers between devices  387 us (50%)
  local copies, waits for them, and re-layouts  169 us (22%)
  matrix products  127 us (16%)
  starting transfers between devices  37.2 us (5%)
  other arithmetic  32.3 us (4%)
  between operations  15 us (2%)
    psum x1, waiting for transfers between devices, body(): grad_qkv, grad_proj = lax.psum((qkv_local, proj_local), ('wide', 'narrow'))  145 us
    all_gather x1, waiting for transfers between devices, body(): all_normed = lax.all_gather(second_normed, 'narrow', axis=0, tiled=True)  48.3 us
    reduce_scatter x1, waiting for transfers between devices, body(): lax.psum_scatter(partial_mix.astype(jnp.bfloat16), 'narrow', scatter_dime...  47.2 us
    all_gather x1, waiting for transfers between devices, body(): all_cotangent = lax.all_gather(cotangent, 'narrow', axis=0, tiled=True)  42.5 us
    unnamed x61, local copies, waits for them, and re-layouts  41.3 us
    psum x1, waiting for transfers between devices, body(): lax.psum(up_share.astype(jnp.bfloat16), 'wide').astype(jnp.float32)  41.3 us
    reduce_scatter x1, waiting for transfers between devices, body(): lax.psum_scatter(partial_back.astype(jnp.bfloat16), 'narrow', scatter_dim...  37.3 us
    reshape x16, local copies, waits for them, and re-layouts, split_heads(): block.reshape(row_count // BALL, BALL, columns // head_size, head_size)  31.4 us
  transfers between devices with their start and end apart: 11, of which 8 were waited for; matrix products, arithmetic and copies ran while one was open for 21% of the time, Pallas kernels for 0%

commit v1 on v0

v1 whole, which is shorter than its diff:
```python
import jax
import jax.numpy as jnp
from jax import lax
from jax.experimental import pallas as pl
from jax.experimental.pallas import tpu as pltpu
from jax.sharding import PartitionSpec as P

HEADS = 8
BALL = 256
EPSILON = 1e-06
LANES = 128
VMEM_BYTES = 56 * 1024 * 1024

F32 = jnp.float32
BF16 = jnp.bfloat16


def mm(left, right):
    return lax.dot_general(left, right, (((1,), (0,)), ((), ())), preferred_element_type=F32)


def mm_nt(left, right):
    return lax.dot_general(left, right, (((1,), (1,)), ((), ())), preferred_element_type=F32)


def mm_tn(left, right):
    return lax.dot_general(left, right, (((0,), (0,)), ((), ())), preferred_element_type=F32)


def iota(shape, dimension):
    return lax.broadcasted_iota(jnp.int32, shape, dimension)


def row_scale(values):
    return lax.rsqrt(jnp.mean(values * values, axis=-1, keepdims=True) + EPSILON)


def norm_back(values, scaling, gradient):
    unit = values * scaling
    return scaling * (gradient - unit * jnp.mean(gradient * unit, axis=-1, keepdims=True))


def flip(block):
    return block.astype(F32).T.astype(BF16)


def as_column(row):
    return jnp.broadcast_to(row, (8, row.shape[1])).T[:, :1]


def onehot(condition):
    return jnp.where(condition, 1.0, 0.0).astype(BF16)


def head_mask(columns, head, head_size, value):
    lane = iota((1, columns), 1)
    inside = (lane >= head * head_size) & (lane < (head + 1) * head_size)
    return jnp.where(inside, value, 0.0).astype(BF16)


def ball_weights(queries, key_rows, head, head_size):
    columns = queries.shape[1]
    asked = queries * head_mask(columns, head, head_size, head_size ** (-0.5))
    scores = mm_nt(key_rows, asked)
    raised = jnp.exp(scores - jnp.max(scores, axis=0, keepdims=True))
    return raised * (1.0 / jnp.sum(raised, axis=0, keepdims=True)), asked


def ball_attend(packed, head_size):
    columns = packed.shape[1] // 3
    queries, key_rows = packed[:, :columns], packed[:, columns : 2 * columns]
    values_t = flip(packed[:, 2 * columns :])
    parts = []
    for head in range(columns // head_size):
        weights, _ = ball_weights(queries, key_rows, head, head_size)
        own = values_t[head * head_size : (head + 1) * head_size]
        parts.append(mm(own, weights.astype(BF16)))
    return jnp.concatenate(parts, axis=0).T.astype(BF16)


def ball_attend_back(packed, grad_out, head_size):
    columns = packed.shape[1] // 3
    queries, key_rows = packed[:, :columns], packed[:, columns : 2 * columns]
    values = packed[:, 2 * columns :]
    keys_t = flip(key_rows * jnp.asarray(head_size ** (-0.5), BF16))
    asked_all, upstream_all, rounded_all, dscore_all, grad_queries = [], [], [], [], []
    for head in range(columns // head_size):
        weights, asked = ball_weights(queries, key_rows, head, head_size)
        upstream = grad_out * head_mask(columns, head, head_size, 1.0)
        dprob = mm_nt(values, upstream)
        dscore = weights * (dprob - jnp.sum(dprob * weights, axis=0, keepdims=True))
        dscore = dscore.astype(BF16)
        own = keys_t[head * head_size : (head + 1) * head_size]
        grad_queries.append(mm(own, dscore))
        asked_all.append(asked)
        upstream_all.append(upstream)
        rounded_all.append(weights.astype(BF16))
        dscore_all.append(dscore)
    grad_values = mm(
        jnp.concatenate(rounded_all, axis=1), jnp.concatenate(upstream_all, axis=0)
    )
    grad_keys = mm(jnp.concatenate(dscore_all, axis=1), jnp.concatenate(asked_all, axis=0))
    grad_queries = jnp.concatenate(grad_queries, axis=0).T
    return jnp.concatenate([grad_queries, grad_keys, grad_values], axis=1).astype(BF16)


def call(kernel, outs, *args, scratch=(), flops=0, name=None):
    size = sum(a.size * a.dtype.itemsize for a in args)
    size += sum(o.size * o.dtype.itemsize for o in outs)
    return pl.pallas_call(
        kernel,
        out_shape=outs,
        in_specs=[pl.BlockSpec(memory_space=pltpu.VMEM)] * len(args),
        out_specs=[pl.BlockSpec(memory_space=pltpu.VMEM)] * len(outs),
        scratch_shapes=list(scratch),
        compiler_params=pltpu.CompilerParams(vmem_limit_bytes=VMEM_BYTES),
        cost_estimate=pl.CostEstimate(flops=flops, bytes_accessed=size, transcendentals=0),
        name=name,
    )(*args)


def shape(dims, dtype=BF16):
    return jax.ShapeDtypeStruct(dims, dtype)


def route_kernel(peers, group_size, capacity, rot_ref, tok_ref, send_ref, pos_ref, slot_ref):
    row_count = tok_ref.shape[0]
    rotation = rot_ref[...]
    target = rotation // (row_count * group_size)
    position = rotation % row_count + 1
    high = (position // 256).astype(F32)
    low = (position % 256).astype(F32)
    step = 256
    earlier = onehot(iota((step, step), 0) < iota((step, step), 1))
    carry = jnp.zeros((peers, 1), F32)
    sums_high = jnp.zeros((peers, LANES), F32)
    sums_low = jnp.zeros((peers, LANES), F32)
    slots = []
    for start in range(0, row_count, step):
        part = slice(start, start + step)
        chosen = jnp.where(iota((peers, step), 0) == target[:, part], 1.0, 0.0)
        before = mm(chosen.astype(BF16), earlier) + carry
        carry = carry + jnp.sum(chosen, axis=1, keepdims=True)
        rank = jnp.sum(chosen * before, axis=0, keepdims=True)
        slots.append(target[:, part] * capacity + rank.astype(jnp.int32))
        place = onehot(iota((LANES, step), 0) == rank.astype(jnp.int32))
        sums_high = sums_high + mm_nt((chosen * high[:, part]).astype(BF16), place)
        sums_low = sums_low + mm_nt((chosen * low[:, part]).astype(BF16), place)
    pos_ref[...] = (sums_high * 256.0 + sums_low).astype(jnp.int32) - 1
    slot = jnp.concatenate(slots, axis=1)
    slot_ref[...] = slot
    tokens = tok_ref[...]
    for start in range(0, peers * capacity, step):
        pick = onehot(iota((step, row_count), 0) + start == slot)
        send_ref[start : start + step, :] = mm(pick, tokens).astype(BF16)


def arrived_row(pos_ref, capacity):
    peers = pos_ref.shape[0]
    slots = peers * capacity
    position = pos_ref[...] + 1
    high = (position // 256).astype(F32).astype(BF16)
    low = (position % 256).astype(F32).astype(BF16)
    place = onehot(iota((LANES, slots), 0) == iota((LANES, slots), 1) % capacity)
    spread = mm(high, place) * 256.0 + mm(low, place)
    own = iota((peers, slots), 0) == iota((peers, slots), 1) // capacity
    return jnp.sum(jnp.where(own, spread, 0.0), axis=0, keepdims=True).astype(jnp.int32) - 1


def first_local_kernel(head_size, tok_ref, wq_ref, cot_ref, down_ref, nrm_ref, pk_ref, heads_ref, act_ref):
    row_count = tok_ref.shape[0]
    weight = wq_ref[...]
    for start in range(0, row_count, BALL):
        rows = slice(start, start + BALL)
        residual = tok_ref[rows, :].astype(F32)
        normed = (residual * row_scale(residual)).astype(BF16)
        nrm_ref[rows, :] = normed
        packed = mm(normed, weight).astype(BF16)
        pk_ref[rows, :] = packed
        heads_ref[rows, :] = ball_attend(packed, head_size)
        act_ref[rows, :] = mm_nt(cot_ref[rows, :], down_ref[...]).astype(BF16)


def moved_kernel(head_size, capacity, got_ref, pos_ref, wq_ref, nrm_ref, pk_ref, row_ref, out_ref, heads_ref):
    row_count = nrm_ref.shape[0]
    slots = got_ref.shape[0]
    arrived = arrived_row(pos_ref, capacity)
    row_ref[...] = arrived
    weight = wq_ref[...]
    got = got_ref[...]
    for start in range(0, row_count, BALL):
        rows = slice(start, start + BALL)
        pick = onehot(iota((BALL, slots), 0) + start == arrived)
        residual = mm(pick, got)
        normed = (residual * row_scale(residual)).astype(BF16)
        nrm_ref[rows, :] = normed
        packed = mm(normed, weight).astype(BF16)
        pk_ref[rows, :] = packed
        heads_ref[rows, :] = ball_attend(packed, head_size)
    back_rows(arrived, heads_ref, out_ref)


def back_rows(arrived, rows_ref, out_ref):
    slots, step = out_ref.shape[0], 256
    row_count = rows_ref.shape[0]
    arrived_col = as_column(arrived.astype(F32)).astype(jnp.int32)
    moved = rows_ref[...]
    for start in range(0, slots, step):
        pick = onehot(iota((step, row_count), 1) == arrived_col[start : start + step])
        out_ref[start : start + step, :] = mm(pick, moved).astype(BF16)


def middle_kernel(
    tok_ref, local_ref, ret_ref, slot_ref, proj_ref, up_ref, cot_ref, act_ref,
    mix_ref, mid_ref, sn_ref, gated_ref, pre_ref, gm_ref, gl_ref, send_ref, gh_ref,
):
    row_count, width = tok_ref.shape
    half = width // 2
    slots = ret_ref.shape[0]
    chunks = up_ref.shape[0] // width
    slot = slot_ref[...]
    slot_col = as_column(slot.astype(F32)).astype(jnp.int32)
    rate = 0.7978845608028654
    cubic = 0.044715 * rate
    for start in range(0, row_count, BALL):
        rows = slice(start, start + BALL)
        pick = onehot(iota((BALL, slots), 1) == slot_col[rows])
        moved = mm(pick, ret_ref[...]).astype(BF16)
        mixed = jnp.concatenate([local_ref[rows, :], moved], axis=1)
        mix_ref[rows, :] = mixed
        middle = (tok_ref[rows, :].astype(F32) + mm(mixed, proj_ref[...])).astype(BF16)
        mid_ref[rows, :] = middle
        middle_f = middle.astype(F32)
        second_scale = row_scale(middle_f)
        normed = (middle_f * second_scale).astype(BF16)
        sn_ref[rows, :] = normed
        grad_second = jnp.zeros((BALL, width), F32)
        for chunk in range(chunks):
            columns = slice(chunk * width, (chunk + 1) * width)
            up = up_ref[columns, :]
            pre = mm(normed, up)
            square = pre * pre
            curve = jnp.tanh(pre * (rate + cubic * square))
            upper = 0.5 + 0.5 * curve
            gated_ref[rows, columns] = (pre * upper).astype(BF16)
            slope = upper + pre * (0.5 - 0.5 * (curve * curve)) * (rate + 3.0 * cubic * square)
            grad_pre = (act_ref[rows, columns].astype(F32) * slope).astype(BF16)
            pre_ref[rows, columns] = grad_pre
            grad_second = grad_second + mm_nt(grad_pre, up)
        grad_middle = (
            cot_ref[rows, :].astype(F32) + norm_back(middle_f, second_scale, grad_second)
        ).astype(BF16)
        gm_ref[rows, :] = grad_middle
        grad_heads = mm_nt(grad_middle, proj_ref[...]).astype(BF16)
        gl_ref[rows, :] = grad_heads[:, :half]
        gh_ref[rows, :] = grad_heads[:, half:]
    moved_grad = gh_ref[...]
    for start in range(0, slots, 256):
        pick = onehot(iota((256, row_count), 0) + start == slot)
        send_ref[start : start + 256, :] = mm(pick, moved_grad).astype(BF16)


def weights_kernel(mid_ref, gated_ref, down_ref, cot_ref, sn_ref, pre_ref, out_ref, gup_ref, gdown_ref):
    row_count = mid_ref.shape[0]
    for start in range(0, row_count, BALL):
        rows = slice(start, start + BALL)
        mixed = mm(gated_ref[rows, :], down_ref[...])
        out_ref[rows, :] = (mid_ref[rows, :].astype(F32) + mixed).astype(BF16)
    width = sn_ref.shape[1]
    normed_t = flip(sn_ref[...])
    cot_t = flip(cot_ref[...])
    for start in range(0, pre_ref.shape[1], width):
        columns = slice(start, start + width)
        gup_ref[columns, :] = mm(normed_t, pre_ref[:, columns]).astype(BF16)
        gdown_ref[columns, :] = mm(cot_t, gated_ref[:, columns]).astype(BF16)


def local_back_kernel(head_size, pk_ref, gl_ref, nrm_ref, wq_ref, mix_ref, gm_ref, first_ref, gq_ref, gp_ref, gpk_ref):
    row_count = pk_ref.shape[0]
    for start in range(0, row_count, BALL):
        rows = slice(start, start + BALL)
        grad_packed = ball_attend_back(pk_ref[rows, :], gl_ref[rows, :], head_size)
        gpk_ref[rows, :] = grad_packed
        first_ref[rows, :] = mm_nt(grad_packed, wq_ref[...])
    gq_ref[...] = mm(flip(nrm_ref[...]), gpk_ref[...]).astype(BF16)
    gp_ref[...] = mm(flip(mix_ref[...]), gm_ref[...]).astype(BF16)


def moved_back_kernel(head_size, got_ref, row_ref, pk_ref, wq_ref, gpk_ref, out_ref, first_ref):
    row_count = pk_ref.shape[0]
    slots = got_ref.shape[0]
    arrived = row_ref[...]
    for start in range(0, row_count, BALL):
        rows = slice(start, start + BALL)
        pick = onehot(iota((BALL, slots), 0) + start == arrived)
        grad_out = mm(pick, got_ref[...]).astype(BF16)
        grad_packed = ball_attend_back(pk_ref[rows, :], grad_out, head_size)
        gpk_ref[rows, :] = grad_packed
        first_ref[rows, :] = mm_nt(grad_packed, wq_ref[...]).astype(BF16)
    back_rows(arrived, first_ref, out_ref)


def moved_weights_kernel(nrm_ref, gpk_ref, gq_ref):
    gq_ref[...] = mm(flip(nrm_ref[...]), gpk_ref[...]).astype(BF16)


def last_kernel(tok_ref, gm_ref, first_ref, ret_ref, slot_ref, out_ref):
    row_count = tok_ref.shape[0]
    slots = ret_ref.shape[0]
    slot_col = as_column(slot_ref[...].astype(F32)).astype(jnp.int32)
    for start in range(0, row_count, BALL):
        rows = slice(start, start + BALL)
        pick = onehot(iota((BALL, slots), 1) == slot_col[rows])
        grad_first = first_ref[rows, :] + mm(pick, ret_ref[...])
        residual = tok_ref[rows, :].astype(F32)
        out_ref[rows, :] = (
            gm_ref[rows, :].astype(F32) + norm_back(residual, row_scale(residual), grad_first)
        ).astype(BF16)


def exchange(rows, peers):
    slots, columns = rows.shape
    sent = rows.reshape(peers, slots // peers, columns)
    got = lax.all_to_all(sent, "wide", split_axis=0, concat_axis=0, tiled=True)
    return got.reshape(slots, columns)


def bind(kernel, *fixed):
    def bound(*refs):
        kernel(*fixed, *refs)

    return bound


def body(tokens, rotation, qkv_weight, proj_weight, up_weight, down_weight, cotangent):
    rows, width = tokens.shape
    half = width // 2
    head_size = width // HEADS
    peers = lax.axis_size("wide")
    group_size = lax.axis_size("narrow")
    capacity = rows // peers + rows // peers // 2
    slots = peers * capacity
    hidden = group_size * up_weight.shape[1]
    unit = 2 * rows * width * width

    send, send_pos, slot = call(
        bind(route_kernel, peers, group_size, capacity),
        [shape((slots, width)), shape((peers, LANES), jnp.int32), shape((1, rows), jnp.int32)],
        rotation.reshape(1, rows), tokens, flops=3 * unit, name="route",
    )
    got_pos = exchange(send_pos, peers)
    got = exchange(send, peers)
    all_up = lax.all_gather(up_weight, "narrow", axis=0, tiled=True)
    all_down = lax.all_gather(down_weight, "narrow", axis=0, tiled=True)

    normed, packed, local_heads, grad_act = call(
        bind(first_local_kernel, head_size),
        [shape((rows, width)), shape((rows, 3 * half)), shape((rows, half)), shape((rows, hidden))],
        tokens, qkv_weight[:, : 3 * half], cotangent, all_down, flops=8 * unit, name="first_local",
    )
    moved_weight = qkv_weight[:, 3 * half :]
    moved_normed, moved_packed, arrived, outgoing = call(
        bind(moved_kernel, head_size, capacity),
        [shape((rows, width)), shape((rows, 3 * half)), shape((1, slots), jnp.int32), shape((slots, half))],
        got, got_pos, moved_weight,
        scratch=[pltpu.VMEM((rows, half), BF16)], flops=8 * unit, name="moved",
    )
    returned = exchange(outgoing, peers)
    mixed_heads, middle, second_normed, activated, grad_pre, grad_middle, grad_local, send_grad = call(
        middle_kernel,
        [
            shape((rows, width)), shape((rows, width)), shape((rows, width)),
            shape((rows, hidden)), shape((rows, hidden)),
            shape((rows, width)), shape((rows, half)), shape((slots, half)),
        ],
        tokens, local_heads, returned, slot, proj_weight, all_up, cotangent, grad_act,
        scratch=[pltpu.VMEM((rows, half), BF16)], flops=16 * unit, name="middle",
    )
    got_grad = exchange(send_grad, peers)
    output, grad_up, grad_down = call(
        weights_kernel,
        [shape((rows, width)), shape((hidden, width)), shape((hidden, width))],
        middle, activated, all_down, cotangent, second_normed, grad_pre,
        flops=12 * unit, name="mlp_weights",
    )
    first_local, qkv_local, proj_share = call(
        bind(local_back_kernel, head_size),
        [shape((rows, width), F32), shape((width, 3 * half)), shape((width, width))],
        packed, grad_local, normed, qkv_weight[:, : 3 * half], mixed_heads, grad_middle,
        scratch=[pltpu.VMEM((rows, 3 * half), BF16)], flops=12 * unit, name="local_back",
    )
    moved_grad_packed, grad_outgoing = call(
        bind(moved_back_kernel, head_size),
        [shape((rows, 3 * half)), shape((slots, width))],
        got_grad, arrived, moved_packed, moved_weight,
        scratch=[pltpu.VMEM((rows, width), BF16)], flops=12 * unit, name="moved_back",
    )
    grad_returned = exchange(grad_outgoing, peers)
    (qkv_moved,) = call(
        moved_weights_kernel, [shape((width, 3 * half))], moved_normed, moved_grad_packed,
        flops=2 * unit, name="moved_weights",
    )
    (grad_tokens,) = call(
        last_kernel, [shape((rows, width))],
        tokens, grad_middle, first_local, grad_returned, slot, flops=3 * unit, name="last",
    )

    up_part = lax.psum_scatter(grad_up, "narrow", scatter_dimension=0, tiled=True)
    down_part = lax.psum_scatter(grad_down, "narrow", scatter_dimension=0, tiled=True)
    up_sum, down_sum = lax.psum((up_part, down_part), "wide")
    qkv_sum, proj_sum, moved_sum = lax.psum((qkv_local, proj_share, qkv_moved), ("wide", "narrow"))
    grad_qkv = jnp.concatenate([qkv_sum, moved_sum], axis=1).astype(F32)
    return (
        output, grad_tokens, grad_qkv, proj_sum.astype(F32),
        up_sum.astype(F32), down_sum.astype(F32).T,
    )


def solution(mesh):
    return jax.shard_map(
        body,
        mesh=mesh,
        in_specs=(
            P(("wide", "narrow"), None),
            P(("wide", "narrow")),
            P(),
            P(),
            P(None, "narrow"),
            P("narrow", None),
            P(("wide", "narrow"), None),
        ),
        out_specs=(
            P(("wide", "narrow"), None),
            P(("wide", "narrow"), None),
            P(),
            P(),
            P(None, "narrow"),
            P("narrow", None),
        ),
        check_vma=False,
    )
```

time: 776 us -> 467 us (0.60)
  local copies, waits for them, and re-layouts: 169 us -> 7.21 us
  matrix products: 127 us -> 0 us
  waiting for transfers between devices: 387 us -> 282 us
  Pallas kernels: 0 us -> 98.4 us
  blocking collectives: 0 us -> 36.2 us
  other arithmetic: 32.3 us -> 6.48 us
  starting transfers between devices: 37.2 us -> 14.7 us
    dot_general x22 -> x0, matrix products: 117 us -> none  [the longest x2 16.1 us: attend_back(): jnp.einsum('bhqk,bqhd->bkhd', dscore, queries, preferred_element_type=jnp...]
    pallas_call x0 -> x9, Pallas kernels: none -> 98.4 us  [call(): pl.pallas_call(kernel, out_shape=outs, in_specs=[pl.BlockSpec(memory_spac...]
    all_gather x2, waiting for transfers between devices: 90.9 us -> 0.02 us  [the longest x1 0.02 us: body(): all_down = lax.all_gather(down_weight, 'narrow', axis=0, tiled=True)]
    reduce_scatter x2, waiting for transfers between devices: 84.6 us -> 4.92 us  [the longest x1 4.9 us: body(): lax.psum_scatter(grad_down, 'narrow', scatter_dimension=0, tiled=True)]
    psum x2, waiting for transfers between devices: 187 us -> 252 us  [the longest x1 157 us: body(): lax.psum((qkv_local, proj_share, qkv_moved), ('wide', 'narrow'))]
    reshape x29 -> x0, local copies, waits for them, and re-layouts: 48.7 us -> none  [the longest x16 31.4 us: split_heads(): block.reshape(row_count // BALL, BALL, columns // head_size, head_size)]
    gather x4 -> x0, local copies, waits for them, and re-layouts: 41.2 us -> none  [the longest x1 19.6 us: body(): grad_moved = grad_returned[target, slot_index]]
    all_to_all x0 -> x2, blocking collectives: none -> 36.2 us  [exchange(): got = lax.all_to_all(sent, 'wide', split_axis=0, concat_axis=0, tiled=True)]
  transfers between devices with their start and end apart: 11 -> 9, of which waited for: 8 -> 5; matrix products, arithmetic and copies ran while one was open for 21% -> 1% of each run, Pallas kernels for 0% -> 14%
where the time goes in v1:
time: 467 us; the launch traced here: 459 us
  waiting for transfers between devices  282 us (60%)
  Pallas kernels  98.4 us (21%)
  blocking collectives  36.2 us (8%)
  starting transfers between devices  14.7 us (3%)
  between operations  14.6 us (3%)
  local copies, waits for them, and re-layouts  7.21 us (2%)
  other arithmetic  6.48 us (1%)
    psum x1, waiting for transfers between devices, body(): lax.psum((qkv_local, proj_share, qkv_moved), ('wide', 'narrow'))  157 us
    pallas_call x9, Pallas kernels, call(): pl.pallas_call(kernel, out_shape=outs, in_specs=[pl.BlockSpec(memory_spac...  98.4 us
    psum x1, waiting for transfers between devices, body(): up_sum, down_sum = lax.psum((up_part, down_part), 'wide')  95.2 us
    all_to_all x2, blocking collectives, exchange(): got = lax.all_to_all(sent, 'wide', split_axis=0, concat_axis=0, tiled=True)  36.2 us
    all_to_all x3, waiting for transfers between devices, exchange(): got = lax.all_to_all(sent, 'wide', split_axis=0, concat_axis=0, tiled=True)  23.3 us
    all_to_all x3, starting transfers between devices, exchange(): got = lax.all_to_all(sent, 'wide', split_axis=0, concat_axis=0, tiled=True)  13.7 us
  transfers between devices with their start and end apart: 9, of which 5 were waited for; matrix products, arithmetic and copies ran while one was open for 1% of the time, Pallas kernels for 14%

profile of v1, /device:TPU:1, one launch (start us, length us, event | category | flops | bytes accessed | tf_op | source)
XLA Modules:
  0.0 459.4 jit_solution(7450305734723197843)
XLA Ops:
  7.2 0.0 all-gather.3.cloned.1.call-start
  7.2 0.7 all-gather.3.cloned.1.call-update
  7.9 0.0 all-gather.5.cloned.1.call-start
  7.9 0.7 all-gather.5.cloned.1.call-update
  8.6 4.8 %route.1 = (bf16[1536,512]{1,0:T(8,128)(2,1)}, s32[32,128]{1,0:T(8,128)}, s32[1,1024]{1,0:T(1,128)}) custom-call(s32[1,1024]{1,0:T(1,128)} %bitcast.25, bf16[1024,512]{1,0:T(8,128)(2,1)} %tok_ref.3), custom_call_target="tpu_custom_call" | custom-call | flops 1610612736 | bytes 2646016 | tf_op jit(solution)/shard_map/route/pallas_call | solution.py:110
  13.5 0.0 copy-start.1
  13.5 16.6 %all_to_all.25 = s32[32,1,128]{2,1,0:T(1,128)} all-to-all(s32[32,1,128]{2,1,0:T(1,128)} %bitcast.24), channel_id=1, replica_groups=mesh['wide'=32,'narrow'=4] {'wide'}, dimensions={0} | all-to-all | bytes 32768 | tf_op jit(solution)/shard_map/all_to_all | solution.py:324
  30.1 4.1 all-to-all-start
  34.2 0.0 copy-done.1
  34.2 1.3 fusion
  35.5 21.0 %all-to-all-done = bf16[32,48,512]{2,1,0:T(8,128)(2,1)S(1)} async-done(((bf16[32,48,512]{2,1,0:T(8,128)(2,1)}), bf16[32,48,512]{2,1,0:T(8,128)(2,1)S(1)}, u32[]{:S(2)}, u32[]{:S(2)}) %all-to-all-start) | async-done | bytes 1572896 | tf_op jit(solution)/shard_map/all_to_all | solution.py:324
  56.4 0.0 copy-start.2
  56.4 1.1 copy-done.2
  57.6 10.6 %moved.1 = (bf16[1024,512]{1,0:T(8,128)(2,1)}, bf16[1024,768]{1,0:T(8,128)(2,1)}, s32[1,1536]{1,0:T(1,128)}, bf16[1536,256]{1,0:T(8,128)(2,1)}) custom-call(bf16[1536,512]{1,0:T(8,128)(2,1)} %bitcast.16, s32[32,128]{1,0:T(8,128)} %bitcast.23, bf16[512,768]{1,0:T(8,128)(2,1)} %get-tuple-element.77.refs_2_.refs_3_), custom_call_target="tpu_custom_call" | custom-call | flops 4294967296 | bytes 5789696 | tf_op jit(solution)/shard_map/moved/pallas_call | solution.py:110
  68.2 5.6 %all-to-all-start.2 = ((bf16[32,48,256]{2,1,0:T(8,128)(2,1)}), bf16[32,48,256]{2,1,0:T(8,128)(2,1)S(1)}, u32[]{:S(2)}, u32[]{:S(2)}) async-start(bf16[32,48,256]{2,1,0:T(8,128)(2,1)} %bitcast.20), calls=%async_computation.2 | async-start | bytes 1572864 | tf_op jit(solution)/shard_map/all_to_all | solution.py:324
  73.8 0.5 reduce-scatter.3.cloned.1.call-start
  74.3 0.0 all-gather.3.cloned.1.call-done.refs_3_.down_ref
  74.3 11.5 %first_local.1 = (bf16[1024,512]{1,0:T(8,128)(2,1)}, bf16[1024,768]{1,0:T(8,128)(2,1)}, bf16[1024,256]{1,0:T(8,128)(2,1)}, bf16[1024,2048]{1,0:T(8,128)(2,1)}) custom-call(bf16[1024,512]{1,0:T(8,128)(2,1)} %tok_ref.3, bf16[512,768]{1,0:T(8,128)(2,1)} %get-tuple-element.78.refs_1_.refs_3_, bf16[1024,512]{1,0:T(8,128)(2,1)} %cot_ref.3, ...), custom_call_target="tpu_custom_call" | custom-call | flops 4294967296 | bytes 12320768 | tf_op jit(solution)/shard_map/first_local/pallas_call | solution.py:110
  85.8 2.3 all-to-all-done.2
  88.1 0.9 copy-done.6
  89.0 21.4 %middle.1 = (bf16[1024,512]{1,0:T(8,128)(2,1)}, bf16[1024,512]{1,0:T(8,128)(2,1)}, bf16[1024,512]{1,0:T(8,128)(2,1)}, bf16[1024,2048]{1,0:T(8,128)(2,1)}, bf16[1...) custom-call(bf16[1024,512]{1,0:T(8,128)(2,1)} %tok_ref.3, ...), custom_call_target="tpu_custom_call" | custom-call | flops 8589934592 | bytes 24121344 | tf_op jit(solution)/shard_map/middle/pallas_call | solution.py:110
  110.4 13.2 %mlp_weights.1 = (bf16[1024,512]{1,0:T(8,128)(2,1)}, bf16[2048,512]{1,0:T(8,128)(2,1)}, bf16[2048,512]{1,0:T(8,128)(2,1)}) custom-call(bf16[1024,512]{1,0:T(8,128)(2,1)} %get-tuple-element.39.mid_ref, bf16[1024,2048]{1,0:T(8,128)(2,1)} %get-tuple-element.40.gated_ref, bf16[2048,512]{1,0:T(8,128)(2,1)} %all-gather.3.cloned.1.call-done.refs_3_.down_ref, ...), custom_call_target="tpu_custom_call" | custom-call | flops 6442450944 | bytes 18874368 | tf_op jit(solution)/shard_map/mlp_weights/pallas_call | solution.py:110
  123.6 0.0 reduce-scatter.3.cloned.1.call-update
  123.6 0.0 reduce-scatter.5.cloned.1.call-start
  123.7 0.5 reduce-scatter.5.cloned.1.call-update
  124.2 0.5 copy-done.5
  124.7 19.7 %all_to_all.26 = bf16[32,48,256]{2,1,0:T(8,128)(2,1)} all-to-all(bf16[32,48,256]{2,1,0:T(8,128)(2,1)S(1)} %bitcast.18), channel_id=1, replica_groups=mesh['wide'=32,'narrow'=4] {'wide'}, dimensions={0} | all-to-all | bytes 1572864 | tf_op jit(solution)/shard_map/all_to_all | solution.py:324
  144.4 14.5 %moved_back.1 = (bf16[1024,768]{1,0:T(8,128)(2,1)}, bf16[1536,512]{1,0:T(8,128)(2,1)}) custom-call(bf16[1536,256]{1,0:T(8,128)(2,1)} %bitcast.21, s32[1,1536]{1,0:T(1,128)} %get-tuple-element.51.refs_1_, bf16[1024,768]{1,0:T(8,128)(2,1)} %get-tuple-element.52.refs_2_, bf16[512,768]{1,0:T(8,128)(2,1)} %get-tuple-element.77.refs_2_.refs_3_), custom_call_target="tpu_custom_call" | custom-call | flops 6442450944 | bytes 6297600 | tf_op jit(solution)/shard_map/moved_back/pallas_call | solution.py:110
  158.9 4.0 all-to-all-start.4
  162.9 0.3 all-reduce.5.cloned.1.call-start
  163.2 12.4 %local_back.1 = (f32[1024,512]{1,0:T(8,128)}, bf16[512,768]{1,0:T(8,128)(2,1)}, bf16[512,512]{1,0:T(8,128)(2,1)}) custom-call(bf16[1024,768]{1,0:T(8,128)(2,1)} %get-tuple-element.45.refs_0_, bf16[1024,256]{1,0:T(8,128)(2,1)} %get-tuple-element.46.refs_1_, bf16[1024,512]{1,0:T(8,128)(2,1)} %get-tuple-element.47.refs_2_, ...), custom_call_target="tpu_custom_call" | custom-call | flops 6442450944 | bytes 9437184 | tf_op jit(solution)/shard_map/local_back/pallas_call | solution.py:110
  175.7 3.7 moved_weights.1
  179.3 0.0 all-reduce.5.cloned.1.call-update
  179.4 0.0 all-reduce.7.cloned.1.call-start
  179.4 0.0 reduce-scatter.3.cloned.1.call-done
  179.4 4.9 %reduce-scatter.5.cloned.1.call-done = bf16[512,512]{1,0:T(8,128)(2,1)} async-done(((bf16[2048,512]{1,0:T(8,128)(2,1)}), bf16[512,512]{1,0:T(8,128)(2,1)}) %reduce-scatter.5.cloned.1.call-update) | async-done | bytes 524304 | tf_op jit(solution)/shard_map/reduce_scatter | solution.py:409
  184.3 0.0 all-reduce.7.cloned.1.call-update
  184.4 156.5 %all-reduce.5.cloned.1.call-done = (bf16[512,768]{1,0:T(8,128)(2,1)}, bf16[512,768]{1,0:T(8,128)(2,1)}, bf16[512,512]{1,0:T(8,128)(2,1)}) async-done(((bf16[512,768]{1,0:T(8,128)(2,1)}, bf16[512,768]{1,0:T(8,128)(2,1)}, bf16[512,512]{1,0:T(8,128)(2,1)}), (bf16[512,768]{1,0:T(8,128)(2,1)}, bf16[512,768]{1,0:T(8,128)(2,1)}, bf16[512,512]{1,0:T(8,128)(2,1)})) %all-reduce.5.cloned.1.call-update) | async-done | bytes 2097168 | tf_op jit(solution)/shard_map/psum | solution.py:411
  340.9 2.3 convert_element_type.11
  343.1 0.0 copy-done.3
  343.1 0.0 copy-done.4
  343.1 2.1 maximum_convert_fusion
  345.2 0.0 all-to-all-done.4
  345.2 1.1 copy-done
  346.4 6.2 %last.1 = bf16[1024,512]{1,0:T(8,128)(2,1)} custom-call(bf16[1024,512]{1,0:T(8,128)(2,1)} %tok_ref.3, bf16[1024,512]{1,0:T(8,128)(2,1)} %get-tuple-element.44.refs_5_.gm_ref, f32[1024,512]{1,0:T(8,128)} %get-tuple-element.49.first_ref, bf16[1536,512]{1,0:T(8,128)(2,1)} %bitcast.14, s32[1,1024]{1,0:T(1,128)} %get-tuple-element.37.slot_ref), custom_call_target="tpu_custom_call" | custom-call | flops 1610612736 | bytes 6819840 | tf_op jit(solution)/shard_map/last/pallas_call | solution.py:110
  352.6 95.2 %all-reduce.7.cloned.1.call-done = (bf16[512,512]{0,1:T(8,128)(2,1)}, bf16[512,512]{1,0:T(8,128)(2,1)}) async-done(((bf16[512,512]{0,1:T(8,128)(2,1)}, bf16[512,512]{1,0:T(8,128)(2,1)}), (bf16[512,512]{0,1:T(8,128)(2,1)}, bf16[512,512]{1,0:T(8,128)(2,1)})) %all-reduce.7.cloned.1.call-update) | async-done | bytes 1048592 | tf_op jit(solution)/shard_map/psum | solution.py:410
  447.8 2.2 copy.15
  450.0 2.1 convert_element_type.12
  (6 shorter events, 0.0 us)
Async XLA Ops:
  7.2 67.1 %all-gather.3.cloned.1.call-start = ((), (), s32[]{:S(2)}) async-start(), calls=%async_computation.7 | async-start | bytes 2621440 | tf_op jit(solution)/shard_map/all_gather | solution.py:354
  7.9 80.2 %all-gather.5.cloned.1.call-start = ((), (), s32[]{:S(2)}) async-start(), calls=%async_computation.8 | async-start | bytes 2621440 | tf_op jit(solution)/shard_map/all_gather | solution.py:353
  13.5 20.7 %copy-start.1 = (bf16[512,1536]{1,0:T(8,128)(2,1)S(1)}, bf16[512,1536]{1,0:T(8,128)(2,1)}, u32[]{:S(2)}) copy-start(bf16[512,1536]{1,0:T(8,128)(2,1)} %param.9) | copy-start | bytes 4718596
  30.1 26.4 %all-to-all-start = ((bf16[32,48,512]{2,1,0:T(8,128)(2,1)}), bf16[32,48,512]{2,1,0:T(8,128)(2,1)S(1)}, u32[]{:S(2)}, u32[]{:S(2)}) async-start(bf16[32,48,512]{2,1,0:T(8,128)(2,1)} %bitcast.17), calls=%async_computation | async-start | bytes 3145728 | tf_op jit(solution)/shard_map/all_to_all | solution.py:324
  56.4 1.1 copy-start.2
  68.2 19.9 %all-to-all-start.2 = ((bf16[32,48,256]{2,1,0:T(8,128)(2,1)}), bf16[32,48,256]{2,1,0:T(8,128)(2,1)S(1)}, u32[]{:S(2)}, u32[]{:S(2)}) async-start(bf16[32,48,256]{2,1,0:T(8,128)(2,1)} %bitcast.20), calls=%async_computation.2 | async-start | bytes 1572864 | tf_op jit(solution)/shard_map/all_to_all | solution.py:324
  73.8 105.7 %reduce-scatter.3.cloned.1.call-start = ((), (), s32[]{:S(2)}) async-start(), calls=%async_computation.9 | async-start | bytes 2621440 | tf_op jit(solution)/shard_map/reduce_scatter | solution.py:408
  88.1 0.9 copy-start.6
  123.6 1.1 copy-start.5
  123.6 60.7 %reduce-scatter.5.cloned.1.call-start = ((), (), s32[]{:S(2)}) async-start(), calls=%async_computation.10 | async-start | bytes 2621440 | tf_op jit(solution)/shard_map/reduce_scatter | solution.py:409
  158.9 186.3 %all-to-all-start.4 = ((bf16[32,48,512]{2,1,0:T(8,128)(2,1)}), bf16[32,48,512]{2,1,0:T(8,128)(2,1)S(1)}, u32[]{:S(2)}, u32[]{:S(2)}) async-start(bf16[32,48,512]{2,1,0:T(8,128)(2,1)} %bitcast.15), calls=%async_computation.4 | async-start | bytes 3145728 | tf_op jit(solution)/shard_map/all_to_all | solution.py:324
  162.9 177.9 %all-reduce.5.cloned.1.call-start = ((), (), s32[]{:S(2)}) async-start(), calls=%async_computation.11 | async-start | bytes 4194304 | tf_op jit(solution)/shard_map/psum | solution.py:411
  179.4 268.4 %all-reduce.7.cloned.1.call-start = ((), (), s32[]{:S(2)}) async-start(), calls=%async_computation.12 | async-start | bytes 2097152 | tf_op jit(solution)/shard_map/psum | solution.py:410
  340.9 2.3 copy-start.3
  340.9 2.3 copy-start.4
  345.2 1.1 copy-start
Sparse Core Ops, SparseCore 0:
  9.7 34.1 all-gather.2
  45.5 30.8 all-gather.4
  123.7 28.7 reduce-scatter.2
  154.9 29.3 reduce-scatter.4
  190.1 150.7 all-reduce.4
  344.0 103.6 all-reduce.6

commit v2 on v1

v2 whole, which is shorter than its diff:
```python
import jax
import jax.numpy as jnp
from jax import lax
from jax.experimental import pallas as pl
from jax.experimental.pallas import tpu as pltpu
from jax.sharding import Mesh
from jax.sharding import PartitionSpec as P

HEADS = 8
BALL = 256
EPSILON = 1e-06
LANES = 128
VMEM_BYTES = 60 * 1024 * 1024
SMALL_BYTES = 16 * 1024 * 1024

LONG = 10**11

F32 = jnp.float32
BF16 = jnp.bfloat16


def mm(left, right):
    return lax.dot_general(left, right, (((1,), (0,)), ((), ())), preferred_element_type=F32)


def mm_nt(left, right):
    return lax.dot_general(left, right, (((1,), (1,)), ((), ())), preferred_element_type=F32)


def mm_tn(left, right):
    return lax.dot_general(left, right, (((0,), (0,)), ((), ())), preferred_element_type=F32)


def iota(shape, dimension):
    return lax.broadcasted_iota(jnp.int32, shape, dimension)


def row_scale(values):
    return lax.rsqrt(jnp.mean(values * values, axis=-1, keepdims=True) + EPSILON)


def norm_back(values, scaling, gradient):
    unit = values * scaling
    return scaling * (gradient - unit * jnp.mean(gradient * unit, axis=-1, keepdims=True))


def flip(block):
    return block.astype(F32).T.astype(BF16)


def as_column(row):
    return jnp.broadcast_to(row, (8, row.shape[1])).T[:, :1]


def onehot(condition):
    return jnp.where(condition, 1.0, 0.0).astype(BF16)


def head_mask(columns, head, head_size, value):
    lane = iota((1, columns), 1)
    inside = (lane >= head * head_size) & (lane < (head + 1) * head_size)
    return jnp.where(inside, value, 0.0).astype(BF16)


def ball_weights(queries, key_rows, head, head_size):
    columns = queries.shape[1]
    asked = queries * head_mask(columns, head, head_size, head_size ** (-0.5))
    scores = mm_nt(key_rows, asked)
    raised = jnp.exp(scores - jnp.max(scores, axis=0, keepdims=True))
    return raised * (1.0 / jnp.sum(raised, axis=0, keepdims=True)), asked


def ball_attend(packed, head_size):
    columns = packed.shape[1] // 3
    queries, key_rows = packed[:, :columns], packed[:, columns : 2 * columns]
    values_t = flip(packed[:, 2 * columns :])
    parts = []
    for head in range(columns // head_size):
        weights, _ = ball_weights(queries, key_rows, head, head_size)
        own = values_t[head * head_size : (head + 1) * head_size]
        parts.append(mm(own, weights.astype(BF16)))
    return jnp.concatenate(parts, axis=0).T.astype(BF16)


def ball_attend_back(packed, grad_out, head_size):
    columns = packed.shape[1] // 3
    queries, key_rows = packed[:, :columns], packed[:, columns : 2 * columns]
    values = packed[:, 2 * columns :]
    keys_t = flip(key_rows * jnp.asarray(head_size ** (-0.5), BF16))
    asked_all, upstream_all, rounded_all, dscore_all, grad_queries = [], [], [], [], []
    for head in range(columns // head_size):
        weights, asked = ball_weights(queries, key_rows, head, head_size)
        upstream = grad_out * head_mask(columns, head, head_size, 1.0)
        dprob = mm_nt(values, upstream)
        dscore = weights * (dprob - jnp.sum(dprob * weights, axis=0, keepdims=True))
        dscore = dscore.astype(BF16)
        own = keys_t[head * head_size : (head + 1) * head_size]
        grad_queries.append(mm(own, dscore))
        asked_all.append(asked)
        upstream_all.append(upstream)
        rounded_all.append(weights.astype(BF16))
        dscore_all.append(dscore)
    grad_values = mm(
        jnp.concatenate(rounded_all, axis=1), jnp.concatenate(upstream_all, axis=0)
    )
    grad_keys = mm(jnp.concatenate(dscore_all, axis=1), jnp.concatenate(asked_all, axis=0))
    grad_queries = jnp.concatenate(grad_queries, axis=0).T
    return jnp.concatenate([grad_queries, grad_keys, grad_values], axis=1).astype(BF16)


def shape(dims, dtype=BF16):
    return jax.ShapeDtypeStruct(dims, dtype)


def by_row(columns, rows=BALL):
    return pl.BlockSpec((rows, columns), lambda step: (step, 0))


def by_column(rows, columns):
    return pl.BlockSpec((rows, columns), lambda step: (0, step))


def whole(rows, columns, row=0, column=0):
    return pl.BlockSpec((rows, columns), lambda step: (row, column))


FLAG = pl.BlockSpec(memory_space=pltpu.SMEM)
ANY = pl.BlockSpec(memory_space=pl.ANY)


def call(kernel, steps, ins, outs, scratch=(), flops=0, name=None, vmem=SMALL_BYTES):
    return pl.pallas_call(
        kernel,
        grid=(steps,),
        out_shape=[out for out, _ in outs],
        in_specs=[spec for _, spec in ins],
        out_specs=[spec for _, spec in outs],
        scratch_shapes=list(scratch),
        compiler_params=pltpu.CompilerParams(vmem_limit_bytes=vmem),
        cost_estimate=pl.CostEstimate(flops=flops, bytes_accessed=0, transcendentals=0),
        name=name,
    )(*[array for array, _ in ins])


def is_first():
    return pl.program_id(0) == 0


def is_last():
    return pl.program_id(0) == pl.num_programs(0) - 1


def route_kernel(peers, group_size, capacity, stride, rot_ref, tok_ref, send_ref, slot_ref, wide_ref, place_ref):
    row_count = tok_ref.shape[0]
    step = BALL

    @pl.when(is_first())
    def _():
        rotation = rot_ref[...]
        target = rotation // (row_count * group_size)
        position = rotation % row_count + 1
        high = (position // 256).astype(F32)
        low = (position % 256).astype(F32)
        earlier = onehot(iota((step, step), 0) < iota((step, step), 1))
        carry = jnp.zeros((peers, 1), F32)
        sums_high = jnp.zeros((peers, LANES), F32)
        sums_low = jnp.zeros((peers, LANES), F32)
        for start in range(0, row_count, step):
            part = slice(start, start + step)
            chosen = jnp.where(iota((peers, step), 0) == target[:, part], 1.0, 0.0)
            before = mm(chosen.astype(BF16), earlier) + carry
            carry = carry + jnp.sum(chosen, axis=1, keepdims=True)
            rank = jnp.sum(chosen * before, axis=0, keepdims=True).astype(jnp.int32)
            slot_ref[:, part] = target[:, part] * capacity + rank
            wide_ref[:, part] = target[:, part] * stride + rank
            place = onehot(iota((LANES, step), 0) == rank)
            sums_high = sums_high + mm_nt((chosen * high[:, part]).astype(BF16), place)
            sums_low = sums_low + mm_nt((chosen * low[:, part]).astype(BF16), place)
        place_ref[:, :LANES] = sums_high.astype(BF16)
        place_ref[:, LANES:] = sums_low.astype(BF16)

    base = pl.program_id(0) * step
    pick = onehot(iota((step, row_count), 0) + base == wide_ref[...])
    rows = mm(pick, tok_ref[...])
    told = onehot(iota((step, peers), 0) + base == iota((step, peers), 1) * stride + capacity)
    extra = mm(told, place_ref[...])
    send_ref[:, : 2 * LANES] = (rows[:, : 2 * LANES] + extra).astype(BF16)
    send_ref[:, 2 * LANES :] = rows[:, 2 * LANES :].astype(BF16)


def arrived_row(place, stride):
    peers = place.shape[0]
    slots = peers * stride
    column = iota((1, slots), 1)
    source = column // stride
    spot = onehot(iota((LANES, slots), 0) == column - source * stride)
    spread = mm(place[:, :LANES], spot) * 256.0 + mm(place[:, LANES:], spot)
    own = iota((peers, slots), 0) == source
    return jnp.sum(jnp.where(own, spread, 0.0), axis=0, keepdims=True).astype(jnp.int32) - 1


def back_rows(arrived, rows_ref, out_ref):
    slots, step = out_ref.shape[0], 256
    row_count = rows_ref.shape[0]
    arrived_col = as_column(arrived.astype(F32)).astype(jnp.int32)
    moved = rows_ref[...]
    for start in range(0, slots, step):
        pick = onehot(iota((step, row_count), 1) == arrived_col[start : start + step])
        out_ref[start : start + step, :] = mm(pick, moved).astype(BF16)


def first_local_kernel(head_size, tok_ref, wq_ref, nrm_ref, pk_ref, heads_ref):
    residual = tok_ref[...].astype(F32)
    normed = (residual * row_scale(residual)).astype(BF16)
    nrm_ref[...] = normed
    packed = mm(normed, wq_ref[...]).astype(BF16)
    pk_ref[...] = packed
    heads_ref[...] = ball_attend(packed, head_size)


def grad_act_kernel(cot_ref, down_ref, act_ref):
    act_ref[...] = mm_nt(cot_ref[...], down_ref[...]).astype(BF16)


def moved_kernel(
    head_size, peers, capacity, _, got_ref, wq_ref, nrm_ref, pk_ref, row_ref, out_ref, wide_ref, heads_ref
):
    slots = got_ref.shape[0]
    stride = slots // peers

    @pl.when(is_first())
    def _():
        told = onehot(iota((peers, slots), 1) == iota((peers, slots), 0) * stride + capacity)
        place = mm(told, got_ref[:, : 2 * LANES]).astype(BF16)
        wide_ref[...] = arrived_row(place, stride)
        row_ref[...] = arrived_row(place, capacity)

    base = pl.multiple_of(pl.program_id(0) * BALL, BALL)
    pick = onehot(iota((BALL, slots), 0) + base == wide_ref[...])
    residual = mm(pick, got_ref[...])
    normed = (residual * row_scale(residual)).astype(BF16)
    nrm_ref[...] = normed
    packed = mm(normed, wq_ref[...]).astype(BF16)
    pk_ref[...] = packed
    heads_ref[pl.ds(base, BALL), :] = ball_attend(packed, head_size)

    @pl.when(is_last())
    def _():
        back_rows(row_ref[...], heads_ref, out_ref)


def middle_kernel(
    tok_ref, local_ref, ret_ref, part_ref, slot_ref, proj_ref, up_ref, cot_ref, act_ref,
    mix_ref, mid_ref, sn_ref, gated_ref, pre_ref, gm_ref, gl_ref, send_ref, gh_ref,
):
    width = tok_ref.shape[1]
    half = width // 2
    slots = ret_ref.shape[0]
    chunks = up_ref.shape[0] // width
    rate = 0.7978845608028654
    cubic = 0.044715 * rate
    slot_col = as_column(part_ref[...].astype(F32)).astype(jnp.int32)
    pick = onehot(iota((BALL, slots), 1) == slot_col)
    moved = mm(pick, ret_ref[...]).astype(BF16)
    mixed = jnp.concatenate([local_ref[...], moved], axis=1)
    mix_ref[...] = mixed
    middle = (tok_ref[...].astype(F32) + mm(mixed, proj_ref[...])).astype(BF16)
    mid_ref[...] = middle
    middle_f = middle.astype(F32)
    second_scale = row_scale(middle_f)
    normed = (middle_f * second_scale).astype(BF16)
    sn_ref[...] = normed
    grad_second = jnp.zeros((BALL, width), F32)
    for chunk in range(chunks):
        columns = slice(chunk * width, (chunk + 1) * width)
        up = up_ref[columns, :]
        pre = mm(normed, up)
        square = pre * pre
        upper = 0.5 + 0.5 * jnp.tanh(pre * (rate + cubic * square))
        gated_ref[:, columns] = (pre * upper).astype(BF16)
        slope = upper * (1.0 + (1.0 - upper) * (pre * (2.0 * rate + 6.0 * cubic * square)))
        grad_pre = (act_ref[:, columns].astype(F32) * slope).astype(BF16)
        pre_ref[:, columns] = grad_pre
        grad_second = grad_second + mm_nt(grad_pre, up)
    grad_middle = (
        cot_ref[...].astype(F32) + norm_back(middle_f, second_scale, grad_second)
    ).astype(BF16)
    gm_ref[...] = grad_middle
    grad_heads = mm_nt(grad_middle, proj_ref[...]).astype(BF16)
    gl_ref[...] = grad_heads[:, :half]
    base = pl.multiple_of(pl.program_id(0) * BALL, BALL)
    gh_ref[pl.ds(base, BALL), :] = grad_heads[:, half:]

    @pl.when(is_last())
    def _():
        moved_grad = gh_ref[...]
        slot = slot_ref[...]
        for start in range(0, slots, BALL):
            pick = onehot(iota((BALL, slot.shape[1]), 0) + start == slot)
            send_ref[start : start + BALL, :] = mm(pick, moved_grad).astype(BF16)


def weights_kernel(
    mid_ref, gated_ref, down_ref, cot_ref, sn_ref, pre_ref,
    out_ref, both_ref, sn_t_ref, cot_t_ref, sum_ref,
):
    @pl.when(is_first())
    def _():
        sn_t_ref[...] = flip(sn_ref[...])
        cot_t_ref[...] = flip(cot_ref[...])
        sum_ref[...] = mid_ref[...].astype(F32)

    gated = gated_ref[...]
    both_ref[0] = mm(sn_t_ref[...], pre_ref[...]).astype(BF16)
    both_ref[1] = mm(cot_t_ref[...], gated).astype(BF16)
    sum_ref[...] += mm(gated, down_ref[...])

    @pl.when(is_last())
    def _():
        out_ref[...] = sum_ref[...].astype(BF16)


def local_back_kernel(
    head_size, pk_ref, gl_ref, nrm_ref, wq_ref, mix_ref, gm_ref,
    first_ref, gq_ref, gp_ref, gpk_ref,
):
    grad_packed = ball_attend_back(pk_ref[...], gl_ref[...], head_size)
    base = pl.multiple_of(pl.program_id(0) * BALL, BALL)
    gpk_ref[pl.ds(base, BALL), :] = grad_packed
    first_ref[...] = mm_nt(grad_packed, wq_ref[...])

    @pl.when(is_last())
    def _():
        gq_ref[...] = mm(flip(nrm_ref[...]), gpk_ref[...]).astype(BF16)
        gp_ref[...] = mm(flip(mix_ref[...]), gm_ref[...]).astype(BF16)


def moved_back_kernel(head_size, _, got_ref, row_ref, pk_ref, wq_ref, gpk_ref, out_ref, first_ref):
    slots = got_ref.shape[0]
    base = pl.multiple_of(pl.program_id(0) * BALL, BALL)
    pick = onehot(iota((BALL, slots), 0) + base == row_ref[...])
    grad_out = mm(pick, got_ref[...]).astype(BF16)
    grad_packed = ball_attend_back(pk_ref[...], grad_out, head_size)
    gpk_ref[...] = grad_packed
    first_ref[pl.ds(base, BALL), :] = mm_nt(grad_packed, wq_ref[...]).astype(BF16)

    @pl.when(is_last())
    def _():
        back_rows(row_ref[...], first_ref, out_ref)


def moved_weights_kernel(core_ref, nrm_ref, gpk_ref, gq_ref, gp_ref, keep_ref, send_ref, all_ref):
    width, third = gq_ref.shape
    all_ref[:, :third] = gq_ref[...]
    all_ref[:, third : 2 * third] = mm(flip(nrm_ref[...]), gpk_ref[...]).astype(BF16)
    all_ref[:, 2 * third :] = gp_ref[...]
    half = width // 2
    core = core_ref[0]
    for side, out_ref in ((core, keep_ref), (1 - core, send_ref)):
        rows = pl.ds(pl.multiple_of(side * half, half), half)
        for block in range(all_ref.shape[1] // width):
            out_ref[block * half : (block + 1) * half, :] = all_ref[rows, block * width : (block + 1) * width]


def add_split_kernel(count, after, spot_ref, *refs):
    ins, outs, sum_ref = refs[: -count - 1], refs[-count - 1 : -1], refs[-1]
    total = ins[0][...].astype(F32)
    for in_ref in ins[1:]:
        total = total + in_ref[...].astype(F32)
    sum_ref[...] = total.astype(BF16)
    size = sum_ref.shape[0] // count
    for shift, out_ref in enumerate(outs):
        start = lax.rem(spot_ref[0] + shift, count) * size
        out_ref[...] = sum_ref[pl.ds(pl.multiple_of(start, size), size), :]


def add_kernel(after, *refs):
    total = refs[0][...].astype(F32)
    for in_ref in refs[1:-1]:
        total = total + in_ref[...].astype(F32)
    refs[-1][...] = total.astype(BF16)


def spread_kernel(after, in_ref, out_ref):
    total = in_ref[0].astype(F32)
    for part in range(1, in_ref.shape[0]):
        total = total + in_ref[part].astype(F32)
    total = total.astype(BF16)
    for part in range(out_ref.shape[0]):
        out_ref[part] = total


def place_kernel(spot_ref, *refs):
    ins, out_ref = refs[:-1], refs[-1]
    count, size = len(ins), ins[0].shape[0]
    for shift, in_ref in enumerate(ins):
        start = lax.rem(spot_ref[0] + (count - shift), count) * size
        out_ref[pl.ds(pl.multiple_of(start, size), size), :] = in_ref[...]


def last_kernel(tok_ref, gm_ref, first_ref, ret_ref, part_ref, out_ref):
    slots = ret_ref.shape[0]
    slot_col = as_column(part_ref[...].astype(F32)).astype(jnp.int32)
    pick = onehot(iota((BALL, slots), 1) == slot_col)
    grad_first = first_ref[...] + mm(pick, ret_ref[...])
    residual = tok_ref[...].astype(F32)
    out_ref[...] = (
        gm_ref[...].astype(F32) + norm_back(residual, row_scale(residual), grad_first)
    ).astype(BF16)


def finish_mlp_kernel(core_ref, mine_ref, other_ref, up_ref, down_ref):
    core = core_ref[0]

    @pl.when(core == 0)
    def _():
        up_ref[...] = mine_ref[...].astype(F32)
        down_ref[...] = other_ref[...].astype(F32).T

    @pl.when(core != 0)
    def _():
        up_ref[...] = other_ref[...].astype(F32)
        down_ref[...] = mine_ref[...].astype(F32).T


def finish_attention_kernel(_, also, core_ref, mine_ref, other_ref, qkv_ref, proj_ref):
    core = core_ref[0]
    width = mine_ref.shape[1]
    half = mine_ref.shape[0] // 4
    for side, part_ref in ((core, mine_ref), (1 - core, other_ref)):
        rows = pl.ds(pl.multiple_of(side * half, half), half)
        for block in range(3):
            qkv_ref[rows, block * width : (block + 1) * width] = part_ref[block * half : (block + 1) * half, :].astype(F32)
        proj_ref[rows, :] = part_ref[3 * half :, :].astype(F32)


def exchange(rows, peers):
    slots, columns = rows.shape
    sent = rows.reshape(peers, slots // peers, columns)
    got = lax.all_to_all(sent, ("z", "x", "core"), split_axis=0, concat_axis=0, tiled=True)
    return got.reshape(slots, columns)


def swap_core(block):
    return lax.ppermute(block, "core", [(0, 1), (1, 0)])


def whole_array(array):
    return array, whole(*array.shape)


def spot_on(axis):
    return lax.axis_index(axis).astype(jnp.int32).reshape(1), FLAG


def shift_by(block, axis, shift):
    count = lax.axis_size(axis)
    return lax.ppermute(block, axis, [(place, (place + shift) % count) for place in range(count)])


def add_split(parts, axis, after):
    count = lax.axis_size(axis)
    rows, columns = parts[0].shape
    out = (shape((rows // count, columns)), whole(rows // count, columns))
    shares = call(
        bind(add_split_kernel, count), 1,
        [(after, ANY), spot_on(axis)] + [whole_array(part) for part in parts], [out] * count,
        scratch=[pltpu.VMEM((rows, columns), BF16)], name="add_split",
    )
    return [shares[0]] + [shift_by(shares[shift], axis, shift) for shift in range(1, count)]


def gather(block, axis):
    count = lax.axis_size(axis)
    rows, columns = block.shape
    parts = [block] + [shift_by(block, axis, shift) for shift in range(1, count)]
    (joined,) = call(
        place_kernel, 1, [spot_on(axis)] + [whole_array(part) for part in parts],
        [(shape((count * rows, columns)), whole(count * rows, columns))], name="gather",
    )
    return joined


def add(parts, after):
    (block,) = call(
        add_kernel, 1, [(after, ANY)] + [whole_array(part) for part in parts],
        [(shape(parts[0].shape), whole(*parts[0].shape))], name="add",
    )
    return block


def sum_by_steps(block, axes, after):
    parts = [block]
    for axis in axes:
        parts = add_split(parts, axis, after)
    share = block = add(parts, after)
    for axis in reversed(axes):
        block = gather(block, axis)
    return block, share


def sum_at_once(block, axes, after):
    count = lax.axis_size(axes)
    rows, columns = block.shape
    parts = block.reshape(count, rows // count, columns)
    parts = lax.all_to_all(parts, axes, split_axis=0, concat_axis=0, tiled=True)
    spread = (shape(parts.shape), pl.BlockSpec(parts.shape, lambda step: (0, 0, 0)))
    (spread,) = call(
        spread_kernel, 1, [(after, ANY), (parts, spread[1])], [spread], name="add_spread",
    )
    told = lax.all_to_all(spread, axes, split_axis=0, concat_axis=0, tiled=True)
    return told.reshape(rows, columns)


def bind(kernel, *fixed):
    def bound(*refs):
        kernel(*fixed, *refs)

    return bound


def body(tokens, rotation, qkv_weight, proj_weight, up_weight, down_weight, cotangent):
    rows, width = tokens.shape
    half = width // 2
    third = 3 * half
    head_size = width // HEADS
    peers = lax.axis_size(("z", "x", "core"))
    group_size = lax.axis_size("narrow")
    capacity = rows // peers + rows // peers // 2
    stride = capacity + 8
    slots = peers * capacity
    wide_slots = peers * stride
    hidden = group_size * up_weight.shape[1]
    balls = rows // BALL
    core = lax.axis_index("core")
    flag = (core.astype(jnp.int32).reshape(1), FLAG)
    own_weight = jnp.where(core == 0, up_weight, down_weight)
    all_weights = lax.all_gather(own_weight, ("core", "narrow"), axis=0, tiled=True)
    all_up = (all_weights, whole(hidden, width))

    send, slot = call(
        bind(route_kernel, peers, group_size, capacity, stride), wide_slots // BALL,
        [(rotation.reshape(1, rows), whole(1, rows)), (tokens, whole(rows, width))],
        [(shape((wide_slots, width)), by_row(width)), (shape((1, rows), jnp.int32), whole(1, rows))],
        scratch=[pltpu.VMEM((1, rows), jnp.int32), pltpu.VMEM((peers, 2 * LANES), BF16)],
        flops=LONG, name="route",
    )
    got = exchange(send, peers)
    part = (slot, by_column(1, BALL))

    normed, packed, local_heads = call(
        bind(first_local_kernel, head_size), balls,
        [(tokens, by_row(width)), (qkv_weight, whole(width, third))],
        [(shape((rows, width)), by_row(width)), (shape((rows, third)), by_row(third)), (shape((rows, half)), by_row(half))],
        name="first_local",
    )
    moved_weight = (qkv_weight, whole(width, third, 0, 1))
    moved_normed, moved_packed, arrived, outgoing = call(
        bind(moved_kernel, head_size, peers, capacity), balls,
        [(local_heads, ANY), (got, whole(wide_slots, width)), moved_weight],
        [
            (shape((rows, width)), by_row(width)), (shape((rows, third)), by_row(third)),
            (shape((1, slots), jnp.int32), whole(1, slots)), (shape((slots, half)), whole(slots, half)),
        ],
        scratch=[pltpu.VMEM((1, wide_slots), jnp.int32), pltpu.VMEM((rows, half), BF16)],
        flops=LONG, name="moved", vmem=VMEM_BYTES,
    )
    returned = exchange(outgoing, peers)
    (grad_act,) = call(
        grad_act_kernel, balls,
        [(cotangent, by_row(width)), (all_weights, whole(hidden, width, 1))],
        [(shape((rows, hidden)), by_row(hidden))],
        name="grad_act",
    )
    mixed_heads, middle, second_normed, activated, grad_pre, grad_middle, grad_local, send_grad = call(
        middle_kernel, balls,
        [
            (tokens, by_row(width)), (local_heads, by_row(half)), (returned, whole(slots, half)),
            part, (slot, whole(1, rows)), (proj_weight, whole(width, width)), all_up,
            (cotangent, by_row(width)), (grad_act, by_row(hidden)),
        ],
        [
            (shape((rows, width)), by_row(width)), (shape((rows, width)), by_row(width)),
            (shape((rows, width)), by_row(width)), (shape((rows, hidden)), by_row(hidden)),
            (shape((rows, hidden)), by_row(hidden)), (shape((rows, width)), by_row(width)),
            (shape((rows, half)), by_row(half)), (shape((slots, half)), whole(slots, half)),
        ],
        scratch=[pltpu.VMEM((rows, half), BF16)], flops=LONG, name="middle", vmem=VMEM_BYTES,
    )
    got_grad = exchange(send_grad, peers)
    output, mlp_both = call(
        weights_kernel, group_size,
        [
            (middle, whole(rows, width)), (activated, by_column(rows, width)),
            (all_weights, pl.BlockSpec((width, width), lambda step: (group_size + step, 0))),
            (cotangent, whole(rows, width)), (second_normed, whole(rows, width)),
            (grad_pre, by_column(rows, width)),
        ],
        [
            (shape((rows, width)), whole(rows, width)),
            (shape((2, hidden, width)), pl.BlockSpec((2, width, width), lambda step: (0, step, 0))),
        ],
        scratch=[pltpu.VMEM((width, rows), BF16), pltpu.VMEM((width, rows), BF16), pltpu.VMEM((rows, width), F32)],
        name="mlp_weights", vmem=VMEM_BYTES,
    )
    first_local, qkv_local, proj_local = call(
        bind(local_back_kernel, head_size), balls,
        [
            (packed, by_row(third)), (grad_local, by_row(half)), (normed, whole(rows, width)),
            (qkv_weight, whole(width, third)), (mixed_heads, whole(rows, width)), (grad_middle, whole(rows, width)),
        ],
        [
            (shape((rows, width), F32), by_row(width)),
            (shape((width, third)), whole(width, third)), (shape((width, width)), whole(width, width)),
        ],
        scratch=[pltpu.VMEM((rows, third), BF16)],
        name="local_back", vmem=VMEM_BYTES,
    )
    moved_grad_packed, grad_outgoing = call(
        bind(moved_back_kernel, head_size), balls,
        [(output, ANY), (got_grad, whole(slots, half)), (arrived, whole(1, slots)), (moved_packed, by_row(third)), moved_weight],
        [(shape((rows, third)), by_row(third)), (shape((slots, width)), whole(slots, width))],
        scratch=[pltpu.VMEM((rows, width), BF16)], flops=LONG, name="moved_back", vmem=VMEM_BYTES,
    )
    grad_returned = exchange(grad_outgoing, peers)
    stacked = (shape((2 * width, width)), whole(2 * width, width))
    keep, send = call(
        moved_weights_kernel, 1,
        [flag, whole_array(moved_normed), whole_array(moved_grad_packed), whole_array(qkv_local), whole_array(proj_local)],
        [stacked, stacked],
        scratch=[pltpu.VMEM((width, 2 * third + width), BF16)], name="moved_weights",
    )
    (grad_tokens,) = call(
        last_kernel, balls,
        [(tokens, by_row(width)), (grad_middle, by_row(width)), (first_local, by_row(width)), (grad_returned, whole(slots, width)), part],
        [(shape((rows, width)), by_row(width))],
        flops=LONG, name="last",
    )

    mlp_part = lax.psum_scatter(
        mlp_both.reshape(2 * hidden, width), ("core", "narrow"), scatter_dimension=0, tiled=True
    )
    pair = add([keep, swap_core(send)], grad_returned)
    mlp_mine, mlp_share = sum_by_steps(mlp_part, ("x", "z"), pair)
    mlp_other = swap_core(mlp_mine)
    grad_up, grad_down = call(
        finish_mlp_kernel, 1, [flag, whole_array(mlp_mine), whole_array(mlp_other)],
        [(shape((width, width), F32), whole(width, width)), (shape((width, width), F32), whole(width, width))],
        name="finish_mlp",
    )
    mine = sum_at_once(pair, ("narrow", "x", "z"), mlp_share)
    grad_qkv, grad_proj = call(
        finish_attention_kernel, 1, [(grad_tokens, ANY), (grad_up, ANY), flag, whole_array(mine), whole_array(swap_core(mine))],
        [(shape((width, 2 * third), F32), whole(width, 2 * third)), (shape((width, width), F32), whole(width, width))],
        name="finish_attention",
    )
    return output, grad_tokens, grad_qkv, grad_proj, grad_up, grad_down


def solution(mesh):
    wide, narrow = mesh.devices.shape
    axes = ("z", "x", "core", "narrow")
    mesh = Mesh(mesh.devices.reshape(wide // 8, 4, 2, narrow), axes)
    rows = axes
    return jax.shard_map(
        body,
        mesh=mesh,
        in_specs=(
            P(rows, None),
            P(rows),
            P(),
            P(),
            P(None, "narrow"),
            P("narrow", None),
            P(rows, None),
        ),
        out_specs=(
            P(rows, None),
            P(rows, None),
            P(),
            P(),
            P(None, "narrow"),
            P("narrow", None),
        ),
        check_vma=False,
    )
```

time: 467 us -> 265 us (0.57); the launches traced: 459 us -> 264 us
  waiting for transfers between devices: 282 us -> 48.3 us
  starting transfers between devices: 14.7 us -> 72.8 us
  blocking collectives: 36.2 us -> 0 us
  local copies, waits for them, and re-layouts: 7.21 us -> 25.6 us
    psum x2 -> x0, waiting for transfers between devices: 252 us -> none  [the longest x1 157 us: body(): lax.psum((qkv_local, proj_share, qkv_moved), ('wide', 'narrow'))]
    all_to_all x2 -> x0, blocking collectives: 36.2 us -> none  [exchange(): got = lax.all_to_all(sent, 'wide', split_axis=0, concat_axis=0, tiled=True)]
    all_to_all x3 -> x6, starting transfers between devices: 13.7 us -> 43.6 us  [the longest x4 25.8 us: exchange(): lax.all_to_all(sent, ('z', 'x', 'core'), split_axis=0, concat_axis=0, til...]
    ppermute x0 -> x15, starting transfers between devices: none -> 29 us  [the longest x12 25.6 us: shift_by(): lax.ppermute(block, axis, [(place, (place + shift) % count) for place in...]
    ppermute x0 -> x15, waiting for transfers between devices: none -> 25.1 us  [the longest x12 22.6 us: shift_by(): lax.ppermute(block, axis, [(place, (place + shift) % count) for place in...]
    unnamed x15 -> x56, local copies, waits for them, and re-layouts: 5.92 us -> 25.6 us
    convert_element_type x3 -> x0, other arithmetic: 6.48 us -> none  [the longest x1 2.26 us: body(): proj_sum.astype(F32)]
    reduce_scatter x2 -> x1, waiting for transfers between devices: 4.92 us -> 0.02 us  [body(): lax.psum_scatter(mlp_both.reshape(2 * hidden, width), ('core', 'narrow'),...]
  transfers between devices with their start and end apart: 9 -> 23, of which waited for: 5 -> 14; matrix products, arithmetic and copies ran while one was open for 1% -> 1% of each run, Pallas kernels for 14% -> 28%
where the time goes in v2:
time: 265 us; the launch traced here: 264 us
  Pallas kernels  101 us (38%)
  starting transfers between devices  72.8 us (27%)
  waiting for transfers between devices  48.3 us (18%)
  local copies, waits for them, and re-layouts  25.6 us (10%)
  between operations  14.3 us (5%)
    pallas_call x19, Pallas kernels, call(): pl.pallas_call(kernel, grid=(steps,), out_shape=[out for out, _ in outs],...  101 us
    all_to_all x4, starting transfers between devices, exchange(): lax.all_to_all(sent, ('z', 'x', 'core'), split_axis=0, concat_axis=0, til...  25.8 us
    unnamed x56, local copies, waits for them, and re-layouts  25.6 us
    ppermute x12, starting transfers between devices, shift_by(): lax.ppermute(block, axis, [(place, (place + shift) % count) for place in...  25.6 us
    all_to_all x4, waiting for transfers between devices, exchange(): lax.all_to_all(sent, ('z', 'x', 'core'), split_axis=0, concat_axis=0, til...  23.2 us
    ppermute x12, waiting for transfers between devices, shift_by(): lax.ppermute(block, axis, [(place, (place + shift) % count) for place in...  22.6 us
    all_to_all x1, starting transfers between devices, sum_at_once(): parts = lax.all_to_all(parts, axes, split_axis=0, concat_axis=0, tiled=True)  9.81 us
    all_to_all x1, starting transfers between devices, sum_at_once(): told = lax.all_to_all(spread, axes, split_axis=0, concat_axis=0, tiled=True)  8 us
  transfers between devices with their start and end apart: 23, of which 14 were waited for; matrix products, arithmetic and copies ran while one was open for 1% of the time, Pallas kernels for 28%

profile of v2, /device:TPU:1, one launch (start us, length us, event | category | flops | bytes accessed | tf_op | source)
XLA Modules:
  0.0 263.6 jit_solution(1521613519691931401)
XLA Ops:
  7.2 1.2 copy-done.9
  9.1 5.5 %route.1 = (bf16[1792,512]{1,0:T(8,128)(2,1)}, s32[1,1024]{1,0:T(1,128)S(1)}) custom-call(s32[1,1024]{1,0:T(1,128)S(1)} %bitcast.19, bf16[1024,512]{1,0:T(8,128)(2,1)S(1)} %copy-done.9), custom_call_target="tpu_custom_call" | custom-call | flops 99999997952 | tf_op jit(solution)/shard_map/route/pallas_call | solution.py:132
  15.2 9.6 %all-to-all-start = ((bf16[32,56,512]{2,1,0:T(8,128)(2,1)}), bf16[32,56,512]{2,1,0:T(8,128)(2,1)}, u32[]{:S(2)}, u32[]{:S(2)}) async-start(bf16[32,56,512]{2,1,0:T(8,128)(2,1)} %bitcast.1), calls=%async_computation | async-start | bytes 3670016 | tf_op jit(solution)/shard_map/all_to_all | solution.py:440
  24.9 2.0 broadcast_select_fusion
  26.9 5.6 %first_local.1 = (bf16[1024,512]{1,0:T(8,128)(2,1)S(1)}, bf16[1024,768]{1,0:T(8,128)(2,1)S(1)}, bf16[1024,256]{1,0:T(8,128)(2,1)S(1)}) custom-call(bf16[1024,512]{1,0:T(8,128)(2,1)S(1)} %copy-done.10, bf16[512,1536]{1,0:T(8,128)(2,1)S(1)} %copy-done.1), custom_call_target="tpu_custom_call" | custom-call | tf_op jit(solution)/shard_map/first_local/pallas_call | solution.py:132
  32.5 1.2 copy-done.6
  35.5 14.3 %all-to-all-done = bf16[32,56,512]{2,1,0:T(8,128)(2,1)} async-done(((bf16[32,56,512]{2,1,0:T(8,128)(2,1)}), bf16[32,56,512]{2,1,0:T(8,128)(2,1)}, u32[]{:S(2)}, u32[]{:S(2)}) %all-to-all-start) | async-done | bytes 1835040 | tf_op jit(solution)/shard_map/all_to_all | solution.py:440
  49.8 13.2 %moved.1 = (bf16[1024,512]{1,0:T(8,128)(2,1)}, bf16[1024,768]{1,0:T(8,128)(2,1)}, s32[1,1536]{1,0:T(1,128)}, bf16[1536,256]{1,0:T(8,128)(2,1)}) custom-call(bf16[1024,256]{1,0:T(8,128)(2,1)} %copy-done.21, bf16[1792,512]{1,0:T(8,128)(2,1)} %bitcast.2.refs_1_, bf16[512,1536]{1,0:T(8,128)(2,1)} %refs_4_.1), custom_call_target="tpu_custom_call" | custom-call | flops 99999997952 | tf_op jit(solution)/shard_map/moved/pallas_call | solution.py:132
  63.0 6.0 %all-to-all-start.1 = ((bf16[32,48,256]{2,1,0:T(8,128)(2,1)}), bf16[32,48,256]{2,1,0:T(8,128)(2,1)S(1)}, u32[]{:S(2)}, u32[]{:S(2)}) async-start(bf16[32,48,256]{2,1,0:T(8,128)(2,1)} %bitcast.25), calls=%async_computation.1 | async-start | bytes 1572864 | tf_op jit(solution)/shard_map/all_to_all | solution.py:440
  69.0 2.2 copy-done
  71.2 3.0 %grad_act.1.act_ref = bf16[1024,2048]{1,0:T(8,128)(2,1)S(1)} custom-call(bf16[1024,512]{1,0:T(8,128)(2,1)S(1)} %copy-done.4, bf16[4096,512]{1,0:T(8,128)(2,1)S(1)} %copy-done), custom_call_target="tpu_custom_call" | custom-call | tf_op jit(solution)/shard_map/grad_act/pallas_call | solution.py:132
  74.2 2.0 copy-done.2
  76.2 7.1 %all-to-all-done.1 = bf16[32,48,256]{2,1,0:T(8,128)(2,1)S(1)} async-done(((bf16[32,48,256]{2,1,0:T(8,128)(2,1)}), bf16[32,48,256]{2,1,0:T(8,128)(2,1)S(1)}, u32[]{:S(2)}, u32[]{:S(2)}) %all-to-all-start.1) | async-done | bytes 786464 | tf_op jit(solution)/shard_map/all_to_all | solution.py:440
  84.2 19.9 %middle.1 = (bf16[1024,512]{1,0:T(8,128)(2,1)}, bf16[1024,512]{1,0:T(8,128)(2,1)}, bf16[1024,512]{1,0:T(8,128)(2,1)}, bf16[1024,2048]{1,0:T(8,128)(2,1)}, bf16[1...) custom-call(bf16[1024,512]{1,0:T(8,128)(2,1)} %tok_ref.3, ...), custom_call_target="tpu_custom_call" | custom-call | flops 99999997952 | tf_op jit(solution)/shard_map/middle/pallas_call | solution.py:132
  104.1 4.1 %all-to-all-start.2 = ((bf16[32,48,256]{2,1,0:T(8,128)(2,1)}), bf16[32,48,256]{2,1,0:T(8,128)(2,1)S(1)}, u32[]{:S(2)}, u32[]{:S(2)}) async-start(bf16[32,48,256]{2,1,0:T(8,128)(2,1)} %bitcast.23), calls=%async_computation.2 | async-start | bytes 1572864 | tf_op jit(solution)/shard_map/all_to_all | solution.py:440
  108.5 12.6 %mlp_weights.1 = (bf16[1024,512]{1,0:T(8,128)(2,1)}, bf16[2,2048,512]{2,1,0:T(8,128)(2,1)}) custom-call(bf16[1024,512]{1,0:T(8,128)(2,1)} %get-tuple-element.48.mid_ref, bf16[1024,2048]{1,0:T(8,128)(2,1)} %get-tuple-element.49.gated_ref, bf16[4096,512]{1,0:T(8,128)(2,1)} %all-gather.2.cloned.1.call-done.down_ref.up_ref, bf16[1024,512]{1,0:T(8,128)(2,1)} %cot_ref.5, ...), custom_call_target="tpu_custom_call" | custom-call | tf_op jit(solution)/shard_map/mlp_weights/pallas_call | solution.py:132
  121.1 1.4 all-to-all-done.2
  123.5 15.1 %moved_back.1 = (bf16[1024,768]{1,0:T(8,128)(2,1)}, bf16[1536,512]{1,0:T(8,128)(2,1)}) custom-call(bf16[1024,512]{1,0:T(8,128)(2,1)} %get-tuple-element.38.refs_0_, bf16[1536,256]{1,0:T(8,128)(2,1)} %bitcast.22, s32[1,1536]{1,0:T(1,128)} %get-tuple-element.60.refs_2_, bf16[1024,768]{1,0:T(8,128)(2,1)} %get-tuple-element.61.refs_3_, bf16[512,1536]{1,0:T(8,128)(2,1)} %refs_4_.1), custom_call_target="tpu_custom_call" | custom-call | flops 99999997952 | tf_op jit(solution)/shard_map/moved_back/pallas_call | solution.py:132
  138.5 6.1 %all-to-all-start.3 = ((bf16[32,48,512]{2,1,0:T(8,128)(2,1)}), bf16[32,48,512]{2,1,0:T(8,128)(2,1)S(1)}, u32[]{:S(2)}, u32[]{:S(2)}) async-start(bf16[32,48,512]{2,1,0:T(8,128)(2,1)} %bitcast.21), calls=%async_computation.3 | async-start | bytes 3145728 | tf_op jit(solution)/shard_map/all_to_all | solution.py:440
  144.6 13.5 %local_back.1 = (f32[1024,512]{1,0:T(8,128)}, bf16[512,768]{1,0:T(8,128)(2,1)}, bf16[512,512]{1,0:T(8,128)(2,1)}) custom-call(bf16[1024,768]{1,0:T(8,128)(2,1)} %copy-done.6, bf16[1024,256]{1,0:T(8,128)(2,1)} %get-tuple-element.55.refs_1_, bf16[1024,512]{1,0:T(8,128)(2,1)} %copy-done.13, bf16[512,1536]{1,0:T(8,128)(2,1)} %refs_4_.1, ...), custom_call_target="tpu_custom_call" | custom-call | tf_op jit(solution)/shard_map/local_back/pallas_call | solution.py:132
  158.2 1.2 copy-done.14
  161.6 1.2 moved_weights.1
  164.0 2.4 collective-permute-done.refs_1_
  166.8 1.2 copy-done.16
  168.0 1.2 add.5.refs_0_.after
  169.2 9.8 %all-to-all-start.4 = ((bf16[64,16,512]{2,1,0:T(8,128)(2,1)}), bf16[64,16,512]{2,1,0:T(8,128)(2,1)S(1)}, u32[]{:S(2)}, u32[]{:S(2)}) async-start(bf16[64,16,512]{2,1,0:T(8,128)(2,1)} %bitcast.13), calls=%async_computation.5 | async-start | bytes 2097152 | tf_op jit(solution)/shard_map/all_to_all | solution.py:506
  180.2 1.3 collective-permute-start.1
  181.5 2.4 collective-permute-start.2
  185.1 10.6 %collective-permute-done.1.refs_3_ = bf16[128,512]{1,0:T(8,128)(2,1)S(1)} collective-permute-done((bf16[128,512]{1,0:T(8,128)(2,1)S(1)}, bf16[128,512]{1,0:T(8,128)(2,1)S(1)}, u32[]{:S(2)}, u32[]{:S(2)}) %collective-permute-start.1) | collective-permute-done | bytes 131104 | tf_op jit(solution)/shard_map/ppermute | solution.py:458
  195.7 2.7 %collective-permute-done.2.refs_4_ = bf16[128,512]{1,0:T(8,128)(2,1)S(1)} collective-permute-done((bf16[128,512]{1,0:T(8,128)(2,1)S(1)}, bf16[128,512]{1,0:T(8,128)(2,1)S(1)}, u32[]{:S(2)}, u32[]{:S(2)}) %collective-permute-start.2) | collective-permute-done | bytes 131104 | tf_op jit(solution)/shard_map/ppermute | solution.py:458
  198.5 1.3 collective-permute-start.4
  199.8 2.4 collective-permute-start.5
  206.2 8.0 %all-to-all-start.5 = ((bf16[64,16,512]{2,1,0:T(8,128)(2,1)}), bf16[64,16,512]{2,1,0:T(8,128)(2,1)S(1)}, u32[]{:S(2)}, u32[]{:S(2)}) async-start(bf16[64,16,512]{2,1,0:T(8,128)(2,1)} %copy-done.3), calls=%async_computation.6 | async-start | bytes 2097152 | tf_op jit(solution)/shard_map/all_to_all | solution.py:511
  215.3 2.4 collective-permute-start.8
  218.9 1.7 collective-permute-done.8.refs_2_
  220.5 1.5 collective-permute-done.9.refs_3_
  222.1 1.3 collective-permute-start.10
  223.4 9.9 %collective-permute-start.11 = (bf16[128,512]{1,0:T(8,128)(2,1)S(1)}, bf16[128,512]{1,0:T(8,128)(2,1)S(1)}, u32[]{:S(2)}, u32[]{:S(2)}) collective-permute-start(bf16[128,512]{1,0:T(8,128)(2,1)S(1)} %gather.2.refs_0_), channel_id=1, source_target_pairs={{0,16},{8,24},{16,0},{24,8},{1,17},{9,25},{17,1},{25,9},{2,18},{10... | collective-permute-start | bytes 393224 | tf_op jit(solution)/shard_map/ppermute | solution.py:458
  234.5 2.8 %collective-permute-done.11.refs_2_ = bf16[128,512]{1,0:T(8,128)(2,1)S(1)} collective-permute-done((bf16[128,512]{1,0:T(8,128)(2,1)S(1)}, bf16[128,512]{1,0:T(8,128)(2,1)S(1)}, u32[]{:S(2)}, u32[]{:S(2)}) %collective-permute-start.11) | collective-permute-done | bytes 131104 | tf_op jit(solution)/shard_map/ppermute | solution.py:458
  237.9 3.1 %collective-permute-start.13 = (bf16[512,512]{1,0:T(8,128)(2,1)S(1)}, bf16[512,512]{1,0:T(8,128)(2,1)}, u32[]{:S(2)}, u32[]{:S(2)}) collective-permute-start(bf16[512,512]{1,0:T(8,128)(2,1)S(1)} %gather.3.mine_ref), channel_id=1, source_target_pairs={{0,4},{4,0},{1,5},{5,1},{2,6},{6,2},{3,7},{7,3},{8,12},{12,8},{9,1... | collective-permute-start | bytes 1572872 | tf_op jit(solution)/shard_map/ppermute | solution.py:445
  241.1 1.2 copy-done.11
  242.3 1.2 copy-done.12
  243.5 1.6 copy-done.20
  245.1 4.3 %last.1._ = bf16[1024,512]{1,0:T(8,128)(2,1)} custom-call(bf16[1024,512]{1,0:T(8,128)(2,1)S(1)} %copy-done.11, bf16[1024,512]{1,0:T(8,128)(2,1)S(1)} %copy-done.12, f32[1024,512]{1,0:T(8,128)S(1)} %copy-done.20, bf16[1536,512]{1,0:T(8,128)(2,1)S(1)} %bitcast.16, s32[1,1024]{1,0:T(1,128)S(1)} %copy-done.24), custom_call_target="tpu_custom_call" | custom-call | flops 99999997952 | tf_op jit(solution)/shard_map/last/pallas_call | solution.py:132
  249.4 2.6 finish_mlp.1
  252.1 1.2 copy-done.7
  253.3 1.2 copy-done.8
  254.5 2.2 finish_attention.1
  (76 shorter events, 19.5 us)
Async XLA Ops:
  7.2 1.2 copy-start.9
  15.2 9.7 %copy-start.27 = (bf16[512,512]{1,0:T(8,128)(2,1)S(1)}, bf16[512,512]{1,0:T(8,128)(2,1)}, u32[]{:S(2)}) copy-start(bf16[512,512]{1,0:T(8,128)(2,1)} %param.11) | copy-start | bytes 1572868
  15.2 11.7 %copy-start.10 = (bf16[1024,512]{1,0:T(8,128)(2,1)S(1)}, bf16[1024,512]{1,0:T(8,128)(2,1)}, u32[]{:S(2)}) copy-start(bf16[1024,512]{1,0:T(8,128)(2,1)} %tok_ref.3) | copy-start | bytes 3145732
  15.2 34.6 %all-to-all-start = ((bf16[32,56,512]{2,1,0:T(8,128)(2,1)}), bf16[32,56,512]{2,1,0:T(8,128)(2,1)}, u32[]{:S(2)}, u32[]{:S(2)}) async-start(bf16[32,56,512]{2,1,0:T(8,128)(2,1)} %bitcast.1), calls=%async_computation | async-start | bytes 3670016 | tf_op jit(solution)/shard_map/all_to_all | solution.py:440
  24.8 2.1 copy-start.1
  24.8 44.2 %all-gather.2.cloned.1.call-start = ((), (), s32[]{:S(2)}) async-start(), calls=%async_computation.7 | async-start | bytes 4718592 | tf_op jit(solution)/shard_map/all_gather | solution.py:538
  32.5 1.2 copy-start.6
  33.7 1.0 copy-start.13
  63.0 6.0 %copy-start.4 = (bf16[1024,512]{1,0:T(8,128)(2,1)S(1)}, bf16[1024,512]{1,0:T(8,128)(2,1)}, u32[]{:S(2)}) copy-start(bf16[1024,512]{1,0:T(8,128)(2,1)} %cot_ref.5) | copy-start | bytes 3145732
  63.0 20.3 %all-to-all-start.1 = ((bf16[32,48,256]{2,1,0:T(8,128)(2,1)}), bf16[32,48,256]{2,1,0:T(8,128)(2,1)S(1)}, u32[]{:S(2)}, u32[]{:S(2)}) async-start(bf16[32,48,256]{2,1,0:T(8,128)(2,1)} %bitcast.25), calls=%async_computation.1 | async-start | bytes 1572864 | tf_op jit(solution)/shard_map/all_to_all | solution.py:440
  69.0 2.2 copy-start
  74.2 2.0 copy-start.2
  83.3 0.9 copy-start.26
  104.1 18.5 %all-to-all-start.2 = ((bf16[32,48,256]{2,1,0:T(8,128)(2,1)}), bf16[32,48,256]{2,1,0:T(8,128)(2,1)S(1)}, u32[]{:S(2)}, u32[]{:S(2)}) async-start(bf16[32,48,256]{2,1,0:T(8,128)(2,1)} %bitcast.23), calls=%async_computation.2 | async-start | bytes 1572864 | tf_op jit(solution)/shard_map/all_to_all | solution.py:440
  108.3 70.8 %reduce-scatter.2.cloned.1.call-start = ((), (), s32[]{:S(2)}) async-start(), calls=%async_computation.8 | async-start | bytes 4718592 | tf_op jit(solution)/shard_map/reduce_scatter | solution.py:640
  122.6 0.9 copy-start.25
  138.5 28.3 %all-to-all-start.3 = ((bf16[32,48,512]{2,1,0:T(8,128)(2,1)}), bf16[32,48,512]{2,1,0:T(8,128)(2,1)S(1)}, u32[]{:S(2)}, u32[]{:S(2)}) async-start(bf16[32,48,512]{2,1,0:T(8,128)(2,1)} %bitcast.21), calls=%async_computation.3 | async-start | bytes 3145728 | tf_op jit(solution)/shard_map/all_to_all | solution.py:440
  144.6 13.5 %copy-start.5 = (bf16[1024,768]{1,0:T(8,128)(2,1)S(1)}, bf16[1024,768]{1,0:T(8,128)(2,1)}, u32[]{:S(2)}) copy-start(bf16[1024,768]{1,0:T(8,128)(2,1)} %get-tuple-element.64.gpk_ref) | copy-start | bytes 4718596
  158.1 1.2 copy-start.14
  159.4 1.1 copy-start.17
  160.5 1.1 copy-start.18
  162.8 1.0 copy-start.15
  163.8 2.7 %collective-permute-start = (bf16[1024,512]{1,0:T(8,128)(2,1)S(1)}, bf16[1024,512]{1,0:T(8,128)(2,1)S(1)}, u32[]{:S(2)}, u32[]{:S(2)}) collective-permute-start(bf16[1024,512]{1,0:T(8,128)(2,1)S(1)} %get-tuple-element.68), channel_id=1, source_target_pairs={{0,4},{4,0},{1,5},{5,1},{2,6},{6,2},{3,7},{7,3},{8,12},{12,8},{9,1... | collective-permute-start | bytes 3145736 | tf_op jit(solution)/shard_map/ppermute | solution.py:445
  166.8 1.2 copy-start.16
  169.2 35.7 %all-to-all-start.4 = ((bf16[64,16,512]{2,1,0:T(8,128)(2,1)}), bf16[64,16,512]{2,1,0:T(8,128)(2,1)S(1)}, u32[]{:S(2)}, u32[]{:S(2)}) async-start(bf16[64,16,512]{2,1,0:T(8,128)(2,1)} %bitcast.13), calls=%async_computation.5 | async-start | bytes 2097152 | tf_op jit(solution)/shard_map/all_to_all | solution.py:506
  179.1 1.0 copy-start.19
  180.2 15.5 %collective-permute-start.1 = (bf16[128,512]{1,0:T(8,128)(2,1)S(1)}, bf16[128,512]{1,0:T(8,128)(2,1)S(1)}, u32[]{:S(2)}, u32[]{:S(2)}) collective-permute-start(bf16[128,512]{1,0:T(8,128)(2,1)S(1)} %get-tuple-element.71), channel_id=1, source_target_pairs={{0,8},{8,16},{16,24},{24,0},{1,9},{9,17},{17,25},{25,1},{2,10},{10... | collective-permute-start | bytes 393224 | tf_op jit(solution)/shard_map/ppermute | solution.py:458
  181.5 16.9 %collective-permute-start.2 = (bf16[128,512]{1,0:T(8,128)(2,1)S(1)}, bf16[128,512]{1,0:T(8,128)(2,1)S(1)}, u32[]{:S(2)}, u32[]{:S(2)}) collective-permute-start(bf16[128,512]{1,0:T(8,128)(2,1)S(1)} %get-tuple-element.72), channel_id=1, source_target_pairs={{0,16},{8,24},{16,0},{24,8},{1,17},{9,25},{17,1},{25,9},{2,18},{10... | collective-permute-start | bytes 393224 | tf_op jit(solution)/shard_map/ppermute | solution.py:458
  183.9 14.5 %collective-permute-start.3 = (bf16[128,512]{1,0:T(8,128)(2,1)S(1)}, bf16[128,512]{1,0:T(8,128)(2,1)S(1)}, u32[]{:S(2)}, u32[]{:S(2)}) collective-permute-start(bf16[128,512]{1,0:T(8,128)(2,1)S(1)} %get-tuple-element.73), channel_id=1, source_target_pairs={{0,24},{8,0},{16,8},{24,16},{1,25},{9,1},{17,9},{25,17},{2,26},{10... | collective-permute-start | bytes 393224 | tf_op jit(solution)/shard_map/ppermute | solution.py:458
  198.5 4.8 %collective-permute-start.4 = (bf16[32,512]{1,0:T(8,128)(2,1)S(1)}, bf16[32,512]{1,0:T(8,128)(2,1)S(1)}, u32[]{:S(2)}, u32[]{:S(2)}) collective-permute-start(bf16[32,512]{1,0:T(8,128)(2,1)S(1)} %get-tuple-element.75), channel_id=1, source_target_pairs={{0,32},{32,64},{64,96},{96,0},{1,33},{33,65},{65,97},{97,1},{2,34}... | collective-permute-start | bytes 98312 | tf_op jit(solution)/shard_map/ppermute | solution.py:458
  199.8 4.3 %collective-permute-start.5 = (bf16[32,512]{1,0:T(8,128)(2,1)S(1)}, bf16[32,512]{1,0:T(8,128)(2,1)S(1)}, u32[]{:S(2)}, u32[]{:S(2)}) collective-permute-start(bf16[32,512]{1,0:T(8,128)(2,1)S(1)} %get-tuple-element.76), channel_id=1, source_target_pairs={{0,64},{32,96},{64,0},{96,32},{1,65},{33,97},{65,1},{97,33},{2,66}... | collective-permute-start | bytes 98312 | tf_op jit(solution)/shard_map/ppermute | solution.py:458
  202.2 2.8 %collective-permute-start.6 = (bf16[32,512]{1,0:T(8,128)(2,1)S(1)}, bf16[32,512]{1,0:T(8,128)(2,1)S(1)}, u32[]{:S(2)}, u32[]{:S(2)}) collective-permute-start(bf16[32,512]{1,0:T(8,128)(2,1)S(1)} %get-tuple-element.77), channel_id=1, source_target_pairs={{0,96},{32,0},{64,32},{96,64},{1,97},{33,1},{65,33},{97,65},{2,98}... | collective-permute-start | bytes 98312 | tf_op jit(solution)/shard_map/ppermute | solution.py:458
  205.2 1.0 copy-start.3
  206.2 34.9 %copy-start.24 = (s32[1,1024]{1,0:T(1,128)S(1)}, s32[1,1024]{1,0:T(1,128)}, u32[]{:S(2)}) copy-start(s32[1,1024]{1,0:T(1,128)} %copy-done.23) | copy-start | bytes 12292
  206.2 34.8 %all-to-all-start.5 = ((bf16[64,16,512]{2,1,0:T(8,128)(2,1)}), bf16[64,16,512]{2,1,0:T(8,128)(2,1)S(1)}, u32[]{:S(2)}, u32[]{:S(2)}) async-start(bf16[64,16,512]{2,1,0:T(8,128)(2,1)} %copy-done.3), calls=%async_computation.6 | async-start | bytes 2097152 | tf_op jit(solution)/shard_map/all_to_all | solution.py:511
  214.2 4.7 %collective-permute-start.7 = (bf16[32,512]{1,0:T(8,128)(2,1)S(1)}, bf16[32,512]{1,0:T(8,128)(2,1)S(1)}, u32[]{:S(2)}, u32[]{:S(2)}) collective-permute-start(bf16[32,512]{1,0:T(8,128)(2,1)S(1)} %add.6.refs_0_.after), channel_id=1, source_target_pairs={{0,32},{32,64},{64,96},{96,0},{1,33},{33,65},{65,97},{97,1},{2,34}... | collective-permute-start | bytes 98312 | tf_op jit(solution)/shard_map/ppermute | solution.py:458
  215.3 5.3 %collective-permute-start.8 = (bf16[32,512]{1,0:T(8,128)(2,1)S(1)}, bf16[32,512]{1,0:T(8,128)(2,1)S(1)}, u32[]{:S(2)}, u32[]{:S(2)}) collective-permute-start(bf16[32,512]{1,0:T(8,128)(2,1)S(1)} %add.6.refs_0_.after), channel_id=1, source_target_pairs={{0,64},{32,96},{64,0},{96,32},{1,65},{33,97},{65,1},{97,33},{2,66}... | collective-permute-start | bytes 98312 | tf_op jit(solution)/shard_map/ppermute | solution.py:458
  217.7 4.4 %collective-permute-start.9 = (bf16[32,512]{1,0:T(8,128)(2,1)S(1)}, bf16[32,512]{1,0:T(8,128)(2,1)S(1)}, u32[]{:S(2)}, u32[]{:S(2)}) collective-permute-start(bf16[32,512]{1,0:T(8,128)(2,1)S(1)} %add.6.refs_0_.after), channel_id=1, source_target_pairs={{0,96},{32,0},{64,32},{96,64},{1,97},{33,1},{65,33},{97,65},{2,98}... | collective-permute-start | bytes 98312 | tf_op jit(solution)/shard_map/ppermute | solution.py:458
  222.1 12.4 %collective-permute-start.10 = (bf16[128,512]{1,0:T(8,128)(2,1)S(1)}, bf16[128,512]{1,0:T(8,128)(2,1)S(1)}, u32[]{:S(2)}, u32[]{:S(2)}) collective-permute-start(bf16[128,512]{1,0:T(8,128)(2,1)S(1)} %gather.2.refs_0_), channel_id=1, source_target_pairs={{0,8},{8,16},{16,24},{24,0},{1,9},{9,17},{17,25},{25,1},{2,10},{10... | collective-permute-start | bytes 393224 | tf_op jit(solution)/shard_map/ppermute | solution.py:458
  223.4 13.9 %collective-permute-start.11 = (bf16[128,512]{1,0:T(8,128)(2,1)S(1)}, bf16[128,512]{1,0:T(8,128)(2,1)S(1)}, u32[]{:S(2)}, u32[]{:S(2)}) collective-permute-start(bf16[128,512]{1,0:T(8,128)(2,1)S(1)} %gather.2.refs_0_), channel_id=1, source_target_pairs={{0,16},{8,24},{16,0},{24,8},{1,17},{9,25},{17,1},{25,9},{2,18},{10... | collective-permute-start | bytes 393224 | tf_op jit(solution)/shard_map/ppermute | solution.py:458
  233.3 4.6 %collective-permute-start.12 = (bf16[128,512]{1,0:T(8,128)(2,1)S(1)}, bf16[128,512]{1,0:T(8,128)(2,1)S(1)}, u32[]{:S(2)}, u32[]{:S(2)}) collective-permute-start(bf16[128,512]{1,0:T(8,128)(2,1)S(1)} %gather.2.refs_0_), channel_id=1, source_target_pairs={{0,24},{8,0},{16,8},{24,16},{1,25},{9,1},{17,9},{25,17},{2,26},{10... | collective-permute-start | bytes 393224 | tf_op jit(solution)/shard_map/ppermute | solution.py:458
  237.9 11.6 %collective-permute-start.13 = (bf16[512,512]{1,0:T(8,128)(2,1)S(1)}, bf16[512,512]{1,0:T(8,128)(2,1)}, u32[]{:S(2)}, u32[]{:S(2)}) collective-permute-start(bf16[512,512]{1,0:T(8,128)(2,1)S(1)} %gather.3.mine_ref), channel_id=1, source_target_pairs={{0,4},{4,0},{1,5},{5,1},{2,6},{6,2},{3,7},{7,3},{8,12},{12,8},{9,1... | collective-permute-start | bytes 1572872 | tf_op jit(solution)/shard_map/ppermute | solution.py:445
  241.0 11.1 %collective-permute-start.14 = (bf16[1024,512]{1,0:T(8,128)(2,1)S(1)}, bf16[1024,512]{1,0:T(8,128)(2,1)S(1)}, u32[]{:S(2)}, u32[]{:S(2)}) collective-permute-start(bf16[1024,512]{1,0:T(8,128)(2,1)S(1)} %bitcast.17), channel_id=1, source_target_pairs={{0,4},{4,0},{1,5},{5,1},{2,6},{6,2},{3,7},{7,3},{8,12},{12,8},{9,1... | collective-permute-start | bytes 3145736 | tf_op jit(solution)/shard_map/ppermute | solution.py:445
  241.1 1.2 copy-start.11
  242.3 1.2 copy-start.12
  243.5 1.6 copy-start.20
  252.1 1.2 copy-start.7
  253.3 1.2 copy-start.8
  (3 other events, 2.1 us)
Sparse Core Ops, SparseCore 0:
  27.9 33.7 all-gather.1
  121.3 53.4 reduce-scatter.1

commit v3 on v2

--- a/solution.py
+++ b/solution.py
@@ -62,49 +62,46 @@
     return jnp.where(inside, value, 0.0).astype(BF16)
 
 
-def ball_weights(queries, key_rows, head, head_size):
-    columns = queries.shape[1]
-    asked = queries * head_mask(columns, head, head_size, head_size ** (-0.5))
+def by_head(rows, head_size, value):
+    columns = rows.shape[1]
+    heads = [rows * head_mask(columns, head, head_size, value) for head in range(columns // head_size)]
+    return jnp.concatenate(heads, axis=0)
+
+
+def ball_weights(key_rows, asked):
     scores = mm_nt(key_rows, asked)
     raised = jnp.exp(scores - jnp.max(scores, axis=0, keepdims=True))
-    return raised * (1.0 / jnp.sum(raised, axis=0, keepdims=True)), asked
+    return raised * (1.0 / jnp.sum(raised, axis=0, keepdims=True))
 
 
 def ball_attend(packed, head_size):
     columns = packed.shape[1] // 3
     queries, key_rows = packed[:, :columns], packed[:, columns : 2 * columns]
-    values_t = flip(packed[:, 2 * columns :])
-    parts = []
-    for head in range(columns // head_size):
-        weights, _ = ball_weights(queries, key_rows, head, head_size)
-        own = values_t[head * head_size : (head + 1) * head_size]
-        parts.append(mm(own, weights.astype(BF16)))
-    return jnp.concatenate(parts, axis=0).T.astype(BF16)
+    rounded = ball_weights(key_rows, by_head(queries, head_size, head_size ** (-0.5))).astype(BF16)
+    return per_head(flip(packed[:, 2 * columns :]), rounded, head_size).astype(BF16)
+
+
+def per_head(rows_t, weights, head_size):
+    columns, count = rows_t.shape
+    parts = [
+        mm(rows_t[head * head_size : (head + 1) * head_size], weights[:, head * count : (head + 1) * count])
+        for head in range(columns // head_size)
+    ]
+    return jnp.concatenate(parts, axis=0).T
 
 
 def ball_attend_back(packed, grad_out, head_size):
     columns = packed.shape[1] // 3
     queries, key_rows = packed[:, :columns], packed[:, columns : 2 * columns]
-    values = packed[:, 2 * columns :]
-    keys_t = flip(key_rows * jnp.asarray(head_size ** (-0.5), BF16))
-    asked_all, upstream_all, rounded_all, dscore_all, grad_queries = [], [], [], [], []
-    for head in range(columns // head_size):
-        weights, asked = ball_weights(queries, key_rows, head, head_size)
-        upstream = grad_out * head_mask(columns, head, head_size, 1.0)
-        dprob = mm_nt(values, upstream)
-        dscore = weights * (dprob - jnp.sum(dprob * weights, axis=0, keepdims=True))
-        dscore = dscore.astype(BF16)
-        own = keys_t[head * head_size : (head + 1) * head_size]
-        grad_queries.append(mm(own, dscore))
-        asked_all.append(asked)
-        upstream_all.append(upstream)
-        rounded_all.append(weights.astype(BF16))
-        dscore_all.append(dscore)
-    grad_values = mm(
-        jnp.concatenate(rounded_all, axis=1), jnp.concatenate(upstream_all, axis=0)
-    )
-    grad_keys = mm(jnp.concatenate(dscore_all, axis=1), jnp.concatenate(asked_all, axis=0))
-    grad_queries = jnp.concatenate(grad_queries, axis=0).T
+    asked = by_head(queries, head_size, head_size ** (-0.5))
+    upstream = by_head(grad_out, head_size, 1.0)
+    weights = ball_weights(key_rows, asked)
+    dprob = mm_nt(packed[:, 2 * columns :], upstream)
+    dscore = weights * (dprob - jnp.sum(dprob * weights, axis=0, keepdims=True))
+    dscore = dscore.astype(BF16)
+    grad_values = mm(weights.astype(BF16), upstream)
+    grad_keys = mm(dscore, asked)
+    grad_queries = per_head(flip(key_rows * jnp.asarray(head_size ** (-0.5), BF16)), dscore, head_size)
     return jnp.concatenate([grad_queries, grad_keys, grad_values], axis=1).astype(BF16)
 
 
@@ -271,17 +268,16 @@
     normed = (middle_f * second_scale).astype(BF16)
     sn_ref[...] = normed
     grad_second = jnp.zeros((BALL, width), F32)
-    for chunk in range(chunks):
+    pres = [mm(normed, up_ref[chunk * width : (chunk + 1) * width, :]) for chunk in range(chunks)]
+    for chunk, pre in enumerate(pres):
         columns = slice(chunk * width, (chunk + 1) * width)
-        up = up_ref[columns, :]
-        pre = mm(normed, up)
         square = pre * pre
         upper = 0.5 + 0.5 * jnp.tanh(pre * (rate + cubic * square))
         gated_ref[:, columns] = (pre * upper).astype(BF16)
         slope = upper * (1.0 + (1.0 - upper) * (pre * (2.0 * rate + 6.0 * cubic * square)))
         grad_pre = (act_ref[:, columns].astype(F32) * slope).astype(BF16)
         pre_ref[:, columns] = grad_pre
-        grad_second = grad_second + mm_nt(grad_pre, up)
+        grad_second = grad_second + mm_nt(grad_pre, up_ref[columns, :])
     grad_middle = (
         cot_ref[...].astype(F32) + norm_back(middle_f, second_scale, grad_second)
     ).astype(BF16)
@@ -381,11 +377,15 @@
     refs[-1][...] = total.astype(BF16)
 
 
-def spread_kernel(after, in_ref, out_ref):
+def add_parts(in_ref):
     total = in_ref[0].astype(F32)
     for part in range(1, in_ref.shape[0]):
         total = total + in_ref[part].astype(F32)
-    total = total.astype(BF16)
+    return total.astype(BF16)
+
+
+def spread_kernel(after, also, in_ref, out_ref):
+    total = add_parts(in_ref)
     for part in range(out_ref.shape[0]):
         out_ref[part] = total
 
@@ -398,7 +398,7 @@
         out_ref[pl.ds(pl.multiple_of(start, size), size), :] = in_ref[...]
 
 
-def last_kernel(tok_ref, gm_ref, first_ref, ret_ref, part_ref, out_ref):
+def last_kernel(_, tok_ref, gm_ref, first_ref, ret_ref, part_ref, out_ref):
     slots = ret_ref.shape[0]
     slot_col = as_column(part_ref[...].astype(F32)).astype(jnp.int32)
     pick = onehot(iota((BALL, slots), 1) == slot_col)
@@ -423,7 +423,7 @@
         down_ref[...] = mine_ref[...].astype(F32).T
 
 
-def finish_attention_kernel(_, also, core_ref, mine_ref, other_ref, qkv_ref, proj_ref):
+def finish_attention_kernel(core_ref, mine_ref, other_ref, qkv_ref, proj_ref):
     core = core_ref[0]
     width = mine_ref.shape[1]
     half = mine_ref.shape[0] // 4
@@ -489,27 +489,35 @@
     return block
 
 
+def share_of_sum(block, axes):
+    count = lax.axis_size(axes)
+    rows, columns = block.shape
+    parts = block.reshape(count, rows // count, columns)
+    return lax.all_to_all(parts, axes, split_axis=0, concat_axis=0, tiled=True)
+
+
+def whole_parts(parts):
+    return parts, pl.BlockSpec(parts.shape, lambda step: (0, 0, 0))
+
+
 def sum_by_steps(block, axes, after):
     parts = [block]
     for axis in axes:
         parts = add_split(parts, axis, after)
-    share = block = add(parts, after)
+    halfway = parts[0]
+    block = add(parts, after)
     for axis in reversed(axes):
         block = gather(block, axis)
-    return block, share
-
-
-def sum_at_once(block, axes, after):
-    count = lax.axis_size(axes)
-    rows, columns = block.shape
-    parts = block.reshape(count, rows // count, columns)
-    parts = lax.all_to_all(parts, axes, split_axis=0, concat_axis=0, tiled=True)
-    spread = (shape(parts.shape), pl.BlockSpec(parts.shape, lambda step: (0, 0, 0)))
+    return block, halfway
+
+
+def sum_at_once(block, axes, after, also):
+    parts = share_of_sum(block, axes)
     (spread,) = call(
-        spread_kernel, 1, [(after, ANY), (parts, spread[1])], [spread], name="add_spread",
+        spread_kernel, 1, [(after, ANY), (also, ANY), whole_parts(parts)], [(shape(parts.shape), whole_parts(parts)[1])], name="add_spread",
     )
     told = lax.all_to_all(spread, axes, split_axis=0, concat_axis=0, tiled=True)
-    return told.reshape(rows, columns)
+    return told.reshape(block.shape)
 
 
 def bind(kernel, *fixed):
@@ -603,6 +611,9 @@
         scratch=[pltpu.VMEM((width, rows), BF16), pltpu.VMEM((width, rows), BF16), pltpu.VMEM((rows, width), F32)],
         name="mlp_weights", vmem=VMEM_BYTES,
     )
+    mlp_part = lax.psum_scatter(
+        mlp_both.reshape(2 * hidden, width), ("core", "narrow"), scatter_dimension=0, tiled=True
+    )
     first_local, qkv_local, proj_local = call(
         bind(local_back_kernel, head_size), balls,
         [
@@ -632,25 +643,22 @@
     )
     (grad_tokens,) = call(
         last_kernel, balls,
-        [(tokens, by_row(width)), (grad_middle, by_row(width)), (first_local, by_row(width)), (grad_returned, whole(slots, width)), part],
+        [(mlp_part, ANY), (tokens, by_row(width)), (grad_middle, by_row(width)), (first_local, by_row(width)), (grad_returned, whole(slots, width)), part],
         [(shape((rows, width)), by_row(width))],
         flops=LONG, name="last",
     )
 
-    mlp_part = lax.psum_scatter(
-        mlp_both.reshape(2 * hidden, width), ("core", "narrow"), scatter_dimension=0, tiled=True
-    )
     pair = add([keep, swap_core(send)], grad_returned)
-    mlp_mine, mlp_share = sum_by_steps(mlp_part, ("x", "z"), pair)
+    mlp_mine, halfway = sum_by_steps(mlp_part, ("x", "z"), pair)
     mlp_other = swap_core(mlp_mine)
     grad_up, grad_down = call(
         finish_mlp_kernel, 1, [flag, whole_array(mlp_mine), whole_array(mlp_other)],
         [(shape((width, width), F32), whole(width, width)), (shape((width, width), F32), whole(width, width))],
         name="finish_mlp",
     )
-    mine = sum_at_once(pair, ("narrow", "x", "z"), mlp_share)
+    mine = add([sum_at_once(pair, ("narrow", "x", "z"), grad_tokens, halfway)], mlp_mine)
     grad_qkv, grad_proj = call(
-        finish_attention_kernel, 1, [(grad_tokens, ANY), (grad_up, ANY), flag, whole_array(mine), whole_array(swap_core(mine))],
+        finish_attention_kernel, 1, [flag, whole_array(mine), whole_array(swap_core(mine))],
         [(shape((width, 2 * third), F32), whole(width, 2 * third)), (shape((width, width), F32), whole(width, width))],
         name="finish_attention",
     )

time: 265 us -> 251 us (0.947)
  Pallas kernels: 101 us -> 93.1 us
  starting transfers between devices: 72.8 us -> 69.4 us
    pallas_call x19 -> x20, Pallas kernels: 101 us -> 93.1 us  [call(): pl.pallas_call(kernel, grid=(steps,), out_shape=[out for out, _ in outs],...]
    ppermute x12, waiting for transfers between devices: 22.6 us -> 16.7 us  [shift_by(): lax.ppermute(block, axis, [(place, (place + shift) % count) for place in...]
    ppermute x12, starting transfers between devices: 25.6 us -> 20.6 us  [shift_by(): lax.ppermute(block, axis, [(place, (place + shift) % count) for place in...]
    ppermute x3, waiting for transfers between devices: 2.45 us -> 5.57 us  [swap_core(): return lax.ppermute(block, 'core', [(0, 1), (1, 0)])]
    unnamed x56 -> x54, local copies, waits for them, and re-layouts: 25.6 us -> 23.2 us
  transfers between devices with their start and end apart: 23 -> 23, of which waited for: 14 -> 15; matrix products, arithmetic and copies ran while one was open for 1% -> 1% of each run, Pallas kernels for 28% -> 26%
where the time goes in v3:
time: 251 us; the launch traced here: 250 us
  Pallas kernels  93.1 us (37%)
  starting transfers between devices  69.4 us (28%)
  waiting for transfers between devices  47.5 us (19%)
  local copies, waits for them, and re-layouts  23.2 us (9%)
  between operations  14.3 us (6%)
    pallas_call x20, Pallas kernels, call(): pl.pallas_call(kernel, grid=(steps,), out_shape=[out for out, _ in outs],...  93.1 us
    all_to_all x4, starting transfers between devices, exchange(): lax.all_to_all(sent, ('z', 'x', 'core'), split_axis=0, concat_axis=0, til...  25.8 us
    all_to_all x4, waiting for transfers between devices, exchange(): lax.all_to_all(sent, ('z', 'x', 'core'), split_axis=0, concat_axis=0, til...  25.2 us
    unnamed x54, local copies, waits for them, and re-layouts  23.2 us
    ppermute x12, starting transfers between devices, shift_by(): lax.ppermute(block, axis, [(place, (place + shift) % count) for place in...  20.6 us
    ppermute x12, waiting for transfers between devices, shift_by(): lax.ppermute(block, axis, [(place, (place + shift) % count) for place in...  16.7 us
    all_to_all x1, starting transfers between devices, share_of_sum(): return lax.all_to_all(parts, axes, split_axis=0, concat_axis=0, tiled=True)  9.21 us
    all_to_all x1, starting transfers between devices, sum_at_once(): told = lax.all_to_all(spread, axes, split_axis=0, concat_axis=0, tiled=True)  8.17 us
  transfers between devices with their start and end apart: 23, of which 15 were waited for; matrix products, arithmetic and copies ran while one was open for 1% of the time, Pallas kernels for 26%

profile of v3, /device:TPU:1, one launch (start us, length us, event | category | flops | bytes accessed | tf_op | source)
XLA Modules:
  0.0 249.5 jit_solution(177895863414203497)
XLA Ops:
  7.2 1.2 copy-done.7
  9.1 5.5 %route.1 = (bf16[1792,512]{1,0:T(8,128)(2,1)}, s32[1,1024]{1,0:T(1,128)S(1)}) custom-call(s32[1,1024]{1,0:T(1,128)S(1)} %bitcast.18, bf16[1024,512]{1,0:T(8,128)(2,1)S(1)} %copy-done.7), custom_call_target="tpu_custom_call" | custom-call | flops 99999997952 | tf_op jit(solution)/shard_map/route/pallas_call | solution.py:129
  15.2 9.6 %all-to-all-start = ((bf16[32,56,512]{2,1,0:T(8,128)(2,1)}), bf16[32,56,512]{2,1,0:T(8,128)(2,1)}, u32[]{:S(2)}, u32[]{:S(2)}) async-start(bf16[32,56,512]{2,1,0:T(8,128)(2,1)} %bitcast.1), calls=%async_computation | async-start | bytes 3670016 | tf_op jit(solution)/shard_map/all_to_all | solution.py:440
  24.9 2.0 broadcast_select_fusion
  26.9 4.3 %first_local.1 = (bf16[1024,512]{1,0:T(8,128)(2,1)S(1)}, bf16[1024,768]{1,0:T(8,128)(2,1)S(1)}, bf16[1024,256]{1,0:T(8,128)(2,1)S(1)}) custom-call(bf16[1024,512]{1,0:T(8,128)(2,1)S(1)} %copy-done.8, bf16[512,1536]{1,0:T(8,128)(2,1)S(1)} %copy-done.1), custom_call_target="tpu_custom_call" | custom-call | tf_op jit(solution)/shard_map/first_local/pallas_call | solution.py:129
  34.3 15.5 %all-to-all-done = bf16[32,56,512]{2,1,0:T(8,128)(2,1)} async-done(((bf16[32,56,512]{2,1,0:T(8,128)(2,1)}), bf16[32,56,512]{2,1,0:T(8,128)(2,1)}, u32[]{:S(2)}, u32[]{:S(2)}) %all-to-all-start) | async-done | bytes 1835040 | tf_op jit(solution)/shard_map/all_to_all | solution.py:440
  49.8 11.7 %moved.1 = (bf16[1024,512]{1,0:T(8,128)(2,1)}, bf16[1024,768]{1,0:T(8,128)(2,1)}, s32[1,1536]{1,0:T(1,128)}, bf16[1536,256]{1,0:T(8,128)(2,1)}) custom-call(bf16[1024,256]{1,0:T(8,128)(2,1)} %copy-done.20, bf16[1792,512]{1,0:T(8,128)(2,1)} %bitcast.2.refs_1_, bf16[512,1536]{1,0:T(8,128)(2,1)} %refs_4_.1), custom_call_target="tpu_custom_call" | custom-call | flops 99999997952 | tf_op jit(solution)/shard_map/moved/pallas_call | solution.py:129
  61.5 6.0 %all-to-all-start.1 = ((bf16[32,48,256]{2,1,0:T(8,128)(2,1)}), bf16[32,48,256]{2,1,0:T(8,128)(2,1)S(1)}, u32[]{:S(2)}, u32[]{:S(2)}) async-start(bf16[32,48,256]{2,1,0:T(8,128)(2,1)} %bitcast.24), calls=%async_computation.1 | async-start | bytes 1572864 | tf_op jit(solution)/shard_map/all_to_all | solution.py:440
  67.5 2.2 copy-done
  69.7 3.0 %grad_act.1.act_ref = bf16[1024,2048]{1,0:T(8,128)(2,1)S(1)} custom-call(bf16[1024,512]{1,0:T(8,128)(2,1)S(1)} %copy-done.3, bf16[4096,512]{1,0:T(8,128)(2,1)S(1)} %copy-done), custom_call_target="tpu_custom_call" | custom-call | tf_op jit(solution)/shard_map/grad_act/pallas_call | solution.py:129
  72.7 2.0 copy-done.2
  74.7 7.1 %all-to-all-done.1 = bf16[32,48,256]{2,1,0:T(8,128)(2,1)S(1)} async-done(((bf16[32,48,256]{2,1,0:T(8,128)(2,1)}), bf16[32,48,256]{2,1,0:T(8,128)(2,1)S(1)}, u32[]{:S(2)}, u32[]{:S(2)}) %all-to-all-start.1) | async-done | bytes 786464 | tf_op jit(solution)/shard_map/all_to_all | solution.py:440
  82.7 19.1 %middle.1 = (bf16[1024,512]{1,0:T(8,128)(2,1)}, bf16[1024,512]{1,0:T(8,128)(2,1)}, bf16[1024,512]{1,0:T(8,128)(2,1)}, bf16[1024,2048]{1,0:T(8,128)(2,1)}, bf16[1...) custom-call(bf16[1024,512]{1,0:T(8,128)(2,1)} %tok_ref.3, ...), custom_call_target="tpu_custom_call" | custom-call | flops 99999997952 | tf_op jit(solution)/shard_map/middle/pallas_call | solution.py:129
  101.8 4.1 %all-to-all-start.2 = ((bf16[32,48,256]{2,1,0:T(8,128)(2,1)}), bf16[32,48,256]{2,1,0:T(8,128)(2,1)S(1)}, u32[]{:S(2)}, u32[]{:S(2)}) async-start(bf16[32,48,256]{2,1,0:T(8,128)(2,1)} %bitcast.22), calls=%async_computation.3 | async-start | bytes 1572864 | tf_op jit(solution)/shard_map/all_to_all | solution.py:440
  106.2 12.7 %mlp_weights.1 = (bf16[1024,512]{1,0:T(8,128)(2,1)}, bf16[2,2048,512]{2,1,0:T(8,128)(2,1)}) custom-call(bf16[1024,512]{1,0:T(8,128)(2,1)} %get-tuple-element.48.mid_ref, bf16[1024,2048]{1,0:T(8,128)(2,1)} %get-tuple-element.49.gated_ref, bf16[4096,512]{1,0:T(8,128)(2,1)} %all-gather.2.cloned.1.call-done.down_ref.up_ref, bf16[1024,512]{1,0:T(8,128)(2,1)} %cot_ref.5, ...), custom_call_target="tpu_custom_call" | custom-call | tf_op jit(solution)/shard_map/mlp_weights/pallas_call | solution.py:129
  118.9 1.4 all-to-all-done.2
  121.2 12.0 %moved_back.1 = (bf16[1024,768]{1,0:T(8,128)(2,1)}, bf16[1536,512]{1,0:T(8,128)(2,1)}) custom-call(bf16[1024,512]{1,0:T(8,128)(2,1)} %get-tuple-element.38.refs_0_, bf16[1536,256]{1,0:T(8,128)(2,1)} %bitcast.21, s32[1,1536]{1,0:T(1,128)} %get-tuple-element.61.refs_2_, bf16[1024,768]{1,0:T(8,128)(2,1)} %get-tuple-element.62.refs_3_, bf16[512,1536]{1,0:T(8,128)(2,1)} %refs_4_.1), custom_call_target="tpu_custom_call" | custom-call | flops 99999997952 | tf_op jit(solution)/shard_map/moved_back/pallas_call | solution.py:129
  133.2 6.1 %all-to-all-start.3 = ((bf16[32,48,512]{2,1,0:T(8,128)(2,1)}), bf16[32,48,512]{2,1,0:T(8,128)(2,1)S(1)}, u32[]{:S(2)}, u32[]{:S(2)}) async-start(bf16[32,48,512]{2,1,0:T(8,128)(2,1)} %bitcast.20), calls=%async_computation.4 | async-start | bytes 3145728 | tf_op jit(solution)/shard_map/all_to_all | solution.py:440
  139.3 11.6 %local_back.1 = (f32[1024,512]{1,0:T(8,128)}, bf16[512,768]{1,0:T(8,128)(2,1)}, bf16[512,512]{1,0:T(8,128)(2,1)}) custom-call(bf16[1024,768]{1,0:T(8,128)(2,1)} %copy-done.5, bf16[1024,256]{1,0:T(8,128)(2,1)} %get-tuple-element.56.refs_1_, bf16[1024,512]{1,0:T(8,128)(2,1)} %copy-done.11, bf16[512,1536]{1,0:T(8,128)(2,1)} %refs_4_.1, ...), custom_call_target="tpu_custom_call" | custom-call | tf_op jit(solution)/shard_map/local_back/pallas_call | solution.py:129
  150.9 1.2 copy-done.12
  154.3 2.2 moved_weights.1
  157.7 2.6 %collective-permute-done.refs_1_ = bf16[1024,512]{1,0:T(8,128)(2,1)S(1)} collective-permute-done((bf16[1024,512]{1,0:T(8,128)(2,1)}, bf16[1024,512]{1,0:T(8,128)(2,1)S(1)}, u32[]{:S(2)}, u32[]{:S(2)}) %collective-permute-start) | collective-permute-done | bytes 1048608 | tf_op jit(solution)/shard_map/ppermute | solution.py:445
  161.5 1.2 copy-done.14
  162.8 1.2 add.6.refs_0_.after
  164.0 9.2 %all-to-all-start.4 = ((bf16[64,16,512]{2,1,0:T(8,128)(2,1)}), bf16[64,16,512]{2,1,0:T(8,128)(2,1)S(1)}, u32[]{:S(2)}, u32[]{:S(2)}) async-start(bf16[64,16,512]{2,1,0:T(8,128)(2,1)} %bitcast.13), calls=%async_computation.5 | async-start | bytes 2097152 | tf_op jit(solution)/shard_map/all_to_all | solution.py:496
  175.4 2.4 collective-permute-start.2
  177.8 1.2 collective-permute-start.3
  179.0 1.2 copy-done.9
  180.2 1.2 copy-done.10
  182.5 1.6 copy-done.19
  184.1 4.3 %last.1.after = bf16[1024,512]{1,0:T(8,128)(2,1)} custom-call(bf16[512,512]{1,0:T(8,128)(2,1)S(1)} %copy-done.18, bf16[1024,512]{1,0:T(8,128)(2,1)S(1)} %copy-done.9, bf16[1024,512]{1,0:T(8,128)(2,1)S(1)} %copy-done.10, f32[1024,512]{1,0:T(8,128)S(1)} %copy-done.19, bf16[1536,512]{1,0:T(8,128)(2,1)S(1)} %bitcast.16, s32[1,1024]{1,0:T(1,128)S(1)} %copy-done.23), custom_call_target="tpu_custom_call" | custom-call | flops 99999997952 | tf_op jit(solution)/shard_map/last/pallas_call | solution.py:129
  188.4 1.4 collective-permute-done.1.refs_3_
  189.8 2.8 %collective-permute-done.2.refs_4_ = bf16[128,512]{1,0:T(8,128)(2,1)S(1)} collective-permute-done((bf16[128,512]{1,0:T(8,128)(2,1)S(1)}, bf16[128,512]{1,0:T(8,128)(2,1)S(1)}, u32[]{:S(2)}, u32[]{:S(2)}) %collective-permute-start.2) | collective-permute-done | bytes 131104 | tf_op jit(solution)/shard_map/ppermute | solution.py:458
  192.7 1.2 add_spread.1
  193.9 8.2 %all-to-all-start.5 = ((bf16[64,16,512]{2,1,0:T(8,128)(2,1)}), bf16[64,16,512]{2,1,0:T(8,128)(2,1)S(1)}, u32[]{:S(2)}, u32[]{:S(2)}) async-start(bf16[64,16,512]{2,1,0:T(8,128)(2,1)} %add_spread.1), calls=%async_computation.6 | async-start | bytes 2097152 | tf_op jit(solution)/shard_map/all_to_all | solution.py:519
  203.2 2.4 collective-permute-start.5
  205.6 1.2 collective-permute-start.6
  206.8 2.4 collective-permute-done.5.refs_2_
  209.1 2.1 collective-permute-done.6.refs_3_
  212.8 2.0 collective-permute-start.9
  214.8 4.1 %collective-permute-done.7.refs_1_ = bf16[32,512]{1,0:T(8,128)(2,1)S(1)} collective-permute-done((bf16[32,512]{1,0:T(8,128)(2,1)S(1)}, bf16[32,512]{1,0:T(8,128)(2,1)S(1)}, u32[]{:S(2)}, u32[]{:S(2)}) %collective-permute-start.7) | collective-permute-done | bytes 32800 | tf_op jit(solution)/shard_map/ppermute | solution.py:458
  219.6 3.2 %collective-permute-start.10 = (bf16[128,512]{1,0:T(8,128)(2,1)S(1)}, bf16[128,512]{1,0:T(8,128)(2,1)S(1)}, u32[]{:S(2)}, u32[]{:S(2)}) collective-permute-start(bf16[128,512]{1,0:T(8,128)(2,1)S(1)} %gather.2.refs_0_), channel_id=1, source_target_pairs={{0,8},{8,16},{16,24},{24,0},{1,9},{9,17},{17,25},{25,1},{2,10},{10... | collective-permute-start | bytes 393224 | tf_op jit(solution)/shard_map/ppermute | solution.py:458
  222.8 3.7 %collective-permute-start.11 = (bf16[128,512]{1,0:T(8,128)(2,1)S(1)}, bf16[128,512]{1,0:T(8,128)(2,1)S(1)}, u32[]{:S(2)}, u32[]{:S(2)}) collective-permute-start(bf16[128,512]{1,0:T(8,128)(2,1)S(1)} %gather.2.refs_0_), channel_id=1, source_target_pairs={{0,16},{8,24},{16,0},{24,8},{1,17},{9,25},{17,1},{25,9},{2,18},{10... | collective-permute-start | bytes 393224 | tf_op jit(solution)/shard_map/ppermute | solution.py:458
  227.6 2.6 %collective-permute-done.11.refs_2_ = bf16[128,512]{1,0:T(8,128)(2,1)S(1)} collective-permute-done((bf16[128,512]{1,0:T(8,128)(2,1)S(1)}, bf16[128,512]{1,0:T(8,128)(2,1)S(1)}, u32[]{:S(2)}, u32[]{:S(2)}) %collective-permute-start.11) | collective-permute-done | bytes 131104 | tf_op jit(solution)/shard_map/ppermute | solution.py:458
  230.7 5.1 %collective-permute-start.13 = (bf16[1024,512]{1,0:T(8,128)(2,1)S(1)}, bf16[1024,512]{1,0:T(8,128)(2,1)S(1)}, u32[]{:S(2)}, u32[]{:S(2)}) collective-permute-start(bf16[1024,512]{1,0:T(8,128)(2,1)S(1)} %add.8.mine_ref), channel_id=1, source_target_pairs={{0,4},{4,0},{1,5},{5,1},{2,6},{6,2},{3,7},{7,3},{8,12},{12,8},{9,1... | collective-permute-start | bytes 3145736 | tf_op jit(solution)/shard_map/ppermute | solution.py:445
  235.9 2.9 %collective-permute-done.14.other_ref = bf16[512,512]{1,0:T(8,128)(2,1)S(1)} collective-permute-done((bf16[512,512]{1,0:T(8,128)(2,1)S(1)}, bf16[512,512]{1,0:T(8,128)(2,1)S(1)}, u32[]{:S(2)}, u32[]{:S(2)}) %collective-permute-start.14) | collective-permute-done | bytes 524320 | tf_op jit(solution)/shard_map/ppermute | solution.py:445
  238.8 1.6 finish_mlp.1
  240.4 2.2 finish_attention.1
  (75 shorter events, 19.4 us)
Async XLA Ops:
  7.2 1.2 copy-start.7
  15.2 9.7 %copy-start.26 = (bf16[512,512]{1,0:T(8,128)(2,1)S(1)}, bf16[512,512]{1,0:T(8,128)(2,1)}, u32[]{:S(2)}) copy-start(bf16[512,512]{1,0:T(8,128)(2,1)} %param.11) | copy-start | bytes 1572868
  15.2 11.7 %copy-start.8 = (bf16[1024,512]{1,0:T(8,128)(2,1)S(1)}, bf16[1024,512]{1,0:T(8,128)(2,1)}, u32[]{:S(2)}) copy-start(bf16[1024,512]{1,0:T(8,128)(2,1)} %tok_ref.3) | copy-start | bytes 3145732
  15.2 34.6 %all-to-all-start = ((bf16[32,56,512]{2,1,0:T(8,128)(2,1)}), bf16[32,56,512]{2,1,0:T(8,128)(2,1)}, u32[]{:S(2)}, u32[]{:S(2)}) async-start(bf16[32,56,512]{2,1,0:T(8,128)(2,1)} %bitcast.1), calls=%async_computation | async-start | bytes 3670016 | tf_op jit(solution)/shard_map/all_to_all | solution.py:440
  24.8 2.1 copy-start.1
  24.8 42.7 %all-gather.2.cloned.1.call-start = ((), (), s32[]{:S(2)}) async-start(), calls=%async_computation.7 | async-start | bytes 4718592 | tf_op jit(solution)/shard_map/all_gather | solution.py:546
  31.3 1.2 copy-start.5
  32.5 1.0 copy-start.11
  33.5 0.8 copy-start.20
  61.5 6.0 %copy-start.3 = (bf16[1024,512]{1,0:T(8,128)(2,1)S(1)}, bf16[1024,512]{1,0:T(8,128)(2,1)}, u32[]{:S(2)}) copy-start(bf16[1024,512]{1,0:T(8,128)(2,1)} %cot_ref.5) | copy-start | bytes 3145732
  61.5 20.3 %all-to-all-start.1 = ((bf16[32,48,256]{2,1,0:T(8,128)(2,1)}), bf16[32,48,256]{2,1,0:T(8,128)(2,1)S(1)}, u32[]{:S(2)}, u32[]{:S(2)}) async-start(bf16[32,48,256]{2,1,0:T(8,128)(2,1)} %bitcast.24), calls=%async_computation.1 | async-start | bytes 1572864 | tf_op jit(solution)/shard_map/all_to_all | solution.py:440
  67.5 2.2 copy-start
  72.7 2.0 copy-start.2
  81.8 0.9 copy-start.25
  101.8 18.5 %all-to-all-start.2 = ((bf16[32,48,256]{2,1,0:T(8,128)(2,1)}), bf16[32,48,256]{2,1,0:T(8,128)(2,1)S(1)}, u32[]{:S(2)}, u32[]{:S(2)}) async-start(bf16[32,48,256]{2,1,0:T(8,128)(2,1)} %bitcast.22), calls=%async_computation.3 | async-start | bytes 1572864 | tf_op jit(solution)/shard_map/all_to_all | solution.py:440
  106.0 67.2 %reduce-scatter.2.cloned.1.call-start = ((), (), s32[]{:S(2)}) async-start(), calls=%async_computation.8 | async-start | bytes 4718592 | tf_op jit(solution)/shard_map/reduce_scatter | solution.py:614
  120.3 0.9 copy-start.24
  133.2 28.3 %all-to-all-start.3 = ((bf16[32,48,512]{2,1,0:T(8,128)(2,1)}), bf16[32,48,512]{2,1,0:T(8,128)(2,1)S(1)}, u32[]{:S(2)}, u32[]{:S(2)}) async-start(bf16[32,48,512]{2,1,0:T(8,128)(2,1)} %bitcast.20), calls=%async_computation.4 | async-start | bytes 3145728 | tf_op jit(solution)/shard_map/all_to_all | solution.py:440
  139.3 11.6 %copy-start.4 = (bf16[1024,768]{1,0:T(8,128)(2,1)S(1)}, bf16[1024,768]{1,0:T(8,128)(2,1)}, u32[]{:S(2)}) copy-start(bf16[1024,768]{1,0:T(8,128)(2,1)} %get-tuple-element.65.gpk_ref) | copy-start | bytes 4718596
  150.9 1.2 copy-start.12
  152.1 1.1 copy-start.15
  153.3 1.1 copy-start.16
  156.5 1.0 copy-start.13
  157.5 2.9 %collective-permute-start = (bf16[1024,512]{1,0:T(8,128)(2,1)}, bf16[1024,512]{1,0:T(8,128)(2,1)S(1)}, u32[]{:S(2)}, u32[]{:S(2)}) collective-permute-start(bf16[1024,512]{1,0:T(8,128)(2,1)} %get-tuple-element.69), channel_id=1, source_target_pairs={{0,4},{4,0},{1,5},{5,1},{2,6},{6,2},{3,7},{7,3},{8,12},{12,8},{9,1... | collective-permute-start | bytes 3145736 | tf_op jit(solution)/shard_map/ppermute | solution.py:445
  161.5 1.2 copy-start.14
  164.0 15.0 %copy-start.23 = (s32[1,1024]{1,0:T(1,128)S(1)}, s32[1,1024]{1,0:T(1,128)}, u32[]{:S(2)}) copy-start(s32[1,1024]{1,0:T(1,128)} %copy-done.22) | copy-start | bytes 12292
  164.0 28.7 %all-to-all-start.4 = ((bf16[64,16,512]{2,1,0:T(8,128)(2,1)}), bf16[64,16,512]{2,1,0:T(8,128)(2,1)S(1)}, u32[]{:S(2)}, u32[]{:S(2)}) async-start(bf16[64,16,512]{2,1,0:T(8,128)(2,1)} %bitcast.13), calls=%async_computation.5 | async-start | bytes 2097152 | tf_op jit(solution)/shard_map/all_to_all | solution.py:496
  173.2 1.0 copy-start.17
  174.3 15.5 %collective-permute-start.1 = (bf16[128,512]{1,0:T(8,128)(2,1)S(1)}, bf16[128,512]{1,0:T(8,128)(2,1)S(1)}, u32[]{:S(2)}, u32[]{:S(2)}) collective-permute-start(bf16[128,512]{1,0:T(8,128)(2,1)S(1)} %get-tuple-element.71), channel_id=1, source_target_pairs={{0,8},{8,16},{16,24},{24,0},{1,9},{9,17},{17,25},{25,1},{2,10},{10... | collective-permute-start | bytes 393224 | tf_op jit(solution)/shard_map/ppermute | solution.py:458
  175.4 17.2 %collective-permute-start.2 = (bf16[128,512]{1,0:T(8,128)(2,1)S(1)}, bf16[128,512]{1,0:T(8,128)(2,1)S(1)}, u32[]{:S(2)}, u32[]{:S(2)}) collective-permute-start(bf16[128,512]{1,0:T(8,128)(2,1)S(1)} %get-tuple-element.72), channel_id=1, source_target_pairs={{0,16},{8,24},{16,0},{24,8},{1,17},{9,25},{17,1},{25,9},{2,18},{10... | collective-permute-start | bytes 393224 | tf_op jit(solution)/shard_map/ppermute | solution.py:458
  177.8 14.8 %collective-permute-start.3 = (bf16[128,512]{1,0:T(8,128)(2,1)S(1)}, bf16[128,512]{1,0:T(8,128)(2,1)S(1)}, u32[]{:S(2)}, u32[]{:S(2)}) collective-permute-start(bf16[128,512]{1,0:T(8,128)(2,1)S(1)} %get-tuple-element.73), channel_id=1, source_target_pairs={{0,24},{8,0},{16,8},{24,16},{1,25},{9,1},{17,9},{25,17},{2,26},{10... | collective-permute-start | bytes 393224 | tf_op jit(solution)/shard_map/ppermute | solution.py:458
  179.0 1.2 copy-start.9
  180.2 1.2 copy-start.10
  181.4 1.0 copy-start.18
  182.5 1.6 copy-start.19
  188.4 4.3 %copy-start.6 = (bf16[1024,512]{1,0:T(8,128)(2,1)S(1)}, bf16[1024,512]{1,0:T(8,128)(2,1)}, u32[]{:S(2)}) copy-start(bf16[1024,512]{1,0:T(8,128)(2,1)} %last.1.after) | copy-start | bytes 3145732
  193.9 36.7 %all-to-all-start.5 = ((bf16[64,16,512]{2,1,0:T(8,128)(2,1)}), bf16[64,16,512]{2,1,0:T(8,128)(2,1)S(1)}, u32[]{:S(2)}, u32[]{:S(2)}) async-start(bf16[64,16,512]{2,1,0:T(8,128)(2,1)} %add_spread.1), calls=%async_computation.6 | async-start | bytes 2097152 | tf_op jit(solution)/shard_map/all_to_all | solution.py:519
  202.1 4.7 %collective-permute-start.4 = (bf16[32,512]{1,0:T(8,128)(2,1)S(1)}, bf16[32,512]{1,0:T(8,128)(2,1)S(1)}, u32[]{:S(2)}, u32[]{:S(2)}) collective-permute-start(bf16[32,512]{1,0:T(8,128)(2,1)S(1)} %get-tuple-element.75), channel_id=1, source_target_pairs={{0,32},{32,64},{64,96},{96,0},{1,33},{33,65},{65,97},{97,1},{2,34}... | collective-permute-start | bytes 98312 | tf_op jit(solution)/shard_map/ppermute | solution.py:458
  203.2 5.9 %collective-permute-start.5 = (bf16[32,512]{1,0:T(8,128)(2,1)S(1)}, bf16[32,512]{1,0:T(8,128)(2,1)S(1)}, u32[]{:S(2)}, u32[]{:S(2)}) collective-permute-start(bf16[32,512]{1,0:T(8,128)(2,1)S(1)} %get-tuple-element.76), channel_id=1, source_target_pairs={{0,64},{32,96},{64,0},{96,32},{1,65},{33,97},{65,1},{97,33},{2,66}... | collective-permute-start | bytes 98312 | tf_op jit(solution)/shard_map/ppermute | solution.py:458
  205.6 5.7 %collective-permute-start.6 = (bf16[32,512]{1,0:T(8,128)(2,1)S(1)}, bf16[32,512]{1,0:T(8,128)(2,1)S(1)}, u32[]{:S(2)}, u32[]{:S(2)}) collective-permute-start(bf16[32,512]{1,0:T(8,128)(2,1)S(1)} %get-tuple-element.77), channel_id=1, source_target_pairs={{0,96},{32,0},{64,32},{96,64},{1,97},{33,1},{65,33},{97,65},{2,98}... | collective-permute-start | bytes 98312 | tf_op jit(solution)/shard_map/ppermute | solution.py:458
  211.3 7.6 %collective-permute-start.7 = (bf16[32,512]{1,0:T(8,128)(2,1)S(1)}, bf16[32,512]{1,0:T(8,128)(2,1)S(1)}, u32[]{:S(2)}, u32[]{:S(2)}) collective-permute-start(bf16[32,512]{1,0:T(8,128)(2,1)S(1)} %add.7.refs_0_), channel_id=1, source_target_pairs={{0,32},{32,64},{64,96},{96,0},{1,33},{33,65},{65,97},{97,1},{2,34}... | collective-permute-start | bytes 98312 | tf_op jit(solution)/shard_map/ppermute | solution.py:458
  212.0 7.5 %collective-permute-start.8 = (bf16[32,512]{1,0:T(8,128)(2,1)S(1)}, bf16[32,512]{1,0:T(8,128)(2,1)S(1)}, u32[]{:S(2)}, u32[]{:S(2)}) collective-permute-start(bf16[32,512]{1,0:T(8,128)(2,1)S(1)} %add.7.refs_0_), channel_id=1, source_target_pairs={{0,64},{32,96},{64,0},{96,32},{1,65},{33,97},{65,1},{97,33},{2,66}... | collective-permute-start | bytes 98312 | tf_op jit(solution)/shard_map/ppermute | solution.py:458
  212.8 6.7 %collective-permute-start.9 = (bf16[32,512]{1,0:T(8,128)(2,1)S(1)}, bf16[32,512]{1,0:T(8,128)(2,1)S(1)}, u32[]{:S(2)}, u32[]{:S(2)}) collective-permute-start(bf16[32,512]{1,0:T(8,128)(2,1)S(1)} %add.7.refs_0_), channel_id=1, source_target_pairs={{0,96},{32,0},{64,32},{96,64},{1,97},{33,1},{65,33},{97,65},{2,98}... | collective-permute-start | bytes 98312 | tf_op jit(solution)/shard_map/ppermute | solution.py:458
  219.6 8.1 %collective-permute-start.10 = (bf16[128,512]{1,0:T(8,128)(2,1)S(1)}, bf16[128,512]{1,0:T(8,128)(2,1)S(1)}, u32[]{:S(2)}, u32[]{:S(2)}) collective-permute-start(bf16[128,512]{1,0:T(8,128)(2,1)S(1)} %gather.2.refs_0_), channel_id=1, source_target_pairs={{0,8},{8,16},{16,24},{24,0},{1,9},{9,17},{17,25},{25,1},{2,10},{10... | collective-permute-start | bytes 393224 | tf_op jit(solution)/shard_map/ppermute | solution.py:458
  222.8 7.4 %collective-permute-start.11 = (bf16[128,512]{1,0:T(8,128)(2,1)S(1)}, bf16[128,512]{1,0:T(8,128)(2,1)S(1)}, u32[]{:S(2)}, u32[]{:S(2)}) collective-permute-start(bf16[128,512]{1,0:T(8,128)(2,1)S(1)} %gather.2.refs_0_), channel_id=1, source_target_pairs={{0,16},{8,24},{16,0},{24,8},{1,17},{9,25},{17,1},{25,9},{2,18},{10... | collective-permute-start | bytes 393224 | tf_op jit(solution)/shard_map/ppermute | solution.py:458
  226.5 4.1 %collective-permute-start.12 = (bf16[128,512]{1,0:T(8,128)(2,1)S(1)}, bf16[128,512]{1,0:T(8,128)(2,1)S(1)}, u32[]{:S(2)}, u32[]{:S(2)}) collective-permute-start(bf16[128,512]{1,0:T(8,128)(2,1)S(1)} %gather.2.refs_0_), channel_id=1, source_target_pairs={{0,24},{8,0},{16,8},{24,16},{1,25},{9,1},{17,9},{25,17},{2,26},{10... | collective-permute-start | bytes 393224 | tf_op jit(solution)/shard_map/ppermute | solution.py:458
  230.7 9.7 %collective-permute-start.13 = (bf16[1024,512]{1,0:T(8,128)(2,1)S(1)}, bf16[1024,512]{1,0:T(8,128)(2,1)S(1)}, u32[]{:S(2)}, u32[]{:S(2)}) collective-permute-start(bf16[1024,512]{1,0:T(8,128)(2,1)S(1)} %add.8.mine_ref), channel_id=1, source_target_pairs={{0,4},{4,0},{1,5},{5,1},{2,6},{6,2},{3,7},{7,3},{8,12},{12,8},{9,1... | collective-permute-start | bytes 3145736 | tf_op jit(solution)/shard_map/ppermute | solution.py:445
  235.8 3.0 %collective-permute-start.14 = (bf16[512,512]{1,0:T(8,128)(2,1)S(1)}, bf16[512,512]{1,0:T(8,128)(2,1)S(1)}, u32[]{:S(2)}, u32[]{:S(2)}) collective-permute-start(bf16[512,512]{1,0:T(8,128)(2,1)S(1)} %gather.3.after.mine_ref), channel_id=1, source_target_pairs={{0,4},{4,0},{1,5},{5,1},{2,6},{6,2},{3,7},{7,3},{8,12},{12,8},{9,1... | collective-permute-start | bytes 1572872 | tf_op jit(solution)/shard_map/ppermute | solution.py:445
  (2 other events, 1.3 us)
Sparse Core Ops, SparseCore 0:
  27.9 33.7 all-gather.1
  119.0 53.4 reduce-scatter.1

commit v4 on v3

--- a/solution.py
+++ b/solution.py
@@ -147,9 +147,32 @@
     return pl.program_id(0) == pl.num_programs(0) - 1
 
 
-def route_kernel(peers, group_size, capacity, stride, rot_ref, tok_ref, send_ref, slot_ref, wide_ref, place_ref):
+def late(columns, rows):
+    return [pltpu.VMEM((rows, columns), BF16), pltpu.SemaphoreType.DMA(())]
+
+
+def fetch(source, kept_ref, sem):
+    copy = pltpu.make_async_copy(source, kept_ref, sem)
+
+    @pl.when(is_first())
+    def _():
+        copy.start()
+
+    def arrive():
+        @pl.when(is_first())
+        def _():
+            copy.wait()
+
+    return arrive
+
+
+def route_kernel(
+    peers, group_size, capacity, stride, rot_ref, all_ref, send_ref, slot_ref, wide_ref, place_ref, tok_ref, sem
+):
     row_count = tok_ref.shape[0]
     step = BALL
+    arrive = fetch(all_ref, tok_ref, sem)
+    block = send_ref.shape[0]
 
     @pl.when(is_first())
     def _():
@@ -176,10 +199,11 @@
         place_ref[:, :LANES] = sums_high.astype(BF16)
         place_ref[:, LANES:] = sums_low.astype(BF16)
 
-    base = pl.program_id(0) * step
-    pick = onehot(iota((step, row_count), 0) + base == wide_ref[...])
+    arrive()
+    base = pl.program_id(0) * block
+    pick = onehot(iota((block, row_count), 0) + base == wide_ref[...])
     rows = mm(pick, tok_ref[...])
-    told = onehot(iota((step, peers), 0) + base == iota((step, peers), 1) * stride + capacity)
+    told = onehot(iota((block, peers), 0) + base == iota((block, peers), 1) * stride + capacity)
     extra = mm(told, place_ref[...])
     send_ref[:, : 2 * LANES] = (rows[:, : 2 * LANES] + extra).astype(BF16)
     send_ref[:, 2 * LANES :] = rows[:, 2 * LANES :].astype(BF16)
@@ -197,7 +221,7 @@
 
 
 def back_rows(arrived, rows_ref, out_ref):
-    slots, step = out_ref.shape[0], 256
+    slots, step = out_ref.shape[0], 2 * BALL
     row_count = rows_ref.shape[0]
     arrived_col = as_column(arrived.astype(F32)).astype(jnp.int32)
     moved = rows_ref[...]
@@ -220,26 +244,29 @@
 
 
 def moved_kernel(
-    head_size, peers, capacity, _, got_ref, wq_ref, nrm_ref, pk_ref, row_ref, out_ref, wide_ref, heads_ref
+    head_size, peers, capacity, _, got_ref, wq_ref, nrm_ref, pk_ref, row_ref, out_ref,
+    heads_ref, all_nrm_ref, all_pk_ref,
 ):
     slots = got_ref.shape[0]
+    row_count = heads_ref.shape[0]
     stride = slots // peers
 
     @pl.when(is_first())
     def _():
         told = onehot(iota((peers, slots), 1) == iota((peers, slots), 0) * stride + capacity)
         place = mm(told, got_ref[:, : 2 * LANES]).astype(BF16)
-        wide_ref[...] = arrived_row(place, stride)
         row_ref[...] = arrived_row(place, capacity)
-
-    base = pl.multiple_of(pl.program_id(0) * BALL, BALL)
-    pick = onehot(iota((BALL, slots), 0) + base == wide_ref[...])
-    residual = mm(pick, got_ref[...])
-    normed = (residual * row_scale(residual)).astype(BF16)
-    nrm_ref[...] = normed
-    packed = mm(normed, wq_ref[...]).astype(BF16)
+        pick = onehot(iota((row_count, slots), 0) == arrived_row(place, stride))
+        residual = mm(pick, got_ref[...])
+        normed = (residual * row_scale(residual)).astype(BF16)
+        all_nrm_ref[...] = normed
+        all_pk_ref[...] = mm(normed, wq_ref[...]).astype(BF16)
+
+    rows = pl.ds(pl.multiple_of(pl.program_id(0) * BALL, BALL), BALL)
+    nrm_ref[...] = all_nrm_ref[rows, :]
+    packed = all_pk_ref[rows, :]
     pk_ref[...] = packed
-    heads_ref[pl.ds(base, BALL), :] = ball_attend(packed, head_size)
+    heads_ref[rows, :] = ball_attend(packed, head_size)
 
     @pl.when(is_last())
     def _():
@@ -250,14 +277,14 @@
     tok_ref, local_ref, ret_ref, part_ref, slot_ref, proj_ref, up_ref, cot_ref, act_ref,
     mix_ref, mid_ref, sn_ref, gated_ref, pre_ref, gm_ref, gl_ref, send_ref, gh_ref,
 ):
-    width = tok_ref.shape[1]
+    count, width = tok_ref.shape
     half = width // 2
     slots = ret_ref.shape[0]
     chunks = up_ref.shape[0] // width
     rate = 0.7978845608028654
     cubic = 0.044715 * rate
     slot_col = as_column(part_ref[...].astype(F32)).astype(jnp.int32)
-    pick = onehot(iota((BALL, slots), 1) == slot_col)
+    pick = onehot(iota((count, slots), 1) == slot_col)
     moved = mm(pick, ret_ref[...]).astype(BF16)
     mixed = jnp.concatenate([local_ref[...], moved], axis=1)
     mix_ref[...] = mixed
@@ -267,7 +294,7 @@
     second_scale = row_scale(middle_f)
     normed = (middle_f * second_scale).astype(BF16)
     sn_ref[...] = normed
-    grad_second = jnp.zeros((BALL, width), F32)
+    grad_second = jnp.zeros((count, width), F32)
     pres = [mm(normed, up_ref[chunk * width : (chunk + 1) * width, :]) for chunk in range(chunks)]
     for chunk, pre in enumerate(pres):
         columns = slice(chunk * width, (chunk + 1) * width)
@@ -284,16 +311,17 @@
     gm_ref[...] = grad_middle
     grad_heads = mm_nt(grad_middle, proj_ref[...]).astype(BF16)
     gl_ref[...] = grad_heads[:, :half]
-    base = pl.multiple_of(pl.program_id(0) * BALL, BALL)
-    gh_ref[pl.ds(base, BALL), :] = grad_heads[:, half:]
+    base = pl.multiple_of(pl.program_id(0) * count, count)
+    gh_ref[pl.ds(base, count), :] = grad_heads[:, half:]
 
     @pl.when(is_last())
     def _():
         moved_grad = gh_ref[...]
         slot = slot_ref[...]
-        for start in range(0, slots, BALL):
-            pick = onehot(iota((BALL, slot.shape[1]), 0) + start == slot)
-            send_ref[start : start + BALL, :] = mm(pick, moved_grad).astype(BF16)
+        step = 2 * BALL
+        for start in range(0, slots, step):
+            pick = onehot(iota((step, slot.shape[1]), 0) + start == slot)
+            send_ref[start : start + step, :] = mm(pick, moved_grad).astype(BF16)
 
 
 def weights_kernel(
@@ -331,17 +359,24 @@
         gp_ref[...] = mm(flip(mix_ref[...]), gm_ref[...]).astype(BF16)
 
 
-def moved_back_kernel(head_size, _, got_ref, row_ref, pk_ref, wq_ref, gpk_ref, out_ref, first_ref):
+def moved_back_kernel(
+    head_size, _, got_ref, row_ref, pk_ref, wq_ref, gpk_ref, out_ref, first_ref, grad_ref, all_gpk_ref
+):
     slots = got_ref.shape[0]
-    base = pl.multiple_of(pl.program_id(0) * BALL, BALL)
-    pick = onehot(iota((BALL, slots), 0) + base == row_ref[...])
-    grad_out = mm(pick, got_ref[...]).astype(BF16)
-    grad_packed = ball_attend_back(pk_ref[...], grad_out, head_size)
+
+    @pl.when(is_first())
+    def _():
+        pick = onehot(iota((grad_ref.shape[0], slots), 0) == row_ref[...])
+        grad_ref[...] = mm(pick, got_ref[...]).astype(BF16)
+
+    rows = pl.ds(pl.multiple_of(pl.program_id(0) * BALL, BALL), BALL)
+    grad_packed = ball_attend_back(pk_ref[...], grad_ref[rows, :], head_size)
     gpk_ref[...] = grad_packed
-    first_ref[pl.ds(base, BALL), :] = mm_nt(grad_packed, wq_ref[...]).astype(BF16)
+    all_gpk_ref[rows, :] = grad_packed
 
     @pl.when(is_last())
     def _():
+        first_ref[...] = mm_nt(all_gpk_ref[...], wq_ref[...]).astype(BF16)
         back_rows(row_ref[...], first_ref, out_ref)
 
 
@@ -370,7 +405,7 @@
         out_ref[...] = sum_ref[pl.ds(pl.multiple_of(start, size), size), :]
 
 
-def add_kernel(after, *refs):
+def add_kernel(after, also, *refs):
     total = refs[0][...].astype(F32)
     for in_ref in refs[1:-1]:
         total = total + in_ref[...].astype(F32)
@@ -384,7 +419,7 @@
     return total.astype(BF16)
 
 
-def spread_kernel(after, also, in_ref, out_ref):
+def spread_kernel(after, in_ref, out_ref):
     total = add_parts(in_ref)
     for part in range(out_ref.shape[0]):
         out_ref[part] = total
@@ -481,9 +516,10 @@
     return joined
 
 
-def add(parts, after):
+def add(parts, after, also=None):
+    also = after if also is None else also
     (block,) = call(
-        add_kernel, 1, [(after, ANY)] + [whole_array(part) for part in parts],
+        add_kernel, 1, [(after, ANY), (also, ANY)] + [whole_array(part) for part in parts],
         [(shape(parts[0].shape), whole(*parts[0].shape))], name="add",
     )
     return block
@@ -511,10 +547,10 @@
     return block, halfway
 
 
-def sum_at_once(block, axes, after, also):
+def sum_at_once(block, axes, after):
     parts = share_of_sum(block, axes)
     (spread,) = call(
-        spread_kernel, 1, [(after, ANY), (also, ANY), whole_parts(parts)], [(shape(parts.shape), whole_parts(parts)[1])], name="add_spread",
+        spread_kernel, 1, [(after, ANY), whole_parts(parts)], [(shape(parts.shape), whole_parts(parts)[1])], name="add_spread",
     )
     told = lax.all_to_all(spread, axes, split_axis=0, concat_axis=0, tiled=True)
     return told.reshape(block.shape)
@@ -540,6 +576,7 @@
     wide_slots = peers * stride
     hidden = group_size * up_weight.shape[1]
     balls = rows // BALL
+    block = 2 * BALL
     core = lax.axis_index("core")
     flag = (core.astype(jnp.int32).reshape(1), FLAG)
     own_weight = jnp.where(core == 0, up_weight, down_weight)
@@ -547,11 +584,11 @@
     all_up = (all_weights, whole(hidden, width))
 
     send, slot = call(
-        bind(route_kernel, peers, group_size, capacity, stride), wide_slots // BALL,
-        [(rotation.reshape(1, rows), whole(1, rows)), (tokens, whole(rows, width))],
-        [(shape((wide_slots, width)), by_row(width)), (shape((1, rows), jnp.int32), whole(1, rows))],
-        scratch=[pltpu.VMEM((1, rows), jnp.int32), pltpu.VMEM((peers, 2 * LANES), BF16)],
-        flops=LONG, name="route",
+        bind(route_kernel, peers, group_size, capacity, stride), 2,
+        [(rotation.reshape(1, rows), whole(1, rows)), (tokens, ANY)],
+        [(shape((wide_slots, width)), by_row(width, wide_slots // 2)), (shape((1, rows), jnp.int32), whole(1, rows))],
+        scratch=[pltpu.VMEM((1, rows), jnp.int32), pltpu.VMEM((peers, 2 * LANES), BF16)] + late(width, rows),
+        flops=LONG, name="route", vmem=VMEM_BYTES,
     )
     got = exchange(send, peers)
     part = (slot, by_column(1, BALL))
@@ -570,7 +607,7 @@
             (shape((rows, width)), by_row(width)), (shape((rows, third)), by_row(third)),
             (shape((1, slots), jnp.int32), whole(1, slots)), (shape((slots, half)), whole(slots, half)),
         ],
-        scratch=[pltpu.VMEM((1, wide_slots), jnp.int32), pltpu.VMEM((rows, half), BF16)],
+        scratch=[pltpu.VMEM((rows, half), BF16), pltpu.VMEM((rows, width), BF16), pltpu.VMEM((rows, third), BF16)],
         flops=LONG, name="moved", vmem=VMEM_BYTES,
     )
     returned = exchange(outgoing, peers)
@@ -581,17 +618,17 @@
         name="grad_act",
     )
     mixed_heads, middle, second_normed, activated, grad_pre, grad_middle, grad_local, send_grad = call(
-        middle_kernel, balls,
+        middle_kernel, rows // block,
         [
-            (tokens, by_row(width)), (local_heads, by_row(half)), (returned, whole(slots, half)),
-            part, (slot, whole(1, rows)), (proj_weight, whole(width, width)), all_up,
-            (cotangent, by_row(width)), (grad_act, by_row(hidden)),
+            (tokens, by_row(width, block)), (local_heads, by_row(half, block)), (returned, whole(slots, half)),
+            (slot, by_column(1, block)), (slot, whole(1, rows)), (proj_weight, whole(width, width)), all_up,
+            (cotangent, by_row(width, block)), (grad_act, by_row(hidden, block)),
         ],
         [
-            (shape((rows, width)), by_row(width)), (shape((rows, width)), by_row(width)),
-            (shape((rows, width)), by_row(width)), (shape((rows, hidden)), by_row(hidden)),
-            (shape((rows, hidden)), by_row(hidden)), (shape((rows, width)), by_row(width)),
-            (shape((rows, half)), by_row(half)), (shape((slots, half)), whole(slots, half)),
+            (shape((rows, width)), by_row(width, block)), (shape((rows, width)), by_row(width, block)),
+            (shape((rows, width)), by_row(width, block)), (shape((rows, hidden)), by_row(hidden, block)),
+            (shape((rows, hidden)), by_row(hidden, block)), (shape((rows, width)), by_row(width, block)),
+            (shape((rows, half)), by_row(half, block)), (shape((slots, half)), whole(slots, half)),
         ],
         scratch=[pltpu.VMEM((rows, half), BF16)], flops=LONG, name="middle", vmem=VMEM_BYTES,
     )
@@ -631,7 +668,8 @@
         bind(moved_back_kernel, head_size), balls,
         [(output, ANY), (got_grad, whole(slots, half)), (arrived, whole(1, slots)), (moved_packed, by_row(third)), moved_weight],
         [(shape((rows, third)), by_row(third)), (shape((slots, width)), whole(slots, width))],
-        scratch=[pltpu.VMEM((rows, width), BF16)], flops=LONG, name="moved_back", vmem=VMEM_BYTES,
+        scratch=[pltpu.VMEM((rows, width), BF16), pltpu.VMEM((rows, half), BF16), pltpu.VMEM((rows, third), BF16)],
+        flops=LONG, name="moved_back", vmem=VMEM_BYTES,
     )
     grad_returned = exchange(grad_outgoing, peers)
     stacked = (shape((2 * width, width)), whole(2 * width, width))
@@ -641,22 +679,21 @@
         [stacked, stacked],
         scratch=[pltpu.VMEM((width, 2 * third + width), BF16)], name="moved_weights",
     )
+    pair = add([keep, swap_core(send)], grad_returned)
+    mlp_mine, halfway = sum_by_steps(mlp_part, ("x", "z"), pair)
     (grad_tokens,) = call(
         last_kernel, balls,
-        [(mlp_part, ANY), (tokens, by_row(width)), (grad_middle, by_row(width)), (first_local, by_row(width)), (grad_returned, whole(slots, width)), part],
+        [(halfway, ANY), (tokens, by_row(width)), (grad_middle, by_row(width)), (first_local, by_row(width)), (grad_returned, whole(slots, width)), part],
         [(shape((rows, width)), by_row(width))],
         flops=LONG, name="last",
     )
-
-    pair = add([keep, swap_core(send)], grad_returned)
-    mlp_mine, halfway = sum_by_steps(mlp_part, ("x", "z"), pair)
     mlp_other = swap_core(mlp_mine)
     grad_up, grad_down = call(
         finish_mlp_kernel, 1, [flag, whole_array(mlp_mine), whole_array(mlp_other)],
         [(shape((width, width), F32), whole(width, width)), (shape((width, width), F32), whole(width, width))],
         name="finish_mlp",
     )
-    mine = add([sum_at_once(pair, ("narrow", "x", "z"), grad_tokens, halfway)], mlp_mine)
+    mine = add([sum_at_once(pair, ("narrow", "x", "z"), halfway)], mlp_mine, grad_tokens)
     grad_qkv, grad_proj = call(
         finish_attention_kernel, 1, [flag, whole_array(mine), whole_array(swap_core(mine))],
         [(shape((width, 2 * third), F32), whole(width, 2 * third)), (shape((width, width), F32), whole(width, width))],

time: 251 us -> 244 us (0.972)
  Pallas kernels: 93.1 us -> 89.7 us
  starting transfers between devices: 69.4 us -> 66.2 us
    pallas_call x20, Pallas kernels: 93.1 us -> 89.7 us  [call(): pl.pallas_call(kernel, grid=(steps,), out_shape=[out for out, _ in outs],...]
    ppermute x12, starting transfers between devices: 20.6 us -> 17.9 us  [shift_by(): lax.ppermute(block, axis, [(place, (place + shift) % count) for place in...]
    unnamed x54 -> x48, local copies, waits for them, and re-layouts: 23.2 us -> 21.9 us
  transfers between devices with their start and end apart: 23 -> 23, of which waited for: 15 -> 13; matrix products, arithmetic and copies ran while one was open for 1% -> 1% of each run, Pallas kernels for 26% -> 26%
where the time goes in v4:
time: 244 us; the launch traced here: 243 us
  Pallas kernels  89.7 us (37%)
  starting transfers between devices  66.2 us (27%)
  waiting for transfers between devices  48.5 us (20%)
  local copies, waits for them, and re-layouts  21.9 us (9%)
  between operations  14.4 us (6%)
    pallas_call x20, Pallas kernels, call(): pl.pallas_call(kernel, grid=(steps,), out_shape=[out for out, _ in outs],...  89.7 us
    all_to_all x4, waiting for transfers between devices, exchange(): lax.all_to_all(sent, ('z', 'x', 'core'), split_axis=0, concat_axis=0, til...  26.3 us
    all_to_all x4, starting transfers between devices, exchange(): lax.all_to_all(sent, ('z', 'x', 'core'), split_axis=0, concat_axis=0, til...  25.9 us
    unnamed x48, local copies, waits for them, and re-layouts  21.9 us
    ppermute x12, starting transfers between devices, shift_by(): lax.ppermute(block, axis, [(place, (place + shift) % count) for place in...  17.9 us
    ppermute x12, waiting for transfers between devices, shift_by(): lax.ppermute(block, axis, [(place, (place + shift) % count) for place in...  15.4 us
    all_to_all x1, starting transfers between devices, share_of_sum(): return lax.all_to_all(parts, axes, split_axis=0, concat_axis=0, tiled=True)  7.85 us
    ppermute x3, starting transfers between devices, swap_core(): return lax.ppermute(block, 'core', [(0, 1), (1, 0)])  7.29 us
  transfers between devices with their start and end apart: 23, of which 13 were waited for; matrix products, arithmetic and copies ran while one was open for 1% of the time, Pallas kernels for 26%

profile of v4, /device:TPU:1, one launch (start us, length us, event | category | flops | bytes accessed | tf_op | source)
XLA Modules:
  0.0 242.7 jit_solution(5611520293365269486)
XLA Ops:
  7.2 5.4 %route.1 = (bf16[1792,512]{1,0:T(8,128)(2,1)}, s32[1,1024]{1,0:T(1,128)}) custom-call(s32[1,1024]{1,0:T(1,128)} %bitcast.26, bf16[1024,512]{1,0:T(8,128)(2,1)} %tok_ref.3), custom_call_target="tpu_custom_call" | custom-call | flops 99999997952 | tf_op jit(solution)/shard_map/route/pallas_call | solution.py:129
  12.6 9.6 %all-to-all-start = ((bf16[32,56,512]{2,1,0:T(8,128)(2,1)}), bf16[32,56,512]{2,1,0:T(8,128)(2,1)}, u32[]{:S(2)}, u32[]{:S(2)}) async-start(bf16[32,56,512]{2,1,0:T(8,128)(2,1)} %bitcast.20), calls=%async_computation | async-start | bytes 3670016 | tf_op jit(solution)/shard_map/all_to_all | solution.py:475
  22.3 2.0 broadcast_select_fusion
  24.3 4.3 %first_local.1 = (bf16[1024,512]{1,0:T(8,128)(2,1)S(1)}, bf16[1024,768]{1,0:T(8,128)(2,1)S(1)}, bf16[1024,256]{1,0:T(8,128)(2,1)S(1)}) custom-call(bf16[1024,512]{1,0:T(8,128)(2,1)S(1)} %copy-done.8, bf16[512,1536]{1,0:T(8,128)(2,1)S(1)} %copy-done.1), custom_call_target="tpu_custom_call" | custom-call | tf_op jit(solution)/shard_map/first_local/pallas_call | solution.py:129
  31.7 15.5 %all-to-all-done = bf16[32,56,512]{2,1,0:T(8,128)(2,1)} async-done(((bf16[32,56,512]{2,1,0:T(8,128)(2,1)}), bf16[32,56,512]{2,1,0:T(8,128)(2,1)}, u32[]{:S(2)}, u32[]{:S(2)}) %all-to-all-start) | async-done | bytes 1835040 | tf_op jit(solution)/shard_map/all_to_all | solution.py:475
  47.2 11.9 %moved.1 = (bf16[1024,512]{1,0:T(8,128)(2,1)}, bf16[1024,768]{1,0:T(8,128)(2,1)}, s32[1,1536]{1,0:T(1,128)}, bf16[1536,256]{1,0:T(8,128)(2,1)}) custom-call(bf16[1024,256]{1,0:T(8,128)(2,1)} %copy-done.19, bf16[1792,512]{1,0:T(8,128)(2,1)} %bitcast.2.refs_1_, bf16[512,1536]{1,0:T(8,128)(2,1)} %refs_3_.1), custom_call_target="tpu_custom_call" | custom-call | flops 99999997952 | tf_op jit(solution)/shard_map/moved/pallas_call | solution.py:129
  59.1 6.0 %all-to-all-start.1 = ((bf16[32,48,256]{2,1,0:T(8,128)(2,1)}), bf16[32,48,256]{2,1,0:T(8,128)(2,1)S(1)}, u32[]{:S(2)}, u32[]{:S(2)}) async-start(bf16[32,48,256]{2,1,0:T(8,128)(2,1)} %bitcast.25), calls=%async_computation.1 | async-start | bytes 1572864 | tf_op jit(solution)/shard_map/all_to_all | solution.py:475
  65.1 2.2 copy-done
  67.3 3.0 %grad_act.1.act_ref = bf16[1024,2048]{1,0:T(8,128)(2,1)S(1)} custom-call(bf16[1024,512]{1,0:T(8,128)(2,1)S(1)} %copy-done.4, bf16[4096,512]{1,0:T(8,128)(2,1)S(1)} %copy-done), custom_call_target="tpu_custom_call" | custom-call | tf_op jit(solution)/shard_map/grad_act/pallas_call | solution.py:129
  70.3 2.0 copy-done.2
  72.3 7.1 %all-to-all-done.1 = bf16[32,48,256]{2,1,0:T(8,128)(2,1)S(1)} async-done(((bf16[32,48,256]{2,1,0:T(8,128)(2,1)}), bf16[32,48,256]{2,1,0:T(8,128)(2,1)S(1)}, u32[]{:S(2)}, u32[]{:S(2)}) %all-to-all-start.1) | async-done | bytes 786464 | tf_op jit(solution)/shard_map/all_to_all | solution.py:475
  80.2 17.8 %middle.1 = (bf16[1024,512]{1,0:T(8,128)(2,1)}, bf16[1024,512]{1,0:T(8,128)(2,1)}, bf16[1024,512]{1,0:T(8,128)(2,1)}, bf16[1024,2048]{1,0:T(8,128)(2,1)}, bf16[1...) custom-call(bf16[1024,512]{1,0:T(8,128)(2,1)} %tok_ref.3, ...), custom_call_target="tpu_custom_call" | custom-call | flops 99999997952 | tf_op jit(solution)/shard_map/middle/pallas_call | solution.py:129
  98.0 4.2 %all-to-all-start.2 = ((bf16[32,48,256]{2,1,0:T(8,128)(2,1)}), bf16[32,48,256]{2,1,0:T(8,128)(2,1)S(1)}, u32[]{:S(2)}, u32[]{:S(2)}) async-start(bf16[32,48,256]{2,1,0:T(8,128)(2,1)} %bitcast.23), calls=%async_computation.2 | async-start | bytes 1572864 | tf_op jit(solution)/shard_map/all_to_all | solution.py:475
  102.5 12.7 %mlp_weights.1 = (bf16[1024,512]{1,0:T(8,128)(2,1)}, bf16[2,2048,512]{2,1,0:T(8,128)(2,1)}) custom-call(bf16[1024,512]{1,0:T(8,128)(2,1)} %get-tuple-element.48.mid_ref, bf16[1024,2048]{1,0:T(8,128)(2,1)} %get-tuple-element.49.gated_ref, bf16[4096,512]{1,0:T(8,128)(2,1)} %all-gather.2.cloned.1.call-done.down_ref.up_ref, bf16[1024,512]{1,0:T(8,128)(2,1)} %cot_ref.5, ...), custom_call_target="tpu_custom_call" | custom-call | tf_op jit(solution)/shard_map/mlp_weights/pallas_call | solution.py:129
  115.2 1.4 all-to-all-done.2
  117.4 11.3 %moved_back.1 = (bf16[1024,768]{1,0:T(8,128)(2,1)}, bf16[1536,512]{1,0:T(8,128)(2,1)}) custom-call(bf16[1024,512]{1,0:T(8,128)(2,1)} %get-tuple-element.38.refs_0_, bf16[1536,256]{1,0:T(8,128)(2,1)} %bitcast.22, s32[1,1536]{1,0:T(1,128)} %get-tuple-element.54.refs_2_, bf16[1024,768]{1,0:T(8,128)(2,1)} %get-tuple-element.55.refs_3_, bf16[512,1536]{1,0:T(8,128)(2,1)} %refs_3_.1), custom_call_target="tpu_custom_call" | custom-call | flops 99999997952 | tf_op jit(solution)/shard_map/moved_back/pallas_call | solution.py:129
  128.7 6.1 %all-to-all-start.3 = ((bf16[32,48,512]{2,1,0:T(8,128)(2,1)}), bf16[32,48,512]{2,1,0:T(8,128)(2,1)S(1)}, u32[]{:S(2)}, u32[]{:S(2)}) async-start(bf16[32,48,512]{2,1,0:T(8,128)(2,1)} %bitcast.21), calls=%async_computation.3 | async-start | bytes 3145728 | tf_op jit(solution)/shard_map/all_to_all | solution.py:475
  134.9 11.6 %local_back.1 = (f32[1024,512]{1,0:T(8,128)}, bf16[512,768]{1,0:T(8,128)(2,1)}, bf16[512,512]{1,0:T(8,128)(2,1)}) custom-call(bf16[1024,768]{1,0:T(8,128)(2,1)} %copy-done.6, bf16[1024,256]{1,0:T(8,128)(2,1)} %get-tuple-element.60.refs_1_, bf16[1024,512]{1,0:T(8,128)(2,1)} %copy-done.11, bf16[512,1536]{1,0:T(8,128)(2,1)} %refs_3_.1, ...), custom_call_target="tpu_custom_call" | custom-call | tf_op jit(solution)/shard_map/local_back/pallas_call | solution.py:129
  146.5 1.2 copy-done.12
  149.9 1.2 moved_weights.1
  152.3 2.4 %collective-permute-done.refs_1_ = bf16[1024,512]{1,0:T(8,128)(2,1)S(1)} collective-permute-done((bf16[1024,512]{1,0:T(8,128)(2,1)S(1)}, bf16[1024,512]{1,0:T(8,128)(2,1)S(1)}, u32[]{:S(2)}, u32[]{:S(2)}) %collective-permute-start) | collective-permute-done | bytes 1048608 | tf_op jit(solution)/shard_map/ppermute | solution.py:480
  154.8 2.3 all-to-all-done.3
  157.1 1.2 copy-done.14
  158.3 1.2 add.6.refs_0_.after.also
  159.5 7.8 %all-to-all-start.4 = ((bf16[64,16,512]{2,1,0:T(8,128)(2,1)}), bf16[64,16,512]{2,1,0:T(8,128)(2,1)S(1)}, u32[]{:S(2)}, u32[]{:S(2)}) async-start(bf16[64,16,512]{2,1,0:T(8,128)(2,1)} %bitcast.13), calls=%async_computation.5 | async-start | bytes 2097152 | tf_op jit(solution)/shard_map/all_to_all | solution.py:532
  167.4 1.4 reduce-scatter.2.cloned.1.call-done.refs_2_
  170.5 1.2 collective-permute-start.1
  171.7 2.4 collective-permute-start.2
  174.1 1.2 collective-permute-start.3
  175.3 8.7 %collective-permute-done.1.refs_3_ = bf16[128,512]{1,0:T(8,128)(2,1)S(1)} collective-permute-done((bf16[128,512]{1,0:T(8,128)(2,1)}, bf16[128,512]{1,0:T(8,128)(2,1)S(1)}, u32[]{:S(2)}, u32[]{:S(2)}) %collective-permute-start.1) | collective-permute-done | bytes 131104 | tf_op jit(solution)/shard_map/ppermute | solution.py:493
  184.0 2.7 %collective-permute-done.2.refs_4_ = bf16[128,512]{1,0:T(8,128)(2,1)S(1)} collective-permute-done((bf16[128,512]{1,0:T(8,128)(2,1)S(1)}, bf16[128,512]{1,0:T(8,128)(2,1)S(1)}, u32[]{:S(2)}, u32[]{:S(2)}) %collective-permute-start.2) | collective-permute-done | bytes 131104 | tf_op jit(solution)/shard_map/ppermute | solution.py:493
  186.8 1.3 collective-permute-start.4
  188.1 2.4 collective-permute-start.5
  190.5 1.2 collective-permute-start.6
  193.6 3.3 %collective-permute-start.8 = (bf16[32,512]{1,0:T(8,128)(2,1)S(1)}, bf16[32,512]{1,0:T(8,128)(2,1)S(1)}, u32[]{:S(2)}, u32[]{:S(2)}) collective-permute-start(bf16[32,512]{1,0:T(8,128)(2,1)S(1)} %add.7.refs_0_), channel_id=1, source_target_pairs={{0,64},{32,96},{64,0},{96,32},{1,65},{33,97},{65,1},{97,33},{2,66}... | collective-permute-start | bytes 98312 | tf_op jit(solution)/shard_map/ppermute | solution.py:493
  198.1 6.9 %all-to-all-start.5 = ((bf16[64,16,512]{2,1,0:T(8,128)(2,1)}), bf16[64,16,512]{2,1,0:T(8,128)(2,1)S(1)}, u32[]{:S(2)}, u32[]{:S(2)}) async-start(bf16[64,16,512]{2,1,0:T(8,128)(2,1)} %copy-done.3), calls=%async_computation.6 | async-start | bytes 2097152 | tf_op jit(solution)/shard_map/all_to_all | solution.py:555
  206.2 2.4 collective-permute-start.11
  208.6 1.2 collective-permute-start.12
  209.8 1.2 copy-done.9
  211.0 1.2 copy-done.10
  212.3 1.6 copy-done.18
  213.9 4.3 %last.1.also = bf16[1024,512]{1,0:T(8,128)(2,1)} custom-call(bf16[32,512]{1,0:T(8,128)(2,1)S(1)} %get-tuple-element.73._.refs_0_.after, bf16[1024,512]{1,0:T(8,128)(2,1)S(1)} %copy-done.9, bf16[1024,512]{1,0:T(8,128)(2,1)S(1)} %copy-done.10, f32[1024,512]{1,0:T(8,128)S(1)} %copy-done.18, bf16[1536,512]{1,0:T(8,128)(2,1)S(1)} %bitcast.17, ...), custom_call_target="tpu_custom_call" | custom-call | flops 99999997952 | tf_op jit(solution)/shard_map/last/pallas_call | solution.py:129
  218.9 1.7 collective-permute-done.11.refs_2_
  220.7 1.2 copy-done.7
  222.0 7.0 %collective-permute-start.13 = (bf16[1024,512]{1,0:T(8,128)(2,1)S(1)}, bf16[1024,512]{1,0:T(8,128)(2,1)S(1)}, u32[]{:S(2)}, u32[]{:S(2)}) collective-permute-start(bf16[1024,512]{1,0:T(8,128)(2,1)S(1)} %add.8.mine_ref), channel_id=1, source_target_pairs={{0,4},{4,0},{1,5},{5,1},{2,6},{6,2},{3,7},{7,3},{8,12},{12,8},{9,1... | collective-permute-start | bytes 3145736 | tf_op jit(solution)/shard_map/ppermute | solution.py:480
  229.1 2.9 %collective-permute-done.14.other_ref = bf16[512,512]{1,0:T(8,128)(2,1)S(1)} collective-permute-done((bf16[512,512]{1,0:T(8,128)(2,1)S(1)}, bf16[512,512]{1,0:T(8,128)(2,1)S(1)}, u32[]{:S(2)}, u32[]{:S(2)}) %collective-permute-start.14) | collective-permute-done | bytes 524320 | tf_op jit(solution)/shard_map/ppermute | solution.py:480
  232.0 1.6 finish_mlp.1
  233.6 2.2 finish_attention.1
  (69 shorter events, 15.7 us)
Async XLA Ops:
  12.6 9.7 %copy-start.23 = (bf16[512,512]{1,0:T(8,128)(2,1)S(1)}, bf16[512,512]{1,0:T(8,128)(2,1)}, u32[]{:S(2)}) copy-start(bf16[512,512]{1,0:T(8,128)(2,1)} %param.11) | copy-start | bytes 1572868
  12.6 11.7 %copy-start.8 = (bf16[1024,512]{1,0:T(8,128)(2,1)S(1)}, bf16[1024,512]{1,0:T(8,128)(2,1)}, u32[]{:S(2)}) copy-start(bf16[1024,512]{1,0:T(8,128)(2,1)} %tok_ref.3) | copy-start | bytes 3145732
  12.6 34.6 %all-to-all-start = ((bf16[32,56,512]{2,1,0:T(8,128)(2,1)}), bf16[32,56,512]{2,1,0:T(8,128)(2,1)}, u32[]{:S(2)}, u32[]{:S(2)}) async-start(bf16[32,56,512]{2,1,0:T(8,128)(2,1)} %bitcast.20), calls=%async_computation | async-start | bytes 3670016 | tf_op jit(solution)/shard_map/all_to_all | solution.py:475
  22.2 2.1 copy-start.1
  22.2 42.8 %all-gather.2.cloned.1.call-start = ((), (), s32[]{:S(2)}) async-start(), calls=%async_computation.7 | async-start | bytes 4718592 | tf_op jit(solution)/shard_map/all_gather | solution.py:583
  28.7 1.2 copy-start.6
  29.9 1.0 copy-start.11
  30.9 0.8 copy-start.19
  59.1 6.0 %copy-start.4 = (bf16[1024,512]{1,0:T(8,128)(2,1)S(1)}, bf16[1024,512]{1,0:T(8,128)(2,1)}, u32[]{:S(2)}) copy-start(bf16[1024,512]{1,0:T(8,128)(2,1)} %cot_ref.5) | copy-start | bytes 3145732
  59.1 20.3 %all-to-all-start.1 = ((bf16[32,48,256]{2,1,0:T(8,128)(2,1)}), bf16[32,48,256]{2,1,0:T(8,128)(2,1)S(1)}, u32[]{:S(2)}, u32[]{:S(2)}) async-start(bf16[32,48,256]{2,1,0:T(8,128)(2,1)} %bitcast.25), calls=%async_computation.1 | async-start | bytes 1572864 | tf_op jit(solution)/shard_map/all_to_all | solution.py:475
  65.1 2.2 copy-start
  70.3 2.0 copy-start.2
  79.4 0.9 copy-start.22
  98.0 18.5 %all-to-all-start.2 = ((bf16[32,48,256]{2,1,0:T(8,128)(2,1)}), bf16[32,48,256]{2,1,0:T(8,128)(2,1)S(1)}, u32[]{:S(2)}, u32[]{:S(2)}) async-start(bf16[32,48,256]{2,1,0:T(8,128)(2,1)} %bitcast.23), calls=%async_computation.2 | async-start | bytes 1572864 | tf_op jit(solution)/shard_map/all_to_all | solution.py:475
  102.2 66.6 %reduce-scatter.2.cloned.1.call-start = ((), (), s32[]{:S(2)}) async-start(), calls=%async_computation.8 | async-start | bytes 4718592 | tf_op jit(solution)/shard_map/reduce_scatter | solution.py:651
  116.5 0.9 copy-start.21
  128.7 28.3 %all-to-all-start.3 = ((bf16[32,48,512]{2,1,0:T(8,128)(2,1)}), bf16[32,48,512]{2,1,0:T(8,128)(2,1)S(1)}, u32[]{:S(2)}, u32[]{:S(2)}) async-start(bf16[32,48,512]{2,1,0:T(8,128)(2,1)} %bitcast.21), calls=%async_computation.3 | async-start | bytes 3145728 | tf_op jit(solution)/shard_map/all_to_all | solution.py:475
  134.9 11.6 %copy-start.5 = (bf16[1024,768]{1,0:T(8,128)(2,1)S(1)}, bf16[1024,768]{1,0:T(8,128)(2,1)}, u32[]{:S(2)}) copy-start(bf16[1024,768]{1,0:T(8,128)(2,1)} %get-tuple-element.58.gpk_ref) | copy-start | bytes 4718596
  146.5 1.2 copy-start.12
  147.7 1.1 copy-start.15
  148.9 1.1 copy-start.16
  151.1 1.0 copy-start.13
  152.1 2.7 %collective-permute-start = (bf16[1024,512]{1,0:T(8,128)(2,1)S(1)}, bf16[1024,512]{1,0:T(8,128)(2,1)S(1)}, u32[]{:S(2)}, u32[]{:S(2)}) collective-permute-start(bf16[1024,512]{1,0:T(8,128)(2,1)S(1)} %get-tuple-element.67), channel_id=1, source_target_pairs={{0,4},{4,0},{1,5},{5,1},{2,6},{6,2},{3,7},{7,3},{8,12},{12,8},{9,1... | collective-permute-start | bytes 3145736 | tf_op jit(solution)/shard_map/ppermute | solution.py:480
  157.1 1.2 copy-start.14
  159.5 37.4 %all-to-all-start.4 = ((bf16[64,16,512]{2,1,0:T(8,128)(2,1)}), bf16[64,16,512]{2,1,0:T(8,128)(2,1)S(1)}, u32[]{:S(2)}, u32[]{:S(2)}) async-start(bf16[64,16,512]{2,1,0:T(8,128)(2,1)} %bitcast.13), calls=%async_computation.5 | async-start | bytes 2097152 | tf_op jit(solution)/shard_map/all_to_all | solution.py:532
  168.8 1.0 copy-start.17
  170.5 13.5 %collective-permute-start.1 = (bf16[128,512]{1,0:T(8,128)(2,1)}, bf16[128,512]{1,0:T(8,128)(2,1)S(1)}, u32[]{:S(2)}, u32[]{:S(2)}) collective-permute-start(bf16[128,512]{1,0:T(8,128)(2,1)} %get-tuple-element.70), channel_id=1, source_target_pairs={{0,8},{8,16},{16,24},{24,0},{1,9},{9,17},{17,25},{25,1},{2,10},{10... | collective-permute-start | bytes 393224 | tf_op jit(solution)/shard_map/ppermute | solution.py:493
  171.7 15.0 %collective-permute-start.2 = (bf16[128,512]{1,0:T(8,128)(2,1)S(1)}, bf16[128,512]{1,0:T(8,128)(2,1)S(1)}, u32[]{:S(2)}, u32[]{:S(2)}) collective-permute-start(bf16[128,512]{1,0:T(8,128)(2,1)S(1)} %get-tuple-element.71), channel_id=1, source_target_pairs={{0,16},{8,24},{16,0},{24,8},{1,17},{9,25},{17,1},{25,9},{2,18},{10... | collective-permute-start | bytes 393224 | tf_op jit(solution)/shard_map/ppermute | solution.py:493
  174.1 12.6 %collective-permute-start.3 = (bf16[128,512]{1,0:T(8,128)(2,1)S(1)}, bf16[128,512]{1,0:T(8,128)(2,1)S(1)}, u32[]{:S(2)}, u32[]{:S(2)}) collective-permute-start(bf16[128,512]{1,0:T(8,128)(2,1)S(1)} %get-tuple-element.72), channel_id=1, source_target_pairs={{0,24},{8,0},{16,8},{24,16},{1,25},{9,1},{17,9},{25,17},{2,26},{10... | collective-permute-start | bytes 393224 | tf_op jit(solution)/shard_map/ppermute | solution.py:493
  186.8 4.8 %collective-permute-start.4 = (bf16[32,512]{1,0:T(8,128)(2,1)S(1)}, bf16[32,512]{1,0:T(8,128)(2,1)S(1)}, u32[]{:S(2)}, u32[]{:S(2)}) collective-permute-start(bf16[32,512]{1,0:T(8,128)(2,1)S(1)} %get-tuple-element.75), channel_id=1, source_target_pairs={{0,32},{32,64},{64,96},{96,0},{1,33},{33,65},{65,97},{97,1},{2,34}... | collective-permute-start | bytes 98312 | tf_op jit(solution)/shard_map/ppermute | solution.py:493
  188.1 4.3 %collective-permute-start.5 = (bf16[32,512]{1,0:T(8,128)(2,1)S(1)}, bf16[32,512]{1,0:T(8,128)(2,1)S(1)}, u32[]{:S(2)}, u32[]{:S(2)}) collective-permute-start(bf16[32,512]{1,0:T(8,128)(2,1)S(1)} %get-tuple-element.76), channel_id=1, source_target_pairs={{0,64},{32,96},{64,0},{96,32},{1,65},{33,97},{65,1},{97,33},{2,66}... | collective-permute-start | bytes 98312 | tf_op jit(solution)/shard_map/ppermute | solution.py:493
  190.5 2.8 %collective-permute-start.6 = (bf16[32,512]{1,0:T(8,128)(2,1)S(1)}, bf16[32,512]{1,0:T(8,128)(2,1)S(1)}, u32[]{:S(2)}, u32[]{:S(2)}) collective-permute-start(bf16[32,512]{1,0:T(8,128)(2,1)S(1)} %get-tuple-element.77), channel_id=1, source_target_pairs={{0,96},{32,0},{64,32},{96,64},{1,97},{33,1},{65,33},{97,65},{2,98}... | collective-permute-start | bytes 98312 | tf_op jit(solution)/shard_map/ppermute | solution.py:493
  193.2 16.6 %copy-start.20 = (s32[1,1024]{1,0:T(1,128)S(1)}, s32[1,1024]{1,0:T(1,128)}, u32[]{:S(2)}) copy-start(s32[1,1024]{1,0:T(1,128)} %get-tuple-element.47.part_ref.slot_ref) | copy-start | bytes 12292
  193.3 11.8 %collective-permute-start.7 = (bf16[32,512]{1,0:T(8,128)(2,1)S(1)}, bf16[32,512]{1,0:T(8,128)(2,1)S(1)}, u32[]{:S(2)}, u32[]{:S(2)}) collective-permute-start(bf16[32,512]{1,0:T(8,128)(2,1)S(1)} %add.7.refs_0_), channel_id=1, source_target_pairs={{0,32},{32,64},{64,96},{96,0},{1,33},{33,65},{65,97},{97,1},{2,34}... | collective-permute-start | bytes 98312 | tf_op jit(solution)/shard_map/ppermute | solution.py:493
  193.6 11.5 %collective-permute-start.8 = (bf16[32,512]{1,0:T(8,128)(2,1)S(1)}, bf16[32,512]{1,0:T(8,128)(2,1)S(1)}, u32[]{:S(2)}, u32[]{:S(2)}) collective-permute-start(bf16[32,512]{1,0:T(8,128)(2,1)S(1)} %add.7.refs_0_), channel_id=1, source_target_pairs={{0,64},{32,96},{64,0},{96,32},{1,65},{33,97},{65,1},{97,33},{2,66}... | collective-permute-start | bytes 98312 | tf_op jit(solution)/shard_map/ppermute | solution.py:493
  196.9 8.2 %collective-permute-start.9 = (bf16[32,512]{1,0:T(8,128)(2,1)S(1)}, bf16[32,512]{1,0:T(8,128)(2,1)S(1)}, u32[]{:S(2)}, u32[]{:S(2)}) collective-permute-start(bf16[32,512]{1,0:T(8,128)(2,1)S(1)} %add.7.refs_0_), channel_id=1, source_target_pairs={{0,96},{32,0},{64,32},{96,64},{1,97},{33,1},{65,33},{97,65},{2,98}... | collective-permute-start | bytes 98312 | tf_op jit(solution)/shard_map/ppermute | solution.py:493
  197.2 1.0 copy-start.3
  198.1 22.6 %all-to-all-start.5 = ((bf16[64,16,512]{2,1,0:T(8,128)(2,1)}), bf16[64,16,512]{2,1,0:T(8,128)(2,1)S(1)}, u32[]{:S(2)}, u32[]{:S(2)}) async-start(bf16[64,16,512]{2,1,0:T(8,128)(2,1)} %copy-done.3), calls=%async_computation.6 | async-start | bytes 2097152 | tf_op jit(solution)/shard_map/all_to_all | solution.py:555
  205.2 13.8 %collective-permute-start.10 = (bf16[128,512]{1,0:T(8,128)(2,1)S(1)}, bf16[128,512]{1,0:T(8,128)(2,1)S(1)}, u32[]{:S(2)}, u32[]{:S(2)}) collective-permute-start(bf16[128,512]{1,0:T(8,128)(2,1)S(1)} %gather.2.refs_0_), channel_id=1, source_target_pairs={{0,8},{8,16},{16,24},{24,0},{1,9},{9,17},{17,25},{25,1},{2,10},{10... | collective-permute-start | bytes 393224 | tf_op jit(solution)/shard_map/ppermute | solution.py:493
  206.2 14.4 %collective-permute-start.11 = (bf16[128,512]{1,0:T(8,128)(2,1)S(1)}, bf16[128,512]{1,0:T(8,128)(2,1)S(1)}, u32[]{:S(2)}, u32[]{:S(2)}) collective-permute-start(bf16[128,512]{1,0:T(8,128)(2,1)S(1)} %gather.2.refs_0_), channel_id=1, source_target_pairs={{0,16},{8,24},{16,0},{24,8},{1,17},{9,25},{17,1},{25,9},{2,18},{10... | collective-permute-start | bytes 393224 | tf_op jit(solution)/shard_map/ppermute | solution.py:493
  208.6 12.0 %collective-permute-start.12 = (bf16[128,512]{1,0:T(8,128)(2,1)S(1)}, bf16[128,512]{1,0:T(8,128)(2,1)S(1)}, u32[]{:S(2)}, u32[]{:S(2)}) collective-permute-start(bf16[128,512]{1,0:T(8,128)(2,1)S(1)} %gather.2.refs_0_), channel_id=1, source_target_pairs={{0,24},{8,0},{16,8},{24,16},{1,25},{9,1},{17,9},{25,17},{2,26},{10... | collective-permute-start | bytes 393224 | tf_op jit(solution)/shard_map/ppermute | solution.py:493
  209.8 1.2 copy-start.9
  211.0 1.2 copy-start.10
  212.3 1.6 copy-start.18
  220.7 1.2 copy-start.7
  222.0 11.6 %collective-permute-start.13 = (bf16[1024,512]{1,0:T(8,128)(2,1)S(1)}, bf16[1024,512]{1,0:T(8,128)(2,1)S(1)}, u32[]{:S(2)}, u32[]{:S(2)}) collective-permute-start(bf16[1024,512]{1,0:T(8,128)(2,1)S(1)} %add.8.mine_ref), channel_id=1, source_target_pairs={{0,4},{4,0},{1,5},{5,1},{2,6},{6,2},{3,7},{7,3},{8,12},{12,8},{9,1... | collective-permute-start | bytes 3145736 | tf_op jit(solution)/shard_map/ppermute | solution.py:480
  229.0 3.0 %collective-permute-start.14 = (bf16[512,512]{1,0:T(8,128)(2,1)S(1)}, bf16[512,512]{1,0:T(8,128)(2,1)S(1)}, u32[]{:S(2)}, u32[]{:S(2)}) collective-permute-start(bf16[512,512]{1,0:T(8,128)(2,1)S(1)} %gather.3.after.mine_ref), channel_id=1, source_target_pairs={{0,4},{4,0},{1,5},{5,1},{2,6},{6,2},{3,7},{7,3},{8,12},{12,8},{9,1... | collective-permute-start | bytes 1572872 | tf_op jit(solution)/shard_map/ppermute | solution.py:480
Sparse Core Ops, SparseCore 0:
  25.3 33.7 all-gather.1
  115.3 53.4 reduce-scatter.1

commit v5 on v4

--- a/solution.py
+++ b/solution.py
@@ -335,8 +335,8 @@
         sum_ref[...] = mid_ref[...].astype(F32)
 
     gated = gated_ref[...]
-    both_ref[0] = mm(sn_t_ref[...], pre_ref[...]).astype(BF16)
-    both_ref[1] = mm(cot_t_ref[...], gated).astype(BF16)
+    both_ref[0, 0] = mm(sn_t_ref[...], pre_ref[...]).astype(BF16)
+    both_ref[0, 1] = mm(cot_t_ref[...], gated).astype(BF16)
     sum_ref[...] += mm(gated, down_ref[...])
 
     @pl.when(is_last())
@@ -643,13 +643,13 @@
         ],
         [
             (shape((rows, width)), whole(rows, width)),
-            (shape((2, hidden, width)), pl.BlockSpec((2, width, width), lambda step: (0, step, 0))),
+            (shape((group_size, 2, width, width)), pl.BlockSpec((1, 2, width, width), lambda step: (step, 0, 0, 0))),
         ],
         scratch=[pltpu.VMEM((width, rows), BF16), pltpu.VMEM((width, rows), BF16), pltpu.VMEM((rows, width), F32)],
         name="mlp_weights", vmem=VMEM_BYTES,
     )
     mlp_part = lax.psum_scatter(
-        mlp_both.reshape(2 * hidden, width), ("core", "narrow"), scatter_dimension=0, tiled=True
+        mlp_both.reshape(2 * hidden, width), ("narrow", "core"), scatter_dimension=0, tiled=True
     )
     first_local, qkv_local, proj_local = call(
         bind(local_back_kernel, head_size), balls,

time: 244 us -> 244 us (level)
  transfers between devices with their start and end apart: 23 -> 23, of which waited for: 13 -> 12; matrix products, arithmetic and copies ran while one was open for 1% -> 1% of each run, Pallas kernels for 26% -> 26%
where the time goes in v5:
time: 244 us; the launch traced here: 243 us
  Pallas kernels  89.8 us (37%)
  starting transfers between devices  66 us (27%)
  waiting for transfers between devices  49.1 us (20%)
  local copies, waits for them, and re-layouts  21.9 us (9%)
  between operations  14.4 us (6%)
    pallas_call x20, Pallas kernels, call(): pl.pallas_call(kernel, grid=(steps,), out_shape=[out for out, _ in outs],...  89.8 us
    all_to_all x4, waiting for transfers between devices, exchange(): lax.all_to_all(sent, ('z', 'x', 'core'), split_axis=0, concat_axis=0, til...  26.2 us
    all_to_all x4, starting transfers between devices, exchange(): lax.all_to_all(sent, ('z', 'x', 'core'), split_axis=0, concat_axis=0, til...  25.9 us
    unnamed x48, local copies, waits for them, and re-layouts  21.9 us
    ppermute x12, starting transfers between devices, shift_by(): lax.ppermute(block, axis, [(place, (place + shift) % count) for place in...  18 us
    ppermute x12, waiting for transfers between devices, shift_by(): lax.ppermute(block, axis, [(place, (place + shift) % count) for place in...  17.4 us
    all_to_all x1, starting transfers between devices, share_of_sum(): return lax.all_to_all(parts, axes, split_axis=0, concat_axis=0, tiled=True)  7.94 us
    all_to_all x1, starting transfers between devices, sum_at_once(): told = lax.all_to_all(spread, axes, split_axis=0, concat_axis=0, tiled=True)  6.94 us
  transfers between devices with their start and end apart: 23, of which 12 were waited for; matrix products, arithmetic and copies ran while one was open for 1% of the time, Pallas kernels for 26%

profile of v5, /device:TPU:1, one launch (start us, length us, event | category | flops | bytes accessed | tf_op | source)
XLA Modules:
  0.0 243.1 jit_solution(14258002217462339149)
XLA Ops:
  7.2 5.4 %route.1 = (bf16[1792,512]{1,0:T(8,128)(2,1)}, s32[1,1024]{1,0:T(1,128)}) custom-call(s32[1,1024]{1,0:T(1,128)} %bitcast.26, bf16[1024,512]{1,0:T(8,128)(2,1)} %tok_ref.3), custom_call_target="tpu_custom_call" | custom-call | flops 99999997952 | tf_op jit(solution)/shard_map/route/pallas_call | solution.py:129
  12.6 9.6 %all-to-all-start = ((bf16[32,56,512]{2,1,0:T(8,128)(2,1)}), bf16[32,56,512]{2,1,0:T(8,128)(2,1)}, u32[]{:S(2)}, u32[]{:S(2)}) async-start(bf16[32,56,512]{2,1,0:T(8,128)(2,1)} %bitcast.20), calls=%async_computation | async-start | bytes 3670016 | tf_op jit(solution)/shard_map/all_to_all | solution.py:475
  22.3 2.0 broadcast_select_fusion
  24.3 4.3 %first_local.1 = (bf16[1024,512]{1,0:T(8,128)(2,1)S(1)}, bf16[1024,768]{1,0:T(8,128)(2,1)S(1)}, bf16[1024,256]{1,0:T(8,128)(2,1)S(1)}) custom-call(bf16[1024,512]{1,0:T(8,128)(2,1)S(1)} %copy-done.8, bf16[512,1536]{1,0:T(8,128)(2,1)S(1)} %copy-done.1), custom_call_target="tpu_custom_call" | custom-call | tf_op jit(solution)/shard_map/first_local/pallas_call | solution.py:129
  28.7 1.2 copy-done.6
  31.7 15.5 %all-to-all-done = bf16[32,56,512]{2,1,0:T(8,128)(2,1)} async-done(((bf16[32,56,512]{2,1,0:T(8,128)(2,1)}), bf16[32,56,512]{2,1,0:T(8,128)(2,1)}, u32[]{:S(2)}, u32[]{:S(2)}) %all-to-all-start) | async-done | bytes 1835040 | tf_op jit(solution)/shard_map/all_to_all | solution.py:475
  47.2 11.9 %moved.1 = (bf16[1024,512]{1,0:T(8,128)(2,1)}, bf16[1024,768]{1,0:T(8,128)(2,1)}, s32[1,1536]{1,0:T(1,128)}, bf16[1536,256]{1,0:T(8,128)(2,1)}) custom-call(bf16[1024,256]{1,0:T(8,128)(2,1)} %copy-done.19, bf16[1792,512]{1,0:T(8,128)(2,1)} %bitcast.2.refs_1_, bf16[512,1536]{1,0:T(8,128)(2,1)} %refs_3_.1), custom_call_target="tpu_custom_call" | custom-call | flops 99999997952 | tf_op jit(solution)/shard_map/moved/pallas_call | solution.py:129
  59.1 6.0 %all-to-all-start.1 = ((bf16[32,48,256]{2,1,0:T(8,128)(2,1)}), bf16[32,48,256]{2,1,0:T(8,128)(2,1)S(1)}, u32[]{:S(2)}, u32[]{:S(2)}) async-start(bf16[32,48,256]{2,1,0:T(8,128)(2,1)} %bitcast.25), calls=%async_computation.1 | async-start | bytes 1572864 | tf_op jit(solution)/shard_map/all_to_all | solution.py:475
  65.1 2.2 copy-done
  67.3 3.0 %grad_act.1.act_ref = bf16[1024,2048]{1,0:T(8,128)(2,1)S(1)} custom-call(bf16[1024,512]{1,0:T(8,128)(2,1)S(1)} %copy-done.4, bf16[4096,512]{1,0:T(8,128)(2,1)S(1)} %copy-done), custom_call_target="tpu_custom_call" | custom-call | tf_op jit(solution)/shard_map/grad_act/pallas_call | solution.py:129
  70.3 2.0 copy-done.2
  72.3 7.1 %all-to-all-done.1 = bf16[32,48,256]{2,1,0:T(8,128)(2,1)S(1)} async-done(((bf16[32,48,256]{2,1,0:T(8,128)(2,1)}), bf16[32,48,256]{2,1,0:T(8,128)(2,1)S(1)}, u32[]{:S(2)}, u32[]{:S(2)}) %all-to-all-start.1) | async-done | bytes 786464 | tf_op jit(solution)/shard_map/all_to_all | solution.py:475
  80.2 17.8 %middle.1 = (bf16[1024,512]{1,0:T(8,128)(2,1)}, bf16[1024,512]{1,0:T(8,128)(2,1)}, bf16[1024,512]{1,0:T(8,128)(2,1)}, bf16[1024,2048]{1,0:T(8,128)(2,1)}, bf16[1...) custom-call(bf16[1024,512]{1,0:T(8,128)(2,1)} %tok_ref.3, ...), custom_call_target="tpu_custom_call" | custom-call | flops 99999997952 | tf_op jit(solution)/shard_map/middle/pallas_call | solution.py:129
  98.0 4.2 %all-to-all-start.2 = ((bf16[32,48,256]{2,1,0:T(8,128)(2,1)}), bf16[32,48,256]{2,1,0:T(8,128)(2,1)S(1)}, u32[]{:S(2)}, u32[]{:S(2)}) async-start(bf16[32,48,256]{2,1,0:T(8,128)(2,1)} %bitcast.23), calls=%async_computation.2 | async-start | bytes 1572864 | tf_op jit(solution)/shard_map/all_to_all | solution.py:475
  102.5 12.7 %mlp_weights.1 = (bf16[1024,512]{1,0:T(8,128)(2,1)}, bf16[4,2,512,512]{3,2,1,0:T(8,128)(2,1)}) custom-call(bf16[1024,512]{1,0:T(8,128)(2,1)} %get-tuple-element.48.mid_ref, bf16[1024,2048]{1,0:T(8,128)(2,1)} %get-tuple-element.49.gated_ref, bf16[4096,512]{1,0:T(8,128)(2,1)} %all-gather.2.cloned.1.call-done.down_ref.up_ref, bf16[1024,512]{1,0:T(8,128)(2,1)} %cot_ref.5, ...), custom_call_target="tpu_custom_call" | custom-call | tf_op jit(solution)/shard_map/mlp_weights/pallas_call | solution.py:129
  115.2 1.3 all-to-all-done.2
  117.4 11.3 %moved_back.1 = (bf16[1024,768]{1,0:T(8,128)(2,1)}, bf16[1536,512]{1,0:T(8,128)(2,1)}) custom-call(bf16[1024,512]{1,0:T(8,128)(2,1)} %get-tuple-element.38.refs_0_, bf16[1536,256]{1,0:T(8,128)(2,1)} %bitcast.22, s32[1,1536]{1,0:T(1,128)} %get-tuple-element.54.refs_2_, bf16[1024,768]{1,0:T(8,128)(2,1)} %get-tuple-element.55.refs_3_, bf16[512,1536]{1,0:T(8,128)(2,1)} %refs_3_.1), custom_call_target="tpu_custom_call" | custom-call | flops 99999997952 | tf_op jit(solution)/shard_map/moved_back/pallas_call | solution.py:129
  128.7 6.2 %all-to-all-start.3 = ((bf16[32,48,512]{2,1,0:T(8,128)(2,1)}), bf16[32,48,512]{2,1,0:T(8,128)(2,1)S(1)}, u32[]{:S(2)}, u32[]{:S(2)}) async-start(bf16[32,48,512]{2,1,0:T(8,128)(2,1)} %bitcast.21), calls=%async_computation.3 | async-start | bytes 3145728 | tf_op jit(solution)/shard_map/all_to_all | solution.py:475
  134.9 11.6 %local_back.1 = (f32[1024,512]{1,0:T(8,128)}, bf16[512,768]{1,0:T(8,128)(2,1)}, bf16[512,512]{1,0:T(8,128)(2,1)}) custom-call(bf16[1024,768]{1,0:T(8,128)(2,1)} %copy-done.6, bf16[1024,256]{1,0:T(8,128)(2,1)} %get-tuple-element.60.refs_1_, bf16[1024,512]{1,0:T(8,128)(2,1)} %copy-done.11, bf16[512,1536]{1,0:T(8,128)(2,1)} %refs_3_.1, ...), custom_call_target="tpu_custom_call" | custom-call | tf_op jit(solution)/shard_map/local_back/pallas_call | solution.py:129
  146.5 1.2 copy-done.12
  150.0 1.2 moved_weights.1
  152.3 2.5 %collective-permute-done.refs_1_ = bf16[1024,512]{1,0:T(8,128)(2,1)S(1)} collective-permute-done((bf16[1024,512]{1,0:T(8,128)(2,1)S(1)}, bf16[1024,512]{1,0:T(8,128)(2,1)S(1)}, u32[]{:S(2)}, u32[]{:S(2)}) %collective-permute-start) | collective-permute-done | bytes 1048608 | tf_op jit(solution)/shard_map/ppermute | solution.py:480
  154.8 2.3 all-to-all-done.3
  157.1 1.2 copy-done.14
  158.3 1.2 add.6.refs_0_.after.also
  159.5 7.9 %all-to-all-start.4 = ((bf16[64,16,512]{2,1,0:T(8,128)(2,1)}), bf16[64,16,512]{2,1,0:T(8,128)(2,1)S(1)}, u32[]{:S(2)}, u32[]{:S(2)}) async-start(bf16[64,16,512]{2,1,0:T(8,128)(2,1)} %bitcast.13), calls=%async_computation.5 | async-start | bytes 2097152 | tf_op jit(solution)/shard_map/all_to_all | solution.py:532
  170.3 2.4 collective-permute-start.2
  172.7 1.2 collective-permute-start.3
  173.9 10.2 %collective-permute-done.1.refs_3_ = bf16[128,512]{1,0:T(8,128)(2,1)S(1)} collective-permute-done((bf16[128,512]{1,0:T(8,128)(2,1)}, bf16[128,512]{1,0:T(8,128)(2,1)S(1)}, u32[]{:S(2)}, u32[]{:S(2)}) %collective-permute-start.1) | collective-permute-done | bytes 131104 | tf_op jit(solution)/shard_map/ppermute | solution.py:493
  184.1 2.7 %collective-permute-done.2.refs_4_ = bf16[128,512]{1,0:T(8,128)(2,1)S(1)} collective-permute-done((bf16[128,512]{1,0:T(8,128)(2,1)S(1)}, bf16[128,512]{1,0:T(8,128)(2,1)S(1)}, u32[]{:S(2)}, u32[]{:S(2)}) %collective-permute-start.2) | collective-permute-done | bytes 131104 | tf_op jit(solution)/shard_map/ppermute | solution.py:493
  187.0 1.3 collective-permute-start.4
  188.2 2.4 collective-permute-start.5
  190.6 1.2 collective-permute-start.6
  193.8 3.6 %collective-permute-start.8 = (bf16[32,512]{1,0:T(8,128)(2,1)S(1)}, bf16[32,512]{1,0:T(8,128)(2,1)S(1)}, u32[]{:S(2)}, u32[]{:S(2)}) collective-permute-start(bf16[32,512]{1,0:T(8,128)(2,1)S(1)} %add.7.refs_0_), channel_id=1, source_target_pairs={{0,64},{32,96},{64,0},{96,32},{1,65},{33,97},{65,1},{97,33},{2,66}... | collective-permute-start | bytes 98312 | tf_op jit(solution)/shard_map/ppermute | solution.py:493
  198.6 6.9 %all-to-all-start.5 = ((bf16[64,16,512]{2,1,0:T(8,128)(2,1)}), bf16[64,16,512]{2,1,0:T(8,128)(2,1)S(1)}, u32[]{:S(2)}, u32[]{:S(2)}) async-start(bf16[64,16,512]{2,1,0:T(8,128)(2,1)} %copy-done.3), calls=%async_computation.6 | async-start | bytes 2097152 | tf_op jit(solution)/shard_map/all_to_all | solution.py:555
  206.7 2.4 collective-permute-start.11
  209.1 1.2 collective-permute-start.12
  210.3 1.2 copy-done.9
  211.5 1.2 copy-done.10
  212.7 1.6 copy-done.18
  214.3 4.3 %last.1.also = bf16[1024,512]{1,0:T(8,128)(2,1)} custom-call(bf16[32,512]{1,0:T(8,128)(2,1)S(1)} %get-tuple-element.73._.refs_0_.after, bf16[1024,512]{1,0:T(8,128)(2,1)S(1)} %copy-done.9, bf16[1024,512]{1,0:T(8,128)(2,1)S(1)} %copy-done.10, f32[1024,512]{1,0:T(8,128)S(1)} %copy-done.18, bf16[1536,512]{1,0:T(8,128)(2,1)S(1)} %bitcast.17, ...), custom_call_target="tpu_custom_call" | custom-call | flops 99999997952 | tf_op jit(solution)/shard_map/last/pallas_call | solution.py:129
  218.6 1.2 collective-permute-done.10.refs_1_
  219.8 1.6 collective-permute-done.11.refs_2_
  221.5 1.2 copy-done.7
  222.8 6.6 %collective-permute-start.13 = (bf16[1024,512]{1,0:T(8,128)(2,1)S(1)}, bf16[1024,512]{1,0:T(8,128)(2,1)S(1)}, u32[]{:S(2)}, u32[]{:S(2)}) collective-permute-start(bf16[1024,512]{1,0:T(8,128)(2,1)S(1)} %add.8.mine_ref), channel_id=1, source_target_pairs={{0,4},{4,0},{1,5},{5,1},{2,6},{6,2},{3,7},{7,3},{8,12},{12,8},{9,1... | collective-permute-start | bytes 3145736 | tf_op jit(solution)/shard_map/ppermute | solution.py:480
  229.5 2.9 %collective-permute-done.14.other_ref = bf16[512,512]{1,0:T(8,128)(2,1)S(1)} collective-permute-done((bf16[512,512]{1,0:T(8,128)(2,1)S(1)}, bf16[512,512]{1,0:T(8,128)(2,1)S(1)}, u32[]{:S(2)}, u32[]{:S(2)}) %collective-permute-start.14) | collective-permute-done | bytes 524320 | tf_op jit(solution)/shard_map/ppermute | solution.py:480
  232.5 1.6 finish_mlp.1
  234.1 2.2 finish_attention.1
  (69 shorter events, 14.7 us)
Async XLA Ops:
  12.6 9.7 %copy-start.23 = (bf16[512,512]{1,0:T(8,128)(2,1)S(1)}, bf16[512,512]{1,0:T(8,128)(2,1)}, u32[]{:S(2)}) copy-start(bf16[512,512]{1,0:T(8,128)(2,1)} %param.11) | copy-start | bytes 1572868
  12.6 11.7 %copy-start.8 = (bf16[1024,512]{1,0:T(8,128)(2,1)S(1)}, bf16[1024,512]{1,0:T(8,128)(2,1)}, u32[]{:S(2)}) copy-start(bf16[1024,512]{1,0:T(8,128)(2,1)} %tok_ref.3) | copy-start | bytes 3145732
  12.6 34.6 %all-to-all-start = ((bf16[32,56,512]{2,1,0:T(8,128)(2,1)}), bf16[32,56,512]{2,1,0:T(8,128)(2,1)}, u32[]{:S(2)}, u32[]{:S(2)}) async-start(bf16[32,56,512]{2,1,0:T(8,128)(2,1)} %bitcast.20), calls=%async_computation | async-start | bytes 3670016 | tf_op jit(solution)/shard_map/all_to_all | solution.py:475
  22.2 2.1 copy-start.1
  22.2 42.8 %all-gather.2.cloned.1.call-start = ((), (), s32[]{:S(2)}) async-start(), calls=%async_computation.7 | async-start | bytes 4718592 | tf_op jit(solution)/shard_map/all_gather | solution.py:583
  28.7 1.2 copy-start.6
  29.9 1.0 copy-start.11
  30.9 0.8 copy-start.19
  59.1 6.0 %copy-start.4 = (bf16[1024,512]{1,0:T(8,128)(2,1)S(1)}, bf16[1024,512]{1,0:T(8,128)(2,1)}, u32[]{:S(2)}) copy-start(bf16[1024,512]{1,0:T(8,128)(2,1)} %cot_ref.5) | copy-start | bytes 3145732
  59.1 20.3 %all-to-all-start.1 = ((bf16[32,48,256]{2,1,0:T(8,128)(2,1)}), bf16[32,48,256]{2,1,0:T(8,128)(2,1)S(1)}, u32[]{:S(2)}, u32[]{:S(2)}) async-start(bf16[32,48,256]{2,1,0:T(8,128)(2,1)} %bitcast.25), calls=%async_computation.1 | async-start | bytes 1572864 | tf_op jit(solution)/shard_map/all_to_all | solution.py:475
  65.1 2.2 copy-start
  70.3 2.0 copy-start.2
  79.4 0.9 copy-start.22
  98.0 18.5 %all-to-all-start.2 = ((bf16[32,48,256]{2,1,0:T(8,128)(2,1)}), bf16[32,48,256]{2,1,0:T(8,128)(2,1)S(1)}, u32[]{:S(2)}, u32[]{:S(2)}) async-start(bf16[32,48,256]{2,1,0:T(8,128)(2,1)} %bitcast.23), calls=%async_computation.2 | async-start | bytes 1572864 | tf_op jit(solution)/shard_map/all_to_all | solution.py:475
  102.2 65.3 %reduce-scatter.2.cloned.1.call-start = ((), (), s32[]{:S(2)}) async-start(), calls=%async_computation.8 | async-start | bytes 4718592 | tf_op jit(solution)/shard_map/reduce_scatter | solution.py:651
  116.5 0.9 copy-start.21
  128.7 28.4 %all-to-all-start.3 = ((bf16[32,48,512]{2,1,0:T(8,128)(2,1)}), bf16[32,48,512]{2,1,0:T(8,128)(2,1)S(1)}, u32[]{:S(2)}, u32[]{:S(2)}) async-start(bf16[32,48,512]{2,1,0:T(8,128)(2,1)} %bitcast.21), calls=%async_computation.3 | async-start | bytes 3145728 | tf_op jit(solution)/shard_map/all_to_all | solution.py:475
  134.9 11.6 %copy-start.5 = (bf16[1024,768]{1,0:T(8,128)(2,1)S(1)}, bf16[1024,768]{1,0:T(8,128)(2,1)}, u32[]{:S(2)}) copy-start(bf16[1024,768]{1,0:T(8,128)(2,1)} %get-tuple-element.58.gpk_ref) | copy-start | bytes 4718596
  146.5 1.3 copy-start.12
  147.8 1.1 copy-start.15
  148.9 1.1 copy-start.16
  151.2 1.0 copy-start.13
  152.1 2.7 %collective-permute-start = (bf16[1024,512]{1,0:T(8,128)(2,1)S(1)}, bf16[1024,512]{1,0:T(8,128)(2,1)S(1)}, u32[]{:S(2)}, u32[]{:S(2)}) collective-permute-start(bf16[1024,512]{1,0:T(8,128)(2,1)S(1)} %get-tuple-element.67), channel_id=1, source_target_pairs={{0,4},{4,0},{1,5},{5,1},{2,6},{6,2},{3,7},{7,3},{8,12},{12,8},{9,1... | collective-permute-start | bytes 3145736 | tf_op jit(solution)/shard_map/ppermute | solution.py:480
  157.1 1.2 copy-start.14
  159.5 37.8 %all-to-all-start.4 = ((bf16[64,16,512]{2,1,0:T(8,128)(2,1)}), bf16[64,16,512]{2,1,0:T(8,128)(2,1)S(1)}, u32[]{:S(2)}, u32[]{:S(2)}) async-start(bf16[64,16,512]{2,1,0:T(8,128)(2,1)} %bitcast.13), calls=%async_computation.5 | async-start | bytes 2097152 | tf_op jit(solution)/shard_map/all_to_all | solution.py:532
  167.5 1.0 copy-start.17
  169.3 14.8 %collective-permute-start.1 = (bf16[128,512]{1,0:T(8,128)(2,1)}, bf16[128,512]{1,0:T(8,128)(2,1)S(1)}, u32[]{:S(2)}, u32[]{:S(2)}) collective-permute-start(bf16[128,512]{1,0:T(8,128)(2,1)} %get-tuple-element.70), channel_id=1, source_target_pairs={{0,8},{8,16},{16,24},{24,0},{1,9},{9,17},{17,25},{25,1},{2,10},{10... | collective-permute-start | bytes 393224 | tf_op jit(solution)/shard_map/ppermute | solution.py:493
  170.3 16.5 %collective-permute-start.2 = (bf16[128,512]{1,0:T(8,128)(2,1)S(1)}, bf16[128,512]{1,0:T(8,128)(2,1)S(1)}, u32[]{:S(2)}, u32[]{:S(2)}) collective-permute-start(bf16[128,512]{1,0:T(8,128)(2,1)S(1)} %get-tuple-element.71), channel_id=1, source_target_pairs={{0,16},{8,24},{16,0},{24,8},{1,17},{9,25},{17,1},{25,9},{2,18},{10... | collective-permute-start | bytes 393224 | tf_op jit(solution)/shard_map/ppermute | solution.py:493
  172.7 14.2 %collective-permute-start.3 = (bf16[128,512]{1,0:T(8,128)(2,1)S(1)}, bf16[128,512]{1,0:T(8,128)(2,1)S(1)}, u32[]{:S(2)}, u32[]{:S(2)}) collective-permute-start(bf16[128,512]{1,0:T(8,128)(2,1)S(1)} %get-tuple-element.72), channel_id=1, source_target_pairs={{0,24},{8,0},{16,8},{24,16},{1,25},{9,1},{17,9},{25,17},{2,26},{10... | collective-permute-start | bytes 393224 | tf_op jit(solution)/shard_map/ppermute | solution.py:493
  187.0 4.8 %collective-permute-start.4 = (bf16[32,512]{1,0:T(8,128)(2,1)S(1)}, bf16[32,512]{1,0:T(8,128)(2,1)S(1)}, u32[]{:S(2)}, u32[]{:S(2)}) collective-permute-start(bf16[32,512]{1,0:T(8,128)(2,1)S(1)} %get-tuple-element.75), channel_id=1, source_target_pairs={{0,32},{32,64},{64,96},{96,0},{1,33},{33,65},{65,97},{97,1},{2,34}... | collective-permute-start | bytes 98312 | tf_op jit(solution)/shard_map/ppermute | solution.py:493
  188.2 4.3 %collective-permute-start.5 = (bf16[32,512]{1,0:T(8,128)(2,1)S(1)}, bf16[32,512]{1,0:T(8,128)(2,1)S(1)}, u32[]{:S(2)}, u32[]{:S(2)}) collective-permute-start(bf16[32,512]{1,0:T(8,128)(2,1)S(1)} %get-tuple-element.76), channel_id=1, source_target_pairs={{0,64},{32,96},{64,0},{96,32},{1,65},{33,97},{65,1},{97,33},{2,66}... | collective-permute-start | bytes 98312 | tf_op jit(solution)/shard_map/ppermute | solution.py:493
  190.6 2.8 %collective-permute-start.6 = (bf16[32,512]{1,0:T(8,128)(2,1)S(1)}, bf16[32,512]{1,0:T(8,128)(2,1)S(1)}, u32[]{:S(2)}, u32[]{:S(2)}) collective-permute-start(bf16[32,512]{1,0:T(8,128)(2,1)S(1)} %get-tuple-element.77), channel_id=1, source_target_pairs={{0,96},{32,0},{64,32},{96,64},{1,97},{33,1},{65,33},{97,65},{2,98}... | collective-permute-start | bytes 98312 | tf_op jit(solution)/shard_map/ppermute | solution.py:493
  193.4 16.9 %copy-start.20 = (s32[1,1024]{1,0:T(1,128)S(1)}, s32[1,1024]{1,0:T(1,128)}, u32[]{:S(2)}) copy-start(s32[1,1024]{1,0:T(1,128)} %get-tuple-element.47.part_ref.slot_ref) | copy-start | bytes 12292
  193.4 12.1 %collective-permute-start.7 = (bf16[32,512]{1,0:T(8,128)(2,1)S(1)}, bf16[32,512]{1,0:T(8,128)(2,1)S(1)}, u32[]{:S(2)}, u32[]{:S(2)}) collective-permute-start(bf16[32,512]{1,0:T(8,128)(2,1)S(1)} %add.7.refs_0_), channel_id=1, source_target_pairs={{0,32},{32,64},{64,96},{96,0},{1,33},{33,65},{65,97},{97,1},{2,34}... | collective-permute-start | bytes 98312 | tf_op jit(solution)/shard_map/ppermute | solution.py:493
  193.8 11.8 %collective-permute-start.8 = (bf16[32,512]{1,0:T(8,128)(2,1)S(1)}, bf16[32,512]{1,0:T(8,128)(2,1)S(1)}, u32[]{:S(2)}, u32[]{:S(2)}) collective-permute-start(bf16[32,512]{1,0:T(8,128)(2,1)S(1)} %add.7.refs_0_), channel_id=1, source_target_pairs={{0,64},{32,96},{64,0},{96,32},{1,65},{33,97},{65,1},{97,33},{2,66}... | collective-permute-start | bytes 98312 | tf_op jit(solution)/shard_map/ppermute | solution.py:493
  197.3 8.2 %collective-permute-start.9 = (bf16[32,512]{1,0:T(8,128)(2,1)S(1)}, bf16[32,512]{1,0:T(8,128)(2,1)S(1)}, u32[]{:S(2)}, u32[]{:S(2)}) collective-permute-start(bf16[32,512]{1,0:T(8,128)(2,1)S(1)} %add.7.refs_0_), channel_id=1, source_target_pairs={{0,96},{32,0},{64,32},{96,64},{1,97},{33,1},{65,33},{97,65},{2,98}... | collective-permute-start | bytes 98312 | tf_op jit(solution)/shard_map/ppermute | solution.py:493
  197.6 1.0 copy-start.3
  198.6 22.9 %all-to-all-start.5 = ((bf16[64,16,512]{2,1,0:T(8,128)(2,1)}), bf16[64,16,512]{2,1,0:T(8,128)(2,1)S(1)}, u32[]{:S(2)}, u32[]{:S(2)}) async-start(bf16[64,16,512]{2,1,0:T(8,128)(2,1)} %copy-done.3), calls=%async_computation.6 | async-start | bytes 2097152 | tf_op jit(solution)/shard_map/all_to_all | solution.py:555
  205.6 14.2 %collective-permute-start.10 = (bf16[128,512]{1,0:T(8,128)(2,1)S(1)}, bf16[128,512]{1,0:T(8,128)(2,1)S(1)}, u32[]{:S(2)}, u32[]{:S(2)}) collective-permute-start(bf16[128,512]{1,0:T(8,128)(2,1)S(1)} %gather.2.refs_0_), channel_id=1, source_target_pairs={{0,8},{8,16},{16,24},{24,0},{1,9},{9,17},{17,25},{25,1},{2,10},{10... | collective-permute-start | bytes 393224 | tf_op jit(solution)/shard_map/ppermute | solution.py:493
  206.7 14.8 %collective-permute-start.11 = (bf16[128,512]{1,0:T(8,128)(2,1)S(1)}, bf16[128,512]{1,0:T(8,128)(2,1)S(1)}, u32[]{:S(2)}, u32[]{:S(2)}) collective-permute-start(bf16[128,512]{1,0:T(8,128)(2,1)S(1)} %gather.2.refs_0_), channel_id=1, source_target_pairs={{0,16},{8,24},{16,0},{24,8},{1,17},{9,25},{17,1},{25,9},{2,18},{10... | collective-permute-start | bytes 393224 | tf_op jit(solution)/shard_map/ppermute | solution.py:493
  209.1 12.4 %collective-permute-start.12 = (bf16[128,512]{1,0:T(8,128)(2,1)S(1)}, bf16[128,512]{1,0:T(8,128)(2,1)S(1)}, u32[]{:S(2)}, u32[]{:S(2)}) collective-permute-start(bf16[128,512]{1,0:T(8,128)(2,1)S(1)} %gather.2.refs_0_), channel_id=1, source_target_pairs={{0,24},{8,0},{16,8},{24,16},{1,25},{9,1},{17,9},{25,17},{2,26},{10... | collective-permute-start | bytes 393224 | tf_op jit(solution)/shard_map/ppermute | solution.py:493
  210.3 1.2 copy-start.9
  211.5 1.2 copy-start.10
  212.7 1.6 copy-start.18
  221.5 1.2 copy-start.7
  222.8 11.3 %collective-permute-start.13 = (bf16[1024,512]{1,0:T(8,128)(2,1)S(1)}, bf16[1024,512]{1,0:T(8,128)(2,1)S(1)}, u32[]{:S(2)}, u32[]{:S(2)}) collective-permute-start(bf16[1024,512]{1,0:T(8,128)(2,1)S(1)} %add.8.mine_ref), channel_id=1, source_target_pairs={{0,4},{4,0},{1,5},{5,1},{2,6},{6,2},{3,7},{7,3},{8,12},{12,8},{9,1... | collective-permute-start | bytes 3145736 | tf_op jit(solution)/shard_map/ppermute | solution.py:480
  229.4 3.0 %collective-permute-start.14 = (bf16[512,512]{1,0:T(8,128)(2,1)S(1)}, bf16[512,512]{1,0:T(8,128)(2,1)S(1)}, u32[]{:S(2)}, u32[]{:S(2)}) collective-permute-start(bf16[512,512]{1,0:T(8,128)(2,1)S(1)} %gather.3.after.mine_ref), channel_id=1, source_target_pairs={{0,4},{4,0},{1,5},{5,1},{2,6},{6,2},{3,7},{7,3},{8,12},{12,8},{9,1... | collective-permute-start | bytes 1572872 | tf_op jit(solution)/shard_map/ppermute | solution.py:480
Sparse Core Ops, SparseCore 0:
  25.3 33.7 all-gather.1
  115.3 36.3 reduce-scatter.1

commit v6 on v5

--- a/solution.py
+++ b/solution.py
@@ -419,7 +419,7 @@
     return total.astype(BF16)
 
 
-def spread_kernel(after, in_ref, out_ref):
+def spread_kernel(after, also, in_ref, out_ref):
     total = add_parts(in_ref)
     for part in range(out_ref.shape[0]):
         out_ref[part] = total
@@ -538,19 +538,21 @@
 
 def sum_by_steps(block, axes, after):
     parts = [block]
+    begun = None
     for axis in axes:
         parts = add_split(parts, axis, after)
-    halfway = parts[0]
+        begun = parts[0] if begun is None else begun
+    halfway = parts[1]
     block = add(parts, after)
     for axis in reversed(axes):
         block = gather(block, axis)
-    return block, halfway
-
-
-def sum_at_once(block, axes, after):
+    return block, begun, halfway
+
+
+def sum_at_once(block, axes, after, also):
     parts = share_of_sum(block, axes)
     (spread,) = call(
-        spread_kernel, 1, [(after, ANY), whole_parts(parts)], [(shape(parts.shape), whole_parts(parts)[1])], name="add_spread",
+        spread_kernel, 1, [(after, ANY), (also, ANY), whole_parts(parts)], [(shape(parts.shape), whole_parts(parts)[1])], name="add_spread",
     )
     told = lax.all_to_all(spread, axes, split_axis=0, concat_axis=0, tiled=True)
     return told.reshape(block.shape)
@@ -680,10 +682,10 @@
         scratch=[pltpu.VMEM((width, 2 * third + width), BF16)], name="moved_weights",
     )
     pair = add([keep, swap_core(send)], grad_returned)
-    mlp_mine, halfway = sum_by_steps(mlp_part, ("x", "z"), pair)
+    mlp_mine, begun, halfway = sum_by_steps(mlp_part, ("x", "z"), pair)
     (grad_tokens,) = call(
         last_kernel, balls,
-        [(halfway, ANY), (tokens, by_row(width)), (grad_middle, by_row(width)), (first_local, by_row(width)), (grad_returned, whole(slots, width)), part],
+        [(begun, ANY), (tokens, by_row(width)), (grad_middle, by_row(width)), (first_local, by_row(width)), (grad_returned, whole(slots, width)), part],
         [(shape((rows, width)), by_row(width))],
         flops=LONG, name="last",
     )
@@ -693,7 +695,7 @@
         [(shape((width, width), F32), whole(width, width)), (shape((width, width), F32), whole(width, width))],
         name="finish_mlp",
     )
-    mine = add([sum_at_once(pair, ("narrow", "x", "z"), halfway)], mlp_mine, grad_tokens)
+    mine = add([sum_at_once(pair, ("narrow", "x", "z"), halfway, grad_tokens)], mlp_mine)
     grad_qkv, grad_proj = call(
         finish_attention_kernel, 1, [flag, whole_array(mine), whole_array(swap_core(mine))],
         [(shape((width, 2 * third), F32), whole(width, 2 * third)), (shape((width, width), F32), whole(width, width))],

time: 244 us -> 247 us (1.012)
  waiting for transfers between devices: 49.1 us -> 52.5 us
    all_to_all x1, waiting for transfers between devices: 0.01 us -> 7.3 us  [share_of_sum(): return lax.all_to_all(parts, axes, split_axis=0, concat_axis=0, tiled=True)]
    ppermute x3, starting transfers between devices: 6.93 us -> 2.94 us  [swap_core(): return lax.ppermute(block, 'core', [(0, 1), (1, 0)])]
    ppermute x12, starting transfers between devices: 18 us -> 21 us  [shift_by(): lax.ppermute(block, axis, [(place, (place + shift) % count) for place in...]
    ppermute x12, waiting for transfers between devices: 17.4 us -> 14.5 us  [shift_by(): lax.ppermute(block, axis, [(place, (place + shift) % count) for place in...]
    unnamed x48 -> x46, local copies, waits for them, and re-layouts: 21.9 us -> 20.9 us
  transfers between devices with their start and end apart: 23 -> 23, of which waited for: 12 -> 15; matrix products, arithmetic and copies ran while one was open for 1% -> 1% of each run, Pallas kernels for 26% -> 26%
where the time goes in v6:
time: 247 us; the launch traced here: 246 us
  Pallas kernels  91.7 us (37%)
  starting transfers between devices  64.6 us (26%)
  waiting for transfers between devices  52.5 us (21%)
  local copies, waits for them, and re-layouts  20.9 us (8%)
  between operations  14.3 us (6%)
    pallas_call x20, Pallas kernels, call(): pl.pallas_call(kernel, grid=(steps,), out_shape=[out for out, _ in outs],...  91.7 us
    all_to_all x4, starting transfers between devices, exchange(): lax.all_to_all(sent, ('z', 'x', 'core'), split_axis=0, concat_axis=0, til...  25.9 us
    all_to_all x4, waiting for transfers between devices, exchange(): lax.all_to_all(sent, ('z', 'x', 'core'), split_axis=0, concat_axis=0, til...  25 us
    ppermute x12, starting transfers between devices, shift_by(): lax.ppermute(block, axis, [(place, (place + shift) % count) for place in...  21 us
    unnamed x46, local copies, waits for them, and re-layouts  20.9 us
    ppermute x12, waiting for transfers between devices, shift_by(): lax.ppermute(block, axis, [(place, (place + shift) % count) for place in...  14.5 us
    all_to_all x1, starting transfers between devices, share_of_sum(): return lax.all_to_all(parts, axes, split_axis=0, concat_axis=0, tiled=True)  8.55 us
    all_to_all x1, waiting for transfers between devices, share_of_sum(): return lax.all_to_all(parts, axes, split_axis=0, concat_axis=0, tiled=True)  7.3 us
  transfers between devices with their start and end apart: 23, of which 15 were waited for; matrix products, arithmetic and copies ran while one was open for 1% of the time, Pallas kernels for 26%

profile of v6, /device:TPU:1, one launch (start us, length us, event | category | flops | bytes accessed | tf_op | source)
XLA Modules:
  0.0 246.0 jit_solution(5169565643676384822)
XLA Ops:
  7.2 5.4 %route.1 = (bf16[1792,512]{1,0:T(8,128)(2,1)}, s32[1,1024]{1,0:T(1,128)}) custom-call(s32[1,1024]{1,0:T(1,128)} %bitcast.26, bf16[1024,512]{1,0:T(8,128)(2,1)} %tok_ref.3), custom_call_target="tpu_custom_call" | custom-call | flops 99999997952 | tf_op jit(solution)/shard_map/route/pallas_call | solution.py:129
  12.6 9.6 %all-to-all-start = ((bf16[32,56,512]{2,1,0:T(8,128)(2,1)}), bf16[32,56,512]{2,1,0:T(8,128)(2,1)}, u32[]{:S(2)}, u32[]{:S(2)}) async-start(bf16[32,56,512]{2,1,0:T(8,128)(2,1)} %bitcast.20), calls=%async_computation | async-start | bytes 3670016 | tf_op jit(solution)/shard_map/all_to_all | solution.py:475
  22.3 2.0 broadcast_select_fusion
  24.3 4.3 %first_local.1 = (bf16[1024,512]{1,0:T(8,128)(2,1)S(1)}, bf16[1024,768]{1,0:T(8,128)(2,1)S(1)}, bf16[1024,256]{1,0:T(8,128)(2,1)S(1)}) custom-call(bf16[1024,512]{1,0:T(8,128)(2,1)S(1)} %copy-done.7, bf16[512,1536]{1,0:T(8,128)(2,1)S(1)} %copy-done.1), custom_call_target="tpu_custom_call" | custom-call | tf_op jit(solution)/shard_map/first_local/pallas_call | solution.py:129
  28.7 1.2 copy-done.5
  31.7 15.5 %all-to-all-done = bf16[32,56,512]{2,1,0:T(8,128)(2,1)} async-done(((bf16[32,56,512]{2,1,0:T(8,128)(2,1)}), bf16[32,56,512]{2,1,0:T(8,128)(2,1)}, u32[]{:S(2)}, u32[]{:S(2)}) %all-to-all-start) | async-done | bytes 1835040 | tf_op jit(solution)/shard_map/all_to_all | solution.py:475
  47.2 11.9 %moved.1 = (bf16[1024,512]{1,0:T(8,128)(2,1)}, bf16[1024,768]{1,0:T(8,128)(2,1)}, s32[1,1536]{1,0:T(1,128)}, bf16[1536,256]{1,0:T(8,128)(2,1)}) custom-call(bf16[1024,256]{1,0:T(8,128)(2,1)} %copy-done.18, bf16[1792,512]{1,0:T(8,128)(2,1)} %bitcast.2.refs_1_, bf16[512,1536]{1,0:T(8,128)(2,1)} %refs_3_.1), custom_call_target="tpu_custom_call" | custom-call | flops 99999997952 | tf_op jit(solution)/shard_map/moved/pallas_call | solution.py:129
  59.1 6.0 %all-to-all-start.1 = ((bf16[32,48,256]{2,1,0:T(8,128)(2,1)}), bf16[32,48,256]{2,1,0:T(8,128)(2,1)S(1)}, u32[]{:S(2)}, u32[]{:S(2)}) async-start(bf16[32,48,256]{2,1,0:T(8,128)(2,1)} %bitcast.25), calls=%async_computation.1 | async-start | bytes 1572864 | tf_op jit(solution)/shard_map/all_to_all | solution.py:475
  65.1 2.2 copy-done
  67.3 3.0 %grad_act.1.act_ref = bf16[1024,2048]{1,0:T(8,128)(2,1)S(1)} custom-call(bf16[1024,512]{1,0:T(8,128)(2,1)S(1)} %copy-done.3, bf16[4096,512]{1,0:T(8,128)(2,1)S(1)} %copy-done), custom_call_target="tpu_custom_call" | custom-call | tf_op jit(solution)/shard_map/grad_act/pallas_call | solution.py:129
  70.3 2.0 copy-done.2
  72.3 7.1 %all-to-all-done.1 = bf16[32,48,256]{2,1,0:T(8,128)(2,1)S(1)} async-done(((bf16[32,48,256]{2,1,0:T(8,128)(2,1)}), bf16[32,48,256]{2,1,0:T(8,128)(2,1)S(1)}, u32[]{:S(2)}, u32[]{:S(2)}) %all-to-all-start.1) | async-done | bytes 786464 | tf_op jit(solution)/shard_map/all_to_all | solution.py:475
  80.2 17.8 %middle.1 = (bf16[1024,512]{1,0:T(8,128)(2,1)}, bf16[1024,512]{1,0:T(8,128)(2,1)}, bf16[1024,512]{1,0:T(8,128)(2,1)}, bf16[1024,2048]{1,0:T(8,128)(2,1)}, bf16[1...) custom-call(bf16[1024,512]{1,0:T(8,128)(2,1)} %tok_ref.3, ...), custom_call_target="tpu_custom_call" | custom-call | flops 99999997952 | tf_op jit(solution)/shard_map/middle/pallas_call | solution.py:129
  98.0 4.2 %all-to-all-start.2 = ((bf16[32,48,256]{2,1,0:T(8,128)(2,1)}), bf16[32,48,256]{2,1,0:T(8,128)(2,1)S(1)}, u32[]{:S(2)}, u32[]{:S(2)}) async-start(bf16[32,48,256]{2,1,0:T(8,128)(2,1)} %bitcast.23), calls=%async_computation.2 | async-start | bytes 1572864 | tf_op jit(solution)/shard_map/all_to_all | solution.py:475
  102.5 12.7 %mlp_weights.1 = (bf16[1024,512]{1,0:T(8,128)(2,1)}, bf16[4,2,512,512]{3,2,1,0:T(8,128)(2,1)}) custom-call(bf16[1024,512]{1,0:T(8,128)(2,1)} %get-tuple-element.48.mid_ref, bf16[1024,2048]{1,0:T(8,128)(2,1)} %get-tuple-element.49.gated_ref, bf16[4096,512]{1,0:T(8,128)(2,1)} %all-gather.2.cloned.1.call-done.down_ref.up_ref, bf16[1024,512]{1,0:T(8,128)(2,1)} %cot_ref.5, ...), custom_call_target="tpu_custom_call" | custom-call | tf_op jit(solution)/shard_map/mlp_weights/pallas_call | solution.py:129
  115.2 1.4 all-to-all-done.2
  117.4 11.3 %moved_back.1 = (bf16[1024,768]{1,0:T(8,128)(2,1)}, bf16[1536,512]{1,0:T(8,128)(2,1)}) custom-call(bf16[1024,512]{1,0:T(8,128)(2,1)} %get-tuple-element.38.refs_0_, bf16[1536,256]{1,0:T(8,128)(2,1)} %bitcast.22, s32[1,1536]{1,0:T(1,128)} %get-tuple-element.54.refs_2_, bf16[1024,768]{1,0:T(8,128)(2,1)} %get-tuple-element.55.refs_3_, bf16[512,1536]{1,0:T(8,128)(2,1)} %refs_3_.1), custom_call_target="tpu_custom_call" | custom-call | flops 99999997952 | tf_op jit(solution)/shard_map/moved_back/pallas_call | solution.py:129
  128.7 6.1 %all-to-all-start.3 = ((bf16[32,48,512]{2,1,0:T(8,128)(2,1)}), bf16[32,48,512]{2,1,0:T(8,128)(2,1)S(1)}, u32[]{:S(2)}, u32[]{:S(2)}) async-start(bf16[32,48,512]{2,1,0:T(8,128)(2,1)} %bitcast.21), calls=%async_computation.3 | async-start | bytes 3145728 | tf_op jit(solution)/shard_map/all_to_all | solution.py:475
  134.9 11.6 %local_back.1 = (f32[1024,512]{1,0:T(8,128)}, bf16[512,768]{1,0:T(8,128)(2,1)}, bf16[512,512]{1,0:T(8,128)(2,1)}) custom-call(bf16[1024,768]{1,0:T(8,128)(2,1)} %copy-done.5, bf16[1024,256]{1,0:T(8,128)(2,1)} %get-tuple-element.60.refs_1_, bf16[1024,512]{1,0:T(8,128)(2,1)} %copy-done.10, bf16[512,1536]{1,0:T(8,128)(2,1)} %refs_3_.1, ...), custom_call_target="tpu_custom_call" | custom-call | tf_op jit(solution)/shard_map/local_back/pallas_call | solution.py:129
  146.5 1.2 copy-done.11
  147.7 1.1 copy-done.14
  149.9 2.2 moved_weights.1
  153.3 2.7 %collective-permute-done.refs_1_ = bf16[1024,512]{1,0:T(8,128)(2,1)S(1)} collective-permute-done((bf16[1024,512]{1,0:T(8,128)(2,1)}, bf16[1024,512]{1,0:T(8,128)(2,1)S(1)}, u32[]{:S(2)}, u32[]{:S(2)}) %collective-permute-start) | collective-permute-done | bytes 1048608 | tf_op jit(solution)/shard_map/ppermute | solution.py:480
  156.0 1.1 all-to-all-done.3
  157.1 1.2 copy-done.13
  158.3 1.2 add.6.refs_0_.after.also
  162.1 2.5 %collective-permute-start.2 = (bf16[128,512]{1,0:T(8,128)(2,1)S(1)}, bf16[128,512]{1,0:T(8,128)(2,1)S(1)}, u32[]{:S(2)}, u32[]{:S(2)}) collective-permute-start(bf16[128,512]{1,0:T(8,128)(2,1)S(1)} %get-tuple-element.72), channel_id=1, source_target_pairs={{0,16},{8,24},{16,0},{24,8},{1,17},{9,25},{17,1},{25,9},{2,18},{10... | collective-permute-start | bytes 393224 | tf_op jit(solution)/shard_map/ppermute | solution.py:493
  165.1 8.6 %all-to-all-start.4 = ((bf16[64,16,512]{2,1,0:T(8,128)(2,1)}), bf16[64,16,512]{2,1,0:T(8,128)(2,1)S(1)}, u32[]{:S(2)}, u32[]{:S(2)}) async-start(bf16[64,16,512]{2,1,0:T(8,128)(2,1)} %bitcast.13), calls=%async_computation.5 | async-start | bytes 2097152 | tf_op jit(solution)/shard_map/all_to_all | solution.py:532
  173.8 1.1 collective-permute-start.4
  174.9 1.2 copy-done.8
  176.2 1.2 copy-done.9
  177.4 1.6 copy-done.17
  179.0 4.3 %last.1.also = bf16[1024,512]{1,0:T(8,128)(2,1)} custom-call(bf16[128,512]{1,0:T(8,128)(2,1)S(1)} %get-tuple-element.69._.refs_2_, bf16[1024,512]{1,0:T(8,128)(2,1)S(1)} %copy-done.8, bf16[1024,512]{1,0:T(8,128)(2,1)S(1)} %copy-done.9, f32[1024,512]{1,0:T(8,128)S(1)} %copy-done.17, bf16[1536,512]{1,0:T(8,128)(2,1)S(1)} %bitcast.17, s32[1,1024]{1,0:T(1,128)S(1)} %copy-done.19), custom_call_target="tpu_custom_call" | custom-call | flops 99999997952 | tf_op jit(solution)/shard_map/last/pallas_call | solution.py:129
  183.3 7.3 %all-to-all-done.4.in_ref = bf16[64,16,512]{2,1,0:T(8,128)(2,1)S(1)} async-done(((bf16[64,16,512]{2,1,0:T(8,128)(2,1)}), bf16[64,16,512]{2,1,0:T(8,128)(2,1)S(1)}, u32[]{:S(2)}, u32[]{:S(2)}) %all-to-all-start.4) | async-done | bytes 1048608 | tf_op jit(solution)/shard_map/all_to_all | solution.py:532
  190.6 1.2 copy-done.6
  191.8 1.2 add_spread.1
  193.0 5.9 %all-to-all-start.5 = ((bf16[64,16,512]{2,1,0:T(8,128)(2,1)}), bf16[64,16,512]{2,1,0:T(8,128)(2,1)S(1)}, u32[]{:S(2)}, u32[]{:S(2)}) async-start(bf16[64,16,512]{2,1,0:T(8,128)(2,1)} %add_spread.1), calls=%async_computation.6 | async-start | bytes 2097152 | tf_op jit(solution)/shard_map/all_to_all | solution.py:557
  199.0 2.6 %collective-permute-start.5 = (bf16[32,512]{1,0:T(8,128)(2,1)S(1)}, bf16[32,512]{1,0:T(8,128)(2,1)S(1)}, u32[]{:S(2)}, u32[]{:S(2)}) collective-permute-start(bf16[32,512]{1,0:T(8,128)(2,1)S(1)} %get-tuple-element.76), channel_id=1, source_target_pairs={{0,64},{32,96},{64,0},{96,32},{1,65},{33,97},{65,1},{97,33},{2,66}... | collective-permute-start | bytes 98312 | tf_op jit(solution)/shard_map/ppermute | solution.py:493
  202.5 1.1 collective-permute-done.5.refs_2_
  203.6 6.1 %collective-permute-done.6.refs_3_ = bf16[32,512]{1,0:T(8,128)(2,1)S(1)} collective-permute-done((bf16[32,512]{1,0:T(8,128)(2,1)S(1)}, bf16[32,512]{1,0:T(8,128)(2,1)S(1)}, u32[]{:S(2)}, u32[]{:S(2)}) %collective-permute-start.6) | collective-permute-done | bytes 32800 | tf_op jit(solution)/shard_map/ppermute | solution.py:493
  209.8 7.3 %collective-permute-start.8 = (bf16[32,512]{1,0:T(8,128)(2,1)S(1)}, bf16[32,512]{1,0:T(8,128)(2,1)S(1)}, u32[]{:S(2)}, u32[]{:S(2)}) collective-permute-start(bf16[32,512]{1,0:T(8,128)(2,1)S(1)} %add.7.refs_0_), channel_id=1, source_target_pairs={{0,64},{32,96},{64,0},{96,32},{1,65},{33,97},{65,1},{97,33},{2,66}... | collective-permute-start | bytes 98312 | tf_op jit(solution)/shard_map/ppermute | solution.py:493
  218.7 1.4 collective-permute-done.9.refs_3_
  220.4 4.1 %collective-permute-start.11 = (bf16[128,512]{1,0:T(8,128)(2,1)S(1)}, bf16[128,512]{1,0:T(8,128)(2,1)S(1)}, u32[]{:S(2)}, u32[]{:S(2)}) collective-permute-start(bf16[128,512]{1,0:T(8,128)(2,1)S(1)} %gather.2.refs_0_), channel_id=1, source_target_pairs={{0,16},{8,24},{16,0},{24,8},{1,17},{9,25},{17,1},{25,9},{2,18},{10... | collective-permute-start | bytes 393224 | tf_op jit(solution)/shard_map/ppermute | solution.py:493
  225.7 2.9 %collective-permute-done.11.refs_2_ = bf16[128,512]{1,0:T(8,128)(2,1)S(1)} collective-permute-done((bf16[128,512]{1,0:T(8,128)(2,1)S(1)}, bf16[128,512]{1,0:T(8,128)(2,1)S(1)}, u32[]{:S(2)}, u32[]{:S(2)}) %collective-permute-start.11) | collective-permute-done | bytes 131104 | tf_op jit(solution)/shard_map/ppermute | solution.py:493
  229.7 2.6 %collective-permute-start.13 = (bf16[1024,512]{1,0:T(8,128)(2,1)S(1)}, bf16[1024,512]{1,0:T(8,128)(2,1)S(1)}, u32[]{:S(2)}, u32[]{:S(2)}) collective-permute-start(bf16[1024,512]{1,0:T(8,128)(2,1)S(1)} %add.8.mine_ref), channel_id=1, source_target_pairs={{0,4},{4,0},{1,5},{5,1},{2,6},{6,2},{3,7},{7,3},{8,12},{12,8},{9,1... | collective-permute-start | bytes 3145736 | tf_op jit(solution)/shard_map/ppermute | solution.py:480
  232.4 2.9 %collective-permute-done.14.other_ref = bf16[512,512]{1,0:T(8,128)(2,1)S(1)} collective-permute-done((bf16[512,512]{1,0:T(8,128)(2,1)S(1)}, bf16[512,512]{1,0:T(8,128)(2,1)S(1)}, u32[]{:S(2)}, u32[]{:S(2)}) %collective-permute-start.14) | collective-permute-done | bytes 524320 | tf_op jit(solution)/shard_map/ppermute | solution.py:480
  235.3 1.6 finish_mlp.1
  236.9 2.2 finish_attention.1
  (67 shorter events, 14.7 us)
Async XLA Ops:
  12.6 9.7 %copy-start.22 = (bf16[512,512]{1,0:T(8,128)(2,1)S(1)}, bf16[512,512]{1,0:T(8,128)(2,1)}, u32[]{:S(2)}) copy-start(bf16[512,512]{1,0:T(8,128)(2,1)} %param.11) | copy-start | bytes 1572868
  12.6 11.7 %copy-start.7 = (bf16[1024,512]{1,0:T(8,128)(2,1)S(1)}, bf16[1024,512]{1,0:T(8,128)(2,1)}, u32[]{:S(2)}) copy-start(bf16[1024,512]{1,0:T(8,128)(2,1)} %tok_ref.3) | copy-start | bytes 3145732
  12.6 34.6 %all-to-all-start = ((bf16[32,56,512]{2,1,0:T(8,128)(2,1)}), bf16[32,56,512]{2,1,0:T(8,128)(2,1)}, u32[]{:S(2)}, u32[]{:S(2)}) async-start(bf16[32,56,512]{2,1,0:T(8,128)(2,1)} %bitcast.20), calls=%async_computation | async-start | bytes 3670016 | tf_op jit(solution)/shard_map/all_to_all | solution.py:475
  22.2 2.1 copy-start.1
  22.2 42.8 %all-gather.2.cloned.1.call-start = ((), (), s32[]{:S(2)}) async-start(), calls=%async_computation.7 | async-start | bytes 4718592 | tf_op jit(solution)/shard_map/all_gather | solution.py:585
  28.7 1.2 copy-start.5
  29.9 1.0 copy-start.10
  30.9 0.8 copy-start.18
  59.1 6.0 %copy-start.3 = (bf16[1024,512]{1,0:T(8,128)(2,1)S(1)}, bf16[1024,512]{1,0:T(8,128)(2,1)}, u32[]{:S(2)}) copy-start(bf16[1024,512]{1,0:T(8,128)(2,1)} %cot_ref.5) | copy-start | bytes 3145732
  59.1 20.3 %all-to-all-start.1 = ((bf16[32,48,256]{2,1,0:T(8,128)(2,1)}), bf16[32,48,256]{2,1,0:T(8,128)(2,1)S(1)}, u32[]{:S(2)}, u32[]{:S(2)}) async-start(bf16[32,48,256]{2,1,0:T(8,128)(2,1)} %bitcast.25), calls=%async_computation.1 | async-start | bytes 1572864 | tf_op jit(solution)/shard_map/all_to_all | solution.py:475
  65.1 2.2 copy-start
  70.3 2.0 copy-start.2
  79.4 0.9 copy-start.21
  98.0 18.5 %all-to-all-start.2 = ((bf16[32,48,256]{2,1,0:T(8,128)(2,1)}), bf16[32,48,256]{2,1,0:T(8,128)(2,1)S(1)}, u32[]{:S(2)}, u32[]{:S(2)}) async-start(bf16[32,48,256]{2,1,0:T(8,128)(2,1)} %bitcast.23), calls=%async_computation.2 | async-start | bytes 1572864 | tf_op jit(solution)/shard_map/all_to_all | solution.py:475
  102.2 57.3 %reduce-scatter.2.cloned.1.call-start = ((), (), s32[]{:S(2)}) async-start(), calls=%async_computation.8 | async-start | bytes 4718592 | tf_op jit(solution)/shard_map/reduce_scatter | solution.py:653
  116.5 0.9 copy-start.20
  128.7 28.3 %all-to-all-start.3 = ((bf16[32,48,512]{2,1,0:T(8,128)(2,1)}), bf16[32,48,512]{2,1,0:T(8,128)(2,1)S(1)}, u32[]{:S(2)}, u32[]{:S(2)}) async-start(bf16[32,48,512]{2,1,0:T(8,128)(2,1)} %bitcast.21), calls=%async_computation.3 | async-start | bytes 3145728 | tf_op jit(solution)/shard_map/all_to_all | solution.py:475
  134.9 11.6 %copy-start.4 = (bf16[1024,768]{1,0:T(8,128)(2,1)S(1)}, bf16[1024,768]{1,0:T(8,128)(2,1)}, u32[]{:S(2)}) copy-start(bf16[1024,768]{1,0:T(8,128)(2,1)} %get-tuple-element.58.gpk_ref) | copy-start | bytes 4718596
  146.5 1.3 copy-start.11
  147.7 1.1 copy-start.14
  148.9 1.1 copy-start.15
  152.1 1.0 copy-start.12
  153.1 2.9 %collective-permute-start = (bf16[1024,512]{1,0:T(8,128)(2,1)}, bf16[1024,512]{1,0:T(8,128)(2,1)S(1)}, u32[]{:S(2)}, u32[]{:S(2)}) collective-permute-start(bf16[1024,512]{1,0:T(8,128)(2,1)} %get-tuple-element.67), channel_id=1, source_target_pairs={{0,4},{4,0},{1,5},{5,1},{2,6},{6,2},{3,7},{7,3},{8,12},{12,8},{9,1... | collective-permute-start | bytes 3145736 | tf_op jit(solution)/shard_map/ppermute | solution.py:480
  157.1 1.2 copy-start.13
  159.5 1.0 copy-start.16
  161.3 12.4 %collective-permute-start.1 = (bf16[128,512]{1,0:T(8,128)(2,1)}, bf16[128,512]{1,0:T(8,128)(2,1)S(1)}, u32[]{:S(2)}, u32[]{:S(2)}) collective-permute-start(bf16[128,512]{1,0:T(8,128)(2,1)} %get-tuple-element.71), channel_id=1, source_target_pairs={{0,8},{8,16},{16,24},{24,0},{1,9},{9,17},{17,25},{25,1},{2,10},{10... | collective-permute-start | bytes 393224 | tf_op jit(solution)/shard_map/ppermute | solution.py:493
  162.1 11.6 %collective-permute-start.2 = (bf16[128,512]{1,0:T(8,128)(2,1)S(1)}, bf16[128,512]{1,0:T(8,128)(2,1)S(1)}, u32[]{:S(2)}, u32[]{:S(2)}) collective-permute-start(bf16[128,512]{1,0:T(8,128)(2,1)S(1)} %get-tuple-element.72), channel_id=1, source_target_pairs={{0,16},{8,24},{16,0},{24,8},{1,17},{9,25},{17,1},{25,9},{2,18},{10... | collective-permute-start | bytes 393224 | tf_op jit(solution)/shard_map/ppermute | solution.py:493
  164.7 9.1 %collective-permute-start.3 = (bf16[128,512]{1,0:T(8,128)(2,1)S(1)}, bf16[128,512]{1,0:T(8,128)(2,1)S(1)}, u32[]{:S(2)}, u32[]{:S(2)}) collective-permute-start(bf16[128,512]{1,0:T(8,128)(2,1)S(1)} %get-tuple-element.73), channel_id=1, source_target_pairs={{0,24},{8,0},{16,8},{24,16},{1,25},{9,1},{17,9},{25,17},{2,26},{10... | collective-permute-start | bytes 393224 | tf_op jit(solution)/shard_map/ppermute | solution.py:493
  165.1 9.8 %copy-start.19 = (s32[1,1024]{1,0:T(1,128)S(1)}, s32[1,1024]{1,0:T(1,128)}, u32[]{:S(2)}) copy-start(s32[1,1024]{1,0:T(1,128)} %get-tuple-element.47.part_ref.slot_ref) | copy-start | bytes 12292
  165.1 25.4 %all-to-all-start.4 = ((bf16[64,16,512]{2,1,0:T(8,128)(2,1)}), bf16[64,16,512]{2,1,0:T(8,128)(2,1)S(1)}, u32[]{:S(2)}, u32[]{:S(2)}) async-start(bf16[64,16,512]{2,1,0:T(8,128)(2,1)} %bitcast.13), calls=%async_computation.5 | async-start | bytes 2097152 | tf_op jit(solution)/shard_map/all_to_all | solution.py:532
  173.8 16.7 %collective-permute-start.4 = (bf16[32,512]{1,0:T(8,128)(2,1)S(1)}, bf16[32,512]{1,0:T(8,128)(2,1)S(1)}, u32[]{:S(2)}, u32[]{:S(2)}) collective-permute-start(bf16[32,512]{1,0:T(8,128)(2,1)S(1)} %get-tuple-element.75), channel_id=1, source_target_pairs={{0,32},{32,64},{64,96},{96,0},{1,33},{33,65},{65,97},{97,1},{2,34}... | collective-permute-start | bytes 98312 | tf_op jit(solution)/shard_map/ppermute | solution.py:493
  174.9 1.2 copy-start.8
  176.2 1.2 copy-start.9
  177.4 1.6 copy-start.17
  190.6 1.2 copy-start.6
  193.0 36.5 %all-to-all-start.5 = ((bf16[64,16,512]{2,1,0:T(8,128)(2,1)}), bf16[64,16,512]{2,1,0:T(8,128)(2,1)S(1)}, u32[]{:S(2)}, u32[]{:S(2)}) async-start(bf16[64,16,512]{2,1,0:T(8,128)(2,1)} %add_spread.1), calls=%async_computation.6 | async-start | bytes 2097152 | tf_op jit(solution)/shard_map/all_to_all | solution.py:557
  199.0 4.6 %collective-permute-start.5 = (bf16[32,512]{1,0:T(8,128)(2,1)S(1)}, bf16[32,512]{1,0:T(8,128)(2,1)S(1)}, u32[]{:S(2)}, u32[]{:S(2)}) collective-permute-start(bf16[32,512]{1,0:T(8,128)(2,1)S(1)} %get-tuple-element.76), channel_id=1, source_target_pairs={{0,64},{32,96},{64,0},{96,32},{1,65},{33,97},{65,1},{97,33},{2,66}... | collective-permute-start | bytes 98312 | tf_op jit(solution)/shard_map/ppermute | solution.py:493
  201.6 8.1 %collective-permute-start.6 = (bf16[32,512]{1,0:T(8,128)(2,1)S(1)}, bf16[32,512]{1,0:T(8,128)(2,1)S(1)}, u32[]{:S(2)}, u32[]{:S(2)}) collective-permute-start(bf16[32,512]{1,0:T(8,128)(2,1)S(1)} %get-tuple-element.77), channel_id=1, source_target_pairs={{0,96},{32,0},{64,32},{96,64},{1,97},{33,1},{65,33},{97,65},{2,98}... | collective-permute-start | bytes 98312 | tf_op jit(solution)/shard_map/ppermute | solution.py:493
  209.7 8.2 %collective-permute-start.7 = (bf16[32,512]{1,0:T(8,128)(2,1)S(1)}, bf16[32,512]{1,0:T(8,128)(2,1)S(1)}, u32[]{:S(2)}, u32[]{:S(2)}) collective-permute-start(bf16[32,512]{1,0:T(8,128)(2,1)S(1)} %add.7.refs_0_), channel_id=1, source_target_pairs={{0,32},{32,64},{64,96},{96,0},{1,33},{33,65},{65,97},{97,1},{2,34}... | collective-permute-start | bytes 98312 | tf_op jit(solution)/shard_map/ppermute | solution.py:493
  209.8 8.9 %collective-permute-start.8 = (bf16[32,512]{1,0:T(8,128)(2,1)S(1)}, bf16[32,512]{1,0:T(8,128)(2,1)S(1)}, u32[]{:S(2)}, u32[]{:S(2)}) collective-permute-start(bf16[32,512]{1,0:T(8,128)(2,1)S(1)} %add.7.refs_0_), channel_id=1, source_target_pairs={{0,64},{32,96},{64,0},{96,32},{1,65},{33,97},{65,1},{97,33},{2,66}... | collective-permute-start | bytes 98312 | tf_op jit(solution)/shard_map/ppermute | solution.py:493
  217.1 3.0 %collective-permute-start.9 = (bf16[32,512]{1,0:T(8,128)(2,1)S(1)}, bf16[32,512]{1,0:T(8,128)(2,1)S(1)}, u32[]{:S(2)}, u32[]{:S(2)}) collective-permute-start(bf16[32,512]{1,0:T(8,128)(2,1)S(1)} %add.7.refs_0_), channel_id=1, source_target_pairs={{0,96},{32,0},{64,32},{96,64},{1,97},{33,1},{65,33},{97,65},{2,98}... | collective-permute-start | bytes 98312 | tf_op jit(solution)/shard_map/ppermute | solution.py:493
  220.1 5.6 %collective-permute-start.10 = (bf16[128,512]{1,0:T(8,128)(2,1)S(1)}, bf16[128,512]{1,0:T(8,128)(2,1)S(1)}, u32[]{:S(2)}, u32[]{:S(2)}) collective-permute-start(bf16[128,512]{1,0:T(8,128)(2,1)S(1)} %gather.2.refs_0_), channel_id=1, source_target_pairs={{0,8},{8,16},{16,24},{24,0},{1,9},{9,17},{17,25},{25,1},{2,10},{10... | collective-permute-start | bytes 393224 | tf_op jit(solution)/shard_map/ppermute | solution.py:493
  220.4 8.2 %collective-permute-start.11 = (bf16[128,512]{1,0:T(8,128)(2,1)S(1)}, bf16[128,512]{1,0:T(8,128)(2,1)S(1)}, u32[]{:S(2)}, u32[]{:S(2)}) collective-permute-start(bf16[128,512]{1,0:T(8,128)(2,1)S(1)} %gather.2.refs_0_), channel_id=1, source_target_pairs={{0,16},{8,24},{16,0},{24,8},{1,17},{9,25},{17,1},{25,9},{2,18},{10... | collective-permute-start | bytes 393224 | tf_op jit(solution)/shard_map/ppermute | solution.py:493
  224.5 5.0 %collective-permute-start.12 = (bf16[128,512]{1,0:T(8,128)(2,1)S(1)}, bf16[128,512]{1,0:T(8,128)(2,1)S(1)}, u32[]{:S(2)}, u32[]{:S(2)}) collective-permute-start(bf16[128,512]{1,0:T(8,128)(2,1)S(1)} %gather.2.refs_0_), channel_id=1, source_target_pairs={{0,24},{8,0},{16,8},{24,16},{1,25},{9,1},{17,9},{25,17},{2,26},{10... | collective-permute-start | bytes 393224 | tf_op jit(solution)/shard_map/ppermute | solution.py:493
  229.7 7.3 %collective-permute-start.13 = (bf16[1024,512]{1,0:T(8,128)(2,1)S(1)}, bf16[1024,512]{1,0:T(8,128)(2,1)S(1)}, u32[]{:S(2)}, u32[]{:S(2)}) collective-permute-start(bf16[1024,512]{1,0:T(8,128)(2,1)S(1)} %add.8.mine_ref), channel_id=1, source_target_pairs={{0,4},{4,0},{1,5},{5,1},{2,6},{6,2},{3,7},{7,3},{8,12},{12,8},{9,1... | collective-permute-start | bytes 3145736 | tf_op jit(solution)/shard_map/ppermute | solution.py:480
  232.3 3.0 %collective-permute-start.14 = (bf16[512,512]{1,0:T(8,128)(2,1)S(1)}, bf16[512,512]{1,0:T(8,128)(2,1)S(1)}, u32[]{:S(2)}, u32[]{:S(2)}) collective-permute-start(bf16[512,512]{1,0:T(8,128)(2,1)S(1)} %gather.3.after.also.mine_ref), channel_id=1, source_target_pairs={{0,4},{4,0},{1,5},{5,1},{2,6},{6,2},{3,7},{7,3},{8,12},{12,8},{9,1... | collective-permute-start | bytes 1572872 | tf_op jit(solution)/shard_map/ppermute | solution.py:480
Sparse Core Ops, SparseCore 0:
  25.3 33.7 all-gather.1
  115.3 36.3 reduce-scatter.1

commit v7 on v5

--- a/solution.py
+++ b/solution.py
@@ -693,7 +693,7 @@
         [(shape((width, width), F32), whole(width, width)), (shape((width, width), F32), whole(width, width))],
         name="finish_mlp",
     )
-    mine = add([sum_at_once(pair, ("narrow", "x", "z"), halfway)], mlp_mine, grad_tokens)
+    mine = add([sum_at_once(pair, ("z", "x", "narrow"), halfway)], mlp_mine, grad_tokens)
     grad_qkv, grad_proj = call(
         finish_attention_kernel, 1, [flag, whole_array(mine), whole_array(swap_core(mine))],
         [(shape((width, 2 * third), F32), whole(width, 2 * third)), (shape((width, width), F32), whole(width, width))],

time: 244 us -> 245 us (level)
  no operation moved by 1% of the time
where the time goes in v7:
time: 245 us; the launch traced here: 243 us
  Pallas kernels  89.8 us (37%)
  starting transfers between devices  65.5 us (27%)
  waiting for transfers between devices  49.9 us (20%)
  local copies, waits for them, and re-layouts  21.9 us (9%)
  between operations  14.4 us (6%)
    pallas_call x20, Pallas kernels, call(): pl.pallas_call(kernel, grid=(steps,), out_shape=[out for out, _ in outs],...  89.8 us
    all_to_all x4, waiting for transfers between devices, exchange(): lax.all_to_all(sent, ('z', 'x', 'core'), split_axis=0, concat_axis=0, til...  26.2 us
    all_to_all x4, starting transfers between devices, exchange(): lax.all_to_all(sent, ('z', 'x', 'core'), split_axis=0, concat_axis=0, til...  25.9 us
    unnamed x48, local copies, waits for them, and re-layouts  21.9 us
    ppermute x12, waiting for transfers between devices, shift_by(): lax.ppermute(block, axis, [(place, (place + shift) % count) for place in...  18.2 us
    ppermute x12, starting transfers between devices, shift_by(): lax.ppermute(block, axis, [(place, (place + shift) % count) for place in...  17.6 us
    all_to_all x1, starting transfers between devices, share_of_sum(): return lax.all_to_all(parts, axes, split_axis=0, concat_axis=0, tiled=True)  7.94 us
    all_to_all x1, starting transfers between devices, sum_at_once(): told = lax.all_to_all(spread, axes, split_axis=0, concat_axis=0, tiled=True)  7.06 us
  transfers between devices with their start and end apart: 23, of which 12 were waited for; matrix products, arithmetic and copies ran while one was open for 1% of the time, Pallas kernels for 26%

profile of v7, /device:TPU:1, one launch (start us, length us, event | category | flops | bytes accessed | tf_op | source)
XLA Modules:
  0.0 243.5 jit_solution(9120302493948158053)
XLA Ops:
  7.2 5.4 %route.1 = (bf16[1792,512]{1,0:T(8,128)(2,1)}, s32[1,1024]{1,0:T(1,128)}) custom-call(s32[1,1024]{1,0:T(1,128)} %bitcast.26, bf16[1024,512]{1,0:T(8,128)(2,1)} %tok_ref.3), custom_call_target="tpu_custom_call" | custom-call | flops 99999997952 | tf_op jit(solution)/shard_map/route/pallas_call | solution.py:129
  12.6 9.6 %all-to-all-start = ((bf16[32,56,512]{2,1,0:T(8,128)(2,1)}), bf16[32,56,512]{2,1,0:T(8,128)(2,1)}, u32[]{:S(2)}, u32[]{:S(2)}) async-start(bf16[32,56,512]{2,1,0:T(8,128)(2,1)} %bitcast.20), calls=%async_computation | async-start | bytes 3670016 | tf_op jit(solution)/shard_map/all_to_all | solution.py:475
  22.3 2.0 broadcast_select_fusion
  24.3 4.3 %first_local.1 = (bf16[1024,512]{1,0:T(8,128)(2,1)S(1)}, bf16[1024,768]{1,0:T(8,128)(2,1)S(1)}, bf16[1024,256]{1,0:T(8,128)(2,1)S(1)}) custom-call(bf16[1024,512]{1,0:T(8,128)(2,1)S(1)} %copy-done.8, bf16[512,1536]{1,0:T(8,128)(2,1)S(1)} %copy-done.1), custom_call_target="tpu_custom_call" | custom-call | tf_op jit(solution)/shard_map/first_local/pallas_call | solution.py:129
  28.7 1.2 copy-done.6
  31.7 15.5 %all-to-all-done = bf16[32,56,512]{2,1,0:T(8,128)(2,1)} async-done(((bf16[32,56,512]{2,1,0:T(8,128)(2,1)}), bf16[32,56,512]{2,1,0:T(8,128)(2,1)}, u32[]{:S(2)}, u32[]{:S(2)}) %all-to-all-start) | async-done | bytes 1835040 | tf_op jit(solution)/shard_map/all_to_all | solution.py:475
  47.2 11.9 %moved.1 = (bf16[1024,512]{1,0:T(8,128)(2,1)}, bf16[1024,768]{1,0:T(8,128)(2,1)}, s32[1,1536]{1,0:T(1,128)}, bf16[1536,256]{1,0:T(8,128)(2,1)}) custom-call(bf16[1024,256]{1,0:T(8,128)(2,1)} %copy-done.19, bf16[1792,512]{1,0:T(8,128)(2,1)} %bitcast.2.refs_1_, bf16[512,1536]{1,0:T(8,128)(2,1)} %refs_3_.1), custom_call_target="tpu_custom_call" | custom-call | flops 99999997952 | tf_op jit(solution)/shard_map/moved/pallas_call | solution.py:129
  59.1 6.0 %all-to-all-start.1 = ((bf16[32,48,256]{2,1,0:T(8,128)(2,1)}), bf16[32,48,256]{2,1,0:T(8,128)(2,1)S(1)}, u32[]{:S(2)}, u32[]{:S(2)}) async-start(bf16[32,48,256]{2,1,0:T(8,128)(2,1)} %bitcast.25), calls=%async_computation.1 | async-start | bytes 1572864 | tf_op jit(solution)/shard_map/all_to_all | solution.py:475
  65.1 2.2 copy-done
  67.3 3.0 %grad_act.1.act_ref = bf16[1024,2048]{1,0:T(8,128)(2,1)S(1)} custom-call(bf16[1024,512]{1,0:T(8,128)(2,1)S(1)} %copy-done.4, bf16[4096,512]{1,0:T(8,128)(2,1)S(1)} %copy-done), custom_call_target="tpu_custom_call" | custom-call | tf_op jit(solution)/shard_map/grad_act/pallas_call | solution.py:129
  70.3 2.0 copy-done.2
  72.3 7.1 %all-to-all-done.1 = bf16[32,48,256]{2,1,0:T(8,128)(2,1)S(1)} async-done(((bf16[32,48,256]{2,1,0:T(8,128)(2,1)}), bf16[32,48,256]{2,1,0:T(8,128)(2,1)S(1)}, u32[]{:S(2)}, u32[]{:S(2)}) %all-to-all-start.1) | async-done | bytes 786464 | tf_op jit(solution)/shard_map/all_to_all | solution.py:475
  80.2 17.8 %middle.1 = (bf16[1024,512]{1,0:T(8,128)(2,1)}, bf16[1024,512]{1,0:T(8,128)(2,1)}, bf16[1024,512]{1,0:T(8,128)(2,1)}, bf16[1024,2048]{1,0:T(8,128)(2,1)}, bf16[1...) custom-call(bf16[1024,512]{1,0:T(8,128)(2,1)} %tok_ref.3, ...), custom_call_target="tpu_custom_call" | custom-call | flops 99999997952 | tf_op jit(solution)/shard_map/middle/pallas_call | solution.py:129
  98.0 4.2 %all-to-all-start.2 = ((bf16[32,48,256]{2,1,0:T(8,128)(2,1)}), bf16[32,48,256]{2,1,0:T(8,128)(2,1)S(1)}, u32[]{:S(2)}, u32[]{:S(2)}) async-start(bf16[32,48,256]{2,1,0:T(8,128)(2,1)} %bitcast.23), calls=%async_computation.2 | async-start | bytes 1572864 | tf_op jit(solution)/shard_map/all_to_all | solution.py:475
  102.5 12.7 %mlp_weights.1 = (bf16[1024,512]{1,0:T(8,128)(2,1)}, bf16[4,2,512,512]{3,2,1,0:T(8,128)(2,1)}) custom-call(bf16[1024,512]{1,0:T(8,128)(2,1)} %get-tuple-element.48.mid_ref, bf16[1024,2048]{1,0:T(8,128)(2,1)} %get-tuple-element.49.gated_ref, bf16[4096,512]{1,0:T(8,128)(2,1)} %all-gather.2.cloned.1.call-done.down_ref.up_ref, bf16[1024,512]{1,0:T(8,128)(2,1)} %cot_ref.5, ...), custom_call_target="tpu_custom_call" | custom-call | tf_op jit(solution)/shard_map/mlp_weights/pallas_call | solution.py:129
  115.2 1.3 all-to-all-done.2
  117.4 11.3 %moved_back.1 = (bf16[1024,768]{1,0:T(8,128)(2,1)}, bf16[1536,512]{1,0:T(8,128)(2,1)}) custom-call(bf16[1024,512]{1,0:T(8,128)(2,1)} %get-tuple-element.38.refs_0_, bf16[1536,256]{1,0:T(8,128)(2,1)} %bitcast.22, s32[1,1536]{1,0:T(1,128)} %get-tuple-element.54.refs_2_, bf16[1024,768]{1,0:T(8,128)(2,1)} %get-tuple-element.55.refs_3_, bf16[512,1536]{1,0:T(8,128)(2,1)} %refs_3_.1), custom_call_target="tpu_custom_call" | custom-call | flops 99999997952 | tf_op jit(solution)/shard_map/moved_back/pallas_call | solution.py:129
  128.7 6.2 %all-to-all-start.3 = ((bf16[32,48,512]{2,1,0:T(8,128)(2,1)}), bf16[32,48,512]{2,1,0:T(8,128)(2,1)S(1)}, u32[]{:S(2)}, u32[]{:S(2)}) async-start(bf16[32,48,512]{2,1,0:T(8,128)(2,1)} %bitcast.21), calls=%async_computation.3 | async-start | bytes 3145728 | tf_op jit(solution)/shard_map/all_to_all | solution.py:475
  134.9 11.6 %local_back.1 = (f32[1024,512]{1,0:T(8,128)}, bf16[512,768]{1,0:T(8,128)(2,1)}, bf16[512,512]{1,0:T(8,128)(2,1)}) custom-call(bf16[1024,768]{1,0:T(8,128)(2,1)} %copy-done.6, bf16[1024,256]{1,0:T(8,128)(2,1)} %get-tuple-element.60.refs_1_, bf16[1024,512]{1,0:T(8,128)(2,1)} %copy-done.11, bf16[512,1536]{1,0:T(8,128)(2,1)} %refs_3_.1, ...), custom_call_target="tpu_custom_call" | custom-call | tf_op jit(solution)/shard_map/local_back/pallas_call | solution.py:129
  146.5 1.2 copy-done.12
  150.0 1.2 moved_weights.1
  152.3 2.5 %collective-permute-done.refs_1_ = bf16[1024,512]{1,0:T(8,128)(2,1)S(1)} collective-permute-done((bf16[1024,512]{1,0:T(8,128)(2,1)S(1)}, bf16[1024,512]{1,0:T(8,128)(2,1)S(1)}, u32[]{:S(2)}, u32[]{:S(2)}) %collective-permute-start) | collective-permute-done | bytes 1048608 | tf_op jit(solution)/shard_map/ppermute | solution.py:480
  154.8 2.3 all-to-all-done.3
  157.1 1.2 copy-done.14
  158.3 1.2 add.6.refs_0_.after.also
  159.5 7.9 %all-to-all-start.4 = ((bf16[64,16,512]{2,1,0:T(8,128)(2,1)}), bf16[64,16,512]{2,1,0:T(8,128)(2,1)S(1)}, u32[]{:S(2)}, u32[]{:S(2)}) async-start(bf16[64,16,512]{2,1,0:T(8,128)(2,1)} %bitcast.13), calls=%async_computation.5 | async-start | bytes 2097152 | tf_op jit(solution)/shard_map/all_to_all | solution.py:532
  170.3 2.4 collective-permute-start.2
  172.7 1.2 collective-permute-start.3
  173.9 10.2 %collective-permute-done.1.refs_3_ = bf16[128,512]{1,0:T(8,128)(2,1)S(1)} collective-permute-done((bf16[128,512]{1,0:T(8,128)(2,1)}, bf16[128,512]{1,0:T(8,128)(2,1)S(1)}, u32[]{:S(2)}, u32[]{:S(2)}) %collective-permute-start.1) | collective-permute-done | bytes 131104 | tf_op jit(solution)/shard_map/ppermute | solution.py:493
  184.1 2.7 %collective-permute-done.2.refs_4_ = bf16[128,512]{1,0:T(8,128)(2,1)S(1)} collective-permute-done((bf16[128,512]{1,0:T(8,128)(2,1)S(1)}, bf16[128,512]{1,0:T(8,128)(2,1)S(1)}, u32[]{:S(2)}, u32[]{:S(2)}) %collective-permute-start.2) | collective-permute-done | bytes 131104 | tf_op jit(solution)/shard_map/ppermute | solution.py:493
  187.0 1.3 collective-permute-start.4
  188.2 2.6 %collective-permute-start.5 = (bf16[32,512]{1,0:T(8,128)(2,1)S(1)}, bf16[32,512]{1,0:T(8,128)(2,1)S(1)}, u32[]{:S(2)}, u32[]{:S(2)}) collective-permute-start(bf16[32,512]{1,0:T(8,128)(2,1)S(1)} %get-tuple-element.76), channel_id=1, source_target_pairs={{0,64},{32,96},{64,0},{96,32},{1,65},{33,97},{65,1},{97,33},{2,66}... | collective-permute-start | bytes 98312 | tf_op jit(solution)/shard_map/ppermute | solution.py:493
  192.5 1.6 collective-permute-done.6.refs_3_
  194.2 3.3 %collective-permute-start.8 = (bf16[32,512]{1,0:T(8,128)(2,1)S(1)}, bf16[32,512]{1,0:T(8,128)(2,1)S(1)}, u32[]{:S(2)}, u32[]{:S(2)}) collective-permute-start(bf16[32,512]{1,0:T(8,128)(2,1)S(1)} %add.7.refs_0_), channel_id=1, source_target_pairs={{0,64},{32,96},{64,0},{96,32},{1,65},{33,97},{65,1},{97,33},{2,66}... | collective-permute-start | bytes 98312 | tf_op jit(solution)/shard_map/ppermute | solution.py:493
  198.8 7.1 %all-to-all-start.5 = ((bf16[64,16,512]{2,1,0:T(8,128)(2,1)}), bf16[64,16,512]{2,1,0:T(8,128)(2,1)S(1)}, u32[]{:S(2)}, u32[]{:S(2)}) async-start(bf16[64,16,512]{2,1,0:T(8,128)(2,1)} %copy-done.3), calls=%async_computation.6 | async-start | bytes 2097152 | tf_op jit(solution)/shard_map/all_to_all | solution.py:555
  207.0 2.4 collective-permute-start.11
  209.4 1.2 collective-permute-start.12
  210.6 1.2 copy-done.9
  211.8 1.2 copy-done.10
  213.0 1.6 copy-done.18
  214.6 4.3 %last.1.also = bf16[1024,512]{1,0:T(8,128)(2,1)} custom-call(bf16[32,512]{1,0:T(8,128)(2,1)S(1)} %get-tuple-element.73._.refs_0_.after, bf16[1024,512]{1,0:T(8,128)(2,1)S(1)} %copy-done.9, bf16[1024,512]{1,0:T(8,128)(2,1)S(1)} %copy-done.10, f32[1024,512]{1,0:T(8,128)S(1)} %copy-done.18, bf16[1536,512]{1,0:T(8,128)(2,1)S(1)} %bitcast.17, ...), custom_call_target="tpu_custom_call" | custom-call | flops 99999997952 | tf_op jit(solution)/shard_map/last/pallas_call | solution.py:129
  218.9 1.3 collective-permute-done.10.refs_1_
  220.2 1.8 collective-permute-done.11.refs_2_
  222.0 1.2 copy-done.7
  223.3 6.4 %collective-permute-start.13 = (bf16[1024,512]{1,0:T(8,128)(2,1)S(1)}, bf16[1024,512]{1,0:T(8,128)(2,1)S(1)}, u32[]{:S(2)}, u32[]{:S(2)}) collective-permute-start(bf16[1024,512]{1,0:T(8,128)(2,1)S(1)} %add.8.mine_ref), channel_id=1, source_target_pairs={{0,4},{4,0},{1,5},{5,1},{2,6},{6,2},{3,7},{7,3},{8,12},{12,8},{9,1... | collective-permute-start | bytes 3145736 | tf_op jit(solution)/shard_map/ppermute | solution.py:480
  229.8 2.9 %collective-permute-done.14.other_ref = bf16[512,512]{1,0:T(8,128)(2,1)S(1)} collective-permute-done((bf16[512,512]{1,0:T(8,128)(2,1)S(1)}, bf16[512,512]{1,0:T(8,128)(2,1)S(1)}, u32[]{:S(2)}, u32[]{:S(2)}) %collective-permute-start.14) | collective-permute-done | bytes 524320 | tf_op jit(solution)/shard_map/ppermute | solution.py:480
  232.8 1.6 finish_mlp.1
  234.4 2.2 finish_attention.1
  (69 shorter events, 14.5 us)
Async XLA Ops:
  12.6 9.7 %copy-start.23 = (bf16[512,512]{1,0:T(8,128)(2,1)S(1)}, bf16[512,512]{1,0:T(8,128)(2,1)}, u32[]{:S(2)}) copy-start(bf16[512,512]{1,0:T(8,128)(2,1)} %param.11) | copy-start | bytes 1572868
  12.6 11.7 %copy-start.8 = (bf16[1024,512]{1,0:T(8,128)(2,1)S(1)}, bf16[1024,512]{1,0:T(8,128)(2,1)}, u32[]{:S(2)}) copy-start(bf16[1024,512]{1,0:T(8,128)(2,1)} %tok_ref.3) | copy-start | bytes 3145732
  12.6 34.6 %all-to-all-start = ((bf16[32,56,512]{2,1,0:T(8,128)(2,1)}), bf16[32,56,512]{2,1,0:T(8,128)(2,1)}, u32[]{:S(2)}, u32[]{:S(2)}) async-start(bf16[32,56,512]{2,1,0:T(8,128)(2,1)} %bitcast.20), calls=%async_computation | async-start | bytes 3670016 | tf_op jit(solution)/shard_map/all_to_all | solution.py:475
  22.2 2.1 copy-start.1
  22.2 42.8 %all-gather.2.cloned.1.call-start = ((), (), s32[]{:S(2)}) async-start(), calls=%async_computation.7 | async-start | bytes 4718592 | tf_op jit(solution)/shard_map/all_gather | solution.py:583
  28.7 1.2 copy-start.6
  29.9 1.0 copy-start.11
  30.9 0.8 copy-start.19
  59.1 6.0 %copy-start.4 = (bf16[1024,512]{1,0:T(8,128)(2,1)S(1)}, bf16[1024,512]{1,0:T(8,128)(2,1)}, u32[]{:S(2)}) copy-start(bf16[1024,512]{1,0:T(8,128)(2,1)} %cot_ref.5) | copy-start | bytes 3145732
  59.1 20.3 %all-to-all-start.1 = ((bf16[32,48,256]{2,1,0:T(8,128)(2,1)}), bf16[32,48,256]{2,1,0:T(8,128)(2,1)S(1)}, u32[]{:S(2)}, u32[]{:S(2)}) async-start(bf16[32,48,256]{2,1,0:T(8,128)(2,1)} %bitcast.25), calls=%async_computation.1 | async-start | bytes 1572864 | tf_op jit(solution)/shard_map/all_to_all | solution.py:475
  65.1 2.2 copy-start
  70.3 2.0 copy-start.2
  79.4 0.9 copy-start.22
  98.0 18.5 %all-to-all-start.2 = ((bf16[32,48,256]{2,1,0:T(8,128)(2,1)}), bf16[32,48,256]{2,1,0:T(8,128)(2,1)S(1)}, u32[]{:S(2)}, u32[]{:S(2)}) async-start(bf16[32,48,256]{2,1,0:T(8,128)(2,1)} %bitcast.23), calls=%async_computation.2 | async-start | bytes 1572864 | tf_op jit(solution)/shard_map/all_to_all | solution.py:475
  102.2 65.3 %reduce-scatter.2.cloned.1.call-start = ((), (), s32[]{:S(2)}) async-start(), calls=%async_computation.8 | async-start | bytes 4718592 | tf_op jit(solution)/shard_map/reduce_scatter | solution.py:651
  116.5 0.9 copy-start.21
  128.7 28.4 %all-to-all-start.3 = ((bf16[32,48,512]{2,1,0:T(8,128)(2,1)}), bf16[32,48,512]{2,1,0:T(8,128)(2,1)S(1)}, u32[]{:S(2)}, u32[]{:S(2)}) async-start(bf16[32,48,512]{2,1,0:T(8,128)(2,1)} %bitcast.21), calls=%async_computation.3 | async-start | bytes 3145728 | tf_op jit(solution)/shard_map/all_to_all | solution.py:475
  134.9 11.6 %copy-start.5 = (bf16[1024,768]{1,0:T(8,128)(2,1)S(1)}, bf16[1024,768]{1,0:T(8,128)(2,1)}, u32[]{:S(2)}) copy-start(bf16[1024,768]{1,0:T(8,128)(2,1)} %get-tuple-element.58.gpk_ref) | copy-start | bytes 4718596
  146.5 1.3 copy-start.12
  147.8 1.1 copy-start.15
  148.9 1.1 copy-start.16
  151.2 1.0 copy-start.13
  152.1 2.7 %collective-permute-start = (bf16[1024,512]{1,0:T(8,128)(2,1)S(1)}, bf16[1024,512]{1,0:T(8,128)(2,1)S(1)}, u32[]{:S(2)}, u32[]{:S(2)}) collective-permute-start(bf16[1024,512]{1,0:T(8,128)(2,1)S(1)} %get-tuple-element.67), channel_id=1, source_target_pairs={{0,4},{4,0},{1,5},{5,1},{2,6},{6,2},{3,7},{7,3},{8,12},{12,8},{9,1... | collective-permute-start | bytes 3145736 | tf_op jit(solution)/shard_map/ppermute | solution.py:480
  157.1 1.2 copy-start.14
  159.5 38.0 %all-to-all-start.4 = ((bf16[64,16,512]{2,1,0:T(8,128)(2,1)}), bf16[64,16,512]{2,1,0:T(8,128)(2,1)S(1)}, u32[]{:S(2)}, u32[]{:S(2)}) async-start(bf16[64,16,512]{2,1,0:T(8,128)(2,1)} %bitcast.13), calls=%async_computation.5 | async-start | bytes 2097152 | tf_op jit(solution)/shard_map/all_to_all | solution.py:532
  167.5 1.0 copy-start.17
  169.3 14.8 %collective-permute-start.1 = (bf16[128,512]{1,0:T(8,128)(2,1)}, bf16[128,512]{1,0:T(8,128)(2,1)S(1)}, u32[]{:S(2)}, u32[]{:S(2)}) collective-permute-start(bf16[128,512]{1,0:T(8,128)(2,1)} %get-tuple-element.70), channel_id=1, source_target_pairs={{0,8},{8,16},{16,24},{24,0},{1,9},{9,17},{17,25},{25,1},{2,10},{10... | collective-permute-start | bytes 393224 | tf_op jit(solution)/shard_map/ppermute | solution.py:493
  170.3 16.5 %collective-permute-start.2 = (bf16[128,512]{1,0:T(8,128)(2,1)S(1)}, bf16[128,512]{1,0:T(8,128)(2,1)S(1)}, u32[]{:S(2)}, u32[]{:S(2)}) collective-permute-start(bf16[128,512]{1,0:T(8,128)(2,1)S(1)} %get-tuple-element.71), channel_id=1, source_target_pairs={{0,16},{8,24},{16,0},{24,8},{1,17},{9,25},{17,1},{25,9},{2,18},{10... | collective-permute-start | bytes 393224 | tf_op jit(solution)/shard_map/ppermute | solution.py:493
  172.7 14.2 %collective-permute-start.3 = (bf16[128,512]{1,0:T(8,128)(2,1)S(1)}, bf16[128,512]{1,0:T(8,128)(2,1)S(1)}, u32[]{:S(2)}, u32[]{:S(2)}) collective-permute-start(bf16[128,512]{1,0:T(8,128)(2,1)S(1)} %get-tuple-element.72), channel_id=1, source_target_pairs={{0,24},{8,0},{16,8},{24,16},{1,25},{9,1},{17,9},{25,17},{2,26},{10... | collective-permute-start | bytes 393224 | tf_op jit(solution)/shard_map/ppermute | solution.py:493
  187.0 5.0 %collective-permute-start.4 = (bf16[32,512]{1,0:T(8,128)(2,1)S(1)}, bf16[32,512]{1,0:T(8,128)(2,1)S(1)}, u32[]{:S(2)}, u32[]{:S(2)}) collective-permute-start(bf16[32,512]{1,0:T(8,128)(2,1)S(1)} %get-tuple-element.75), channel_id=1, source_target_pairs={{0,32},{32,64},{64,96},{96,0},{1,33},{33,65},{65,97},{97,1},{2,34}... | collective-permute-start | bytes 98312 | tf_op jit(solution)/shard_map/ppermute | solution.py:493
  188.2 4.3 %collective-permute-start.5 = (bf16[32,512]{1,0:T(8,128)(2,1)S(1)}, bf16[32,512]{1,0:T(8,128)(2,1)S(1)}, u32[]{:S(2)}, u32[]{:S(2)}) collective-permute-start(bf16[32,512]{1,0:T(8,128)(2,1)S(1)} %get-tuple-element.76), channel_id=1, source_target_pairs={{0,64},{32,96},{64,0},{96,32},{1,65},{33,97},{65,1},{97,33},{2,66}... | collective-permute-start | bytes 98312 | tf_op jit(solution)/shard_map/ppermute | solution.py:493
  190.9 3.2 %collective-permute-start.6 = (bf16[32,512]{1,0:T(8,128)(2,1)S(1)}, bf16[32,512]{1,0:T(8,128)(2,1)S(1)}, u32[]{:S(2)}, u32[]{:S(2)}) collective-permute-start(bf16[32,512]{1,0:T(8,128)(2,1)S(1)} %get-tuple-element.77), channel_id=1, source_target_pairs={{0,96},{32,0},{64,32},{96,64},{1,97},{33,1},{65,33},{97,65},{2,98}... | collective-permute-start | bytes 98312 | tf_op jit(solution)/shard_map/ppermute | solution.py:493
  194.1 16.5 %copy-start.20 = (s32[1,1024]{1,0:T(1,128)S(1)}, s32[1,1024]{1,0:T(1,128)}, u32[]{:S(2)}) copy-start(s32[1,1024]{1,0:T(1,128)} %get-tuple-element.47.part_ref.slot_ref) | copy-start | bytes 12292
  194.1 11.7 %collective-permute-start.7 = (bf16[32,512]{1,0:T(8,128)(2,1)S(1)}, bf16[32,512]{1,0:T(8,128)(2,1)S(1)}, u32[]{:S(2)}, u32[]{:S(2)}) collective-permute-start(bf16[32,512]{1,0:T(8,128)(2,1)S(1)} %add.7.refs_0_), channel_id=1, source_target_pairs={{0,32},{32,64},{64,96},{96,0},{1,33},{33,65},{65,97},{97,1},{2,34}... | collective-permute-start | bytes 98312 | tf_op jit(solution)/shard_map/ppermute | solution.py:493
  194.2 11.7 %collective-permute-start.8 = (bf16[32,512]{1,0:T(8,128)(2,1)S(1)}, bf16[32,512]{1,0:T(8,128)(2,1)S(1)}, u32[]{:S(2)}, u32[]{:S(2)}) collective-permute-start(bf16[32,512]{1,0:T(8,128)(2,1)S(1)} %add.7.refs_0_), channel_id=1, source_target_pairs={{0,64},{32,96},{64,0},{96,32},{1,65},{33,97},{65,1},{97,33},{2,66}... | collective-permute-start | bytes 98312 | tf_op jit(solution)/shard_map/ppermute | solution.py:493
  197.5 8.3 %collective-permute-start.9 = (bf16[32,512]{1,0:T(8,128)(2,1)S(1)}, bf16[32,512]{1,0:T(8,128)(2,1)S(1)}, u32[]{:S(2)}, u32[]{:S(2)}) collective-permute-start(bf16[32,512]{1,0:T(8,128)(2,1)S(1)} %add.7.refs_0_), channel_id=1, source_target_pairs={{0,96},{32,0},{64,32},{96,64},{1,97},{33,1},{65,33},{97,65},{2,98}... | collective-permute-start | bytes 98312 | tf_op jit(solution)/shard_map/ppermute | solution.py:493
  197.8 1.0 copy-start.3
  198.8 23.2 %all-to-all-start.5 = ((bf16[64,16,512]{2,1,0:T(8,128)(2,1)}), bf16[64,16,512]{2,1,0:T(8,128)(2,1)S(1)}, u32[]{:S(2)}, u32[]{:S(2)}) async-start(bf16[64,16,512]{2,1,0:T(8,128)(2,1)} %copy-done.3), calls=%async_computation.6 | async-start | bytes 2097152 | tf_op jit(solution)/shard_map/all_to_all | solution.py:555
  205.9 14.3 %collective-permute-start.10 = (bf16[128,512]{1,0:T(8,128)(2,1)S(1)}, bf16[128,512]{1,0:T(8,128)(2,1)S(1)}, u32[]{:S(2)}, u32[]{:S(2)}) collective-permute-start(bf16[128,512]{1,0:T(8,128)(2,1)S(1)} %gather.2.refs_0_), channel_id=1, source_target_pairs={{0,8},{8,16},{16,24},{24,0},{1,9},{9,17},{17,25},{25,1},{2,10},{10... | collective-permute-start | bytes 393224 | tf_op jit(solution)/shard_map/ppermute | solution.py:493
  207.0 15.0 %collective-permute-start.11 = (bf16[128,512]{1,0:T(8,128)(2,1)S(1)}, bf16[128,512]{1,0:T(8,128)(2,1)S(1)}, u32[]{:S(2)}, u32[]{:S(2)}) collective-permute-start(bf16[128,512]{1,0:T(8,128)(2,1)S(1)} %gather.2.refs_0_), channel_id=1, source_target_pairs={{0,16},{8,24},{16,0},{24,8},{1,17},{9,25},{17,1},{25,9},{2,18},{10... | collective-permute-start | bytes 393224 | tf_op jit(solution)/shard_map/ppermute | solution.py:493
  209.4 12.6 %collective-permute-start.12 = (bf16[128,512]{1,0:T(8,128)(2,1)S(1)}, bf16[128,512]{1,0:T(8,128)(2,1)S(1)}, u32[]{:S(2)}, u32[]{:S(2)}) collective-permute-start(bf16[128,512]{1,0:T(8,128)(2,1)S(1)} %gather.2.refs_0_), channel_id=1, source_target_pairs={{0,24},{8,0},{16,8},{24,16},{1,25},{9,1},{17,9},{25,17},{2,26},{10... | collective-permute-start | bytes 393224 | tf_op jit(solution)/shard_map/ppermute | solution.py:493
  210.6 1.2 copy-start.9
  211.8 1.2 copy-start.10
  213.0 1.6 copy-start.18
  222.0 1.2 copy-start.7
  223.3 11.0 %collective-permute-start.13 = (bf16[1024,512]{1,0:T(8,128)(2,1)S(1)}, bf16[1024,512]{1,0:T(8,128)(2,1)S(1)}, u32[]{:S(2)}, u32[]{:S(2)}) collective-permute-start(bf16[1024,512]{1,0:T(8,128)(2,1)S(1)} %add.8.mine_ref), channel_id=1, source_target_pairs={{0,4},{4,0},{1,5},{5,1},{2,6},{6,2},{3,7},{7,3},{8,12},{12,8},{9,1... | collective-permute-start | bytes 3145736 | tf_op jit(solution)/shard_map/ppermute | solution.py:480
  229.7 3.0 %collective-permute-start.14 = (bf16[512,512]{1,0:T(8,128)(2,1)S(1)}, bf16[512,512]{1,0:T(8,128)(2,1)S(1)}, u32[]{:S(2)}, u32[]{:S(2)}) collective-permute-start(bf16[512,512]{1,0:T(8,128)(2,1)S(1)} %gather.3.after.mine_ref), channel_id=1, source_target_pairs={{0,4},{4,0},{1,5},{5,1},{2,6},{6,2},{3,7},{7,3},{8,12},{12,8},{9,1... | collective-permute-start | bytes 1572872 | tf_op jit(solution)/shard_map/ppermute | solution.py:480
Sparse Core Ops, SparseCore 0:
  25.3 33.7 all-gather.1
  115.3 36.3 reduce-scatter.1
